TPU v7x, 256 devices: a whole 4x4x8 slice. The times are simulated.
256 devices in a mesh: slab: 8 (over x, core), dir: 32 (over z, y).
Axes of the slice: x: 4, y: 4, z: 8, core: 2. Of those that a mesh axis runs over, the one named last changes fastest.
Arguments:
- currents: float32 [2, 512, 128, 256], P(None, ('slab', 'dir')), may hold values from -6 to 6
- near_blocks: float32 [2, 512, 9, 128, 128], P(None, ('slab', 'dir')), may hold values from -0.1875 to 0.1875
- near_index: int32 [512, 9], P(('slab', 'dir')), may hold values from 0 to 5
- aggregate: float32 [2, 256, 128], replicated, may hold values from -0.5 to 0.5
- translations: float32 [2, 64, 256], P(None, None, 'dir'), may hold values from -1 to 1
- inter_source: int32 [512, 32], P('slab'), may hold values from 0 to 191
- inter_shift: int32 [512, 32], P('slab'), may hold values from 0 to 63
- disaggregate: float32 [2, 128, 256], replicated, may hold values from -0.375 to 0.375
Outputs:
- product: float32 [2, 512, 128, 256], P(None, ('slab', 'dir'))
All inputs are finite; a program needn't handle non-finite values.
Results may differ from a plain program's by a relative error of at most 0.0003.
Values sent between devices are 32-bit elements; how exact they have to be, the bound alone decides.
No kernel may reach another device: no remote copies, remote signals or barrier semaphores. Data moves between devices by JAX's collectives and lax.ppermute only.
A program may use at most 64 MiB of HBM per device.

v0:
```python
import jax
import jax.numpy as jnp
from jax import lax
from jax.sharding import PartitionSpec as P


def extended(cells, sides, width, closed):
    for axis, dim in sides:
        count = lax.axis_size(axis)
        ends = count if closed else count - 1
        head = lax.slice_in_dim(cells, 0, width, axis=dim)
        tail = lax.slice_in_dim(cells, cells.shape[dim] - width, cells.shape[dim], axis=dim)
        cells = jnp.concatenate(
            [
                lax.ppermute(tail, axis, [(i, (i + 1) % count) for i in range(ends)]),
                cells,
                lax.ppermute(head, axis, [((i + 1) % count, i) for i in range(ends)]),
            ],
            axis=dim,
        )
    return cells


def cein(form, left, right):

    def single(u, v):
        return jnp.einsum(form, u, v, precision=lax.Precision.HIGHEST)

    real = single(left[0], right[0]) - single(left[1], right[1])
    imag = single(left[0], right[1]) + single(left[1], right[0])
    return jnp.stack([real, imag])


def body(
    currents,
    near_blocks,
    near_index,
    aggregate,
    translations,
    inter_source,
    inter_shift,
    disaggregate,
):
    box_dev = currents.shape[1]
    padded = extended(currents, (("dir", 1),), box_dev, True)
    sources = jnp.take(padded, near_index, axis=1)
    near = cein("bjpq,bjqr->bpr", near_blocks, sources)
    radiated = cein("kp,bpr->bkr", aggregate, currents)
    owned = lax.all_to_all(radiated, "dir", split_axis=2, concat_axis=1, tiled=True)
    slab_count = owned.shape[1]
    widened = extended(owned, (("slab", 1),), slab_count, False)
    positions = jnp.arange(3 * slab_count, dtype=jnp.int32)
    onehot = (inter_source[:, :, None] == positions[None, None, :]).astype(jnp.float32)
    factors = jnp.take(translations, inter_shift, axis=1)
    matrix = jnp.einsum("bis,cbik->ckbs", onehot, factors, precision=lax.Precision.HIGHEST)
    incoming = cein("kbs,skr->bkr", matrix, widened)
    far = cein(
        "pk,bkr->bpr",
        disaggregate,
        lax.all_to_all(incoming, "dir", split_axis=1, concat_axis=2, tiled=True),
    )
    return near + far


def solution(mesh):
    in_specs = (
        P(None, ("slab", "dir"), None, None),
        P(None, ("slab", "dir"), None, None, None),
        P(("slab", "dir"), None),
        P(),
        P(None, None, "dir"),
        P("slab", None),
        P("slab", None),
        P(),
    )
    out_specs = P(None, ("slab", "dir"), None, None)
    return jax.shard_map(body, mesh=mesh, in_specs=in_specs, out_specs=out_specs, check_vma=False)
```

profile of v0, /device:TPU:2, one launch (start us, length us, event | category | flops | bytes accessed | tf_op | source)
XLA Modules:
  0.0 123.9 jit_solution(13927042990659418194)
XLA Ops:
  0.0 1.7 %fusion.70 = f32[2,256,256]{2,1,0:T(8,128)S(1)} fusion(f32[2,2,128,256]{3,2,1,0:T(8,128)} %param.8, f32[2,256,128]{2,1,0:T(8,128)} %param.11), kind=kOutput, calls=%fused_computation.71 | convolution fusion | flops 201326592 | bytes 917504 | tf_op jit(solution)/shard_map/kp,bpr->bkr/dot_general | solution.py:27
  1.7 1.6 %fusion.74 = f32[2,256,256]{2,1,0:T(8,128)S(1)} fusion(f32[2,2,128,256]{3,2,1,0:T(8,128)} %param.8, f32[2,256,128]{2,1,0:T(8,128)} %param.11), kind=kOutput, calls=%fused_computation.75 | convolution fusion | flops 201326592 | bytes 917504 | tf_op jit(solution)/shard_map/kp,bpr->bkr/dot_general | solution.py:27
  3.3 1.6 %fusion.18 = f32[1,2,256,256]{2,3,1,0:T(8,128)S(1)} fusion(f32[2,256,256]{2,1,0:T(8,128)S(1)} %fusion.70, f32[2,2,128,256]{3,2,1,0:T(8,128)} %param.8, f32[2,256,128]{2,1,0:T(8,128)} %param.11), kind=kOutput, calls=%fused_computation.25 | convolution fusion | flops 201457664 | bytes 1441792 | tf_op jit(solution)/shard_map/kp,bpr->bkr/dot_general | solution.py:27
  5.7 1.3 %copy.69 = f32[2,2,256,256]{3,1,0,2:T(2,128)} copy(f32[2,2,256,256]{2,3,1,0:T(8,128)S(1)} %pad_maximum_fusion.1) | data formatting | bytes 2097152 | tf_op jit(solution)/shard_map/stack | solution.py:31
  7.0 11.5 %all-to-all-start = ((f32[2,2,256,256]{3,1,0,2:T(2,128)}), f32[2,2,256,256]{3,1,0,2:T(2,128)S(1)}, u32[]{:S(2)}, u32[]{:S(2)}) async-start(f32[2,2,256,256]{3,1,0,2:T(2,128)} %copy.69), calls=%async_computation | async-start | bytes 2097152 | tf_op jit(solution)/shard_map/all_to_all | solution.py:49
  18.5 5.3 %collective-permute-start.1 = (f32[2,2,128,256]{3,2,1,0:T(8,128)S(1)}, f32[2,2,128,256]{3,2,1,0:T(8,128)}, u32[]{:S(2)}, u32[]{:S(2)}) collective-permute-start(f32[2,2,128,256]{3,2,1,0:T(8,128)S(1)} %copy-done.1), channel_id=1, source_target_pairs={{1,0},{2,1},{3,2},{4,3},{5,4},{6,5},{7,6},{8,7},{9,8},{10,9},{11,1... | collective-permute-start | bytes 1572872 | tf_op jit(solution)/shard_map/ppermute | solution.py:17
  23.9 22.6 %all-to-all-done = f32[2,2,256,256]{3,1,0,2:T(2,128)S(1)} async-done(((f32[2,2,256,256]{3,1,0,2:T(2,128)}), f32[2,2,256,256]{3,1,0,2:T(2,128)S(1)}, u32[]{:S(2)}, u32[]{:S(2)}) %all-to-all-start) | async-done | bytes 1048608 | tf_op jit(solution)/shard_map/all_to_all | solution.py:49
  47.6 1.7 %all_to_all.27 = f32[2,64,8,256]{3,1,2,0:T(8,128)} reshape(f32[2,32,2,8,256]{4,2,1,3,0:T(2,128)S(1)} %copy.71) | data formatting | bytes 2097152 | tf_op jit(solution)/shard_map/all_to_all | solution.py:49
  49.3 1.9 %collective-permute-start.2 = (f32[2,64,8,256]{3,1,2,0:T(8,128)}, f32[2,64,8,256]{3,1,2,0:T(8,128)}, u32[]{:S(2)}, u32[]{:S(2)}) collective-permute-start(f32[2,64,8,256]{3,1,2,0:T(8,128)} %all_to_all.27), channel_id=1, source_target_pairs={{0,32},{32,64},{64,96},{96,128},{128,160},{160,192},{192,224},{1,3... | collective-permute-start | bytes 3145736 | tf_op jit(solution)/shard_map/ppermute | solution.py:15
  51.4 6.8 %gather_fusion.1 = f32[2048,2,8]{2,1,0:T(2,128)S(1)} fusion(f32[2,64,8]{2,0,1:T(2,128)S(1)} %copy.74, s32[2048]{0:T(1024)S(1)} %broadcast_clamp_fusion), kind=kCustom, calls=%fused_computation.1 | custom fusion | bytes 270336 | tf_op jit(solution)/shard_map/jit(_take)/gather | solution.py:54
  59.4 3.8 %collective-permute-start.3 = (f32[2,64,8,256]{3,1,2,0:T(8,128)}, f32[2,64,8,256]{3,1,2,0:T(8,128)S(1)}, u32[]{:S(2)}, u32[]{:S(2)}) collective-permute-start(f32[2,64,8,256]{3,1,2,0:T(8,128)} %all_to_all.27), channel_id=1, source_target_pairs={{32,0},{64,32},{96,64},{128,96},{160,128},{192,160},{224,192},{33,... | collective-permute-start | bytes 3145736 | tf_op jit(solution)/shard_map/ppermute | solution.py:17
  68.3 7.3 %collective-permute-done.3 = f32[2,64,8,256]{3,1,2,0:T(8,128)S(1)} collective-permute-done((f32[2,64,8,256]{3,1,2,0:T(8,128)}, f32[2,64,8,256]{3,1,2,0:T(8,128)S(1)}, u32[]{:S(2)}, u32[]{:S(2)}) %collective-permute-start.3) | collective-permute-done | bytes 1048608 | tf_op jit(solution)/shard_map/ppermute | solution.py:17
  80.9 1.6 %copy.82 = f32[2,64,8,256]{3,2,0,1:T(8,128)} copy(f32[2,64,8,256]{3,1,2,0:T(8,128)S(1)} %pad_maximum_fusion.2) | data formatting | bytes 2097152 | tf_op jit(solution)/shard_map/stack | solution.py:31
  82.5 5.9 %all-to-all-start.1 = ((f32[2,64,8,256]{3,2,0,1:T(8,128)}), f32[2,64,8,256]{3,2,0,1:T(8,128)}, u32[]{:S(2)}, u32[]{:S(2)}) async-start(f32[2,64,8,256]{3,2,0,1:T(8,128)} %copy.82), calls=%async_computation.1 | async-start | bytes 2097152 | tf_op jit(solution)/shard_map/all_to_all | solution.py:60
  88.5 1.3 %pad_maximum_fusion = f32[2,6,128,256]{3,2,1,0:T(8,128)S(1)} fusion(f32[2,2,128,256]{3,2,1,0:T(8,128)} %collective-permute-done.1, f32[2,2,128,256]{3,2,1,0:T(8,128)S(1)} %copy-done.1, f32[2,2,128,256]{3,2,1,0:T(8,128)} %collective-permute-done), kind=kLoop, calls=%fused_computation.14 | loop fusion | flops 786432 | bytes 3145728 | tf_op jit(solution)/shard_map/concatenate | solution.py:13
  89.9 3.0 %gather_fusion = f32[18,2,128,256]{3,2,1,0:T(8,128)} fusion(f32[2,6,128,256]{3,2,1,0:T(8,128)S(1)} %pad_maximum_fusion, s32[1024]{0:T(1024)S(1)} %pad_clamp_fusion), kind=kCustom, calls=%fused_computation | custom fusion | bytes 9437256 | tf_op jit(solution)/shard_map/jit(_take)/gather | solution.py:46
  92.8 6.1 %copy.66 = f32[18,2,128,256]{2,3,0,1:T(8,128)} copy(f32[18,2,128,256]{3,2,1,0:T(8,128)} %gather_fusion) | data formatting | bytes 9437184 | tf_op jit(solution)/shard_map/jit(_take)/gather | solution.py:46
  98.9 3.1 %select_bitcast_fusion = f32[2,2,9,128,256]{3,4,2,1,0:T(8,128)S(1)} fusion(f32[2,9,2,128,256]{3,4,1,0,2:T(8,128)} %bitcast.195, pred[2,9]{1,0:T(4,128)(4,1)S(1)} %compare_and_fusion.1), kind=kLoop, calls=%fused_computation.2 | loop fusion | flops 1179648 | bytes 9437202 | tf_op jit(solution)/shard_map/jit(_take)/select_n | solution.py:46
  102.1 2.2 %fusion.29 = f32[2,256,128]{2,1,0:T(8,128)S(1)} fusion(f32[2,2,9,128,256]{3,4,2,1,0:T(8,128)S(1)} %select_bitcast_fusion, f32[2,2,9,128,128]{4,3,2,1,0:T(8,128)S(1)} %copy-done), kind=kOutput, calls=%fused_computation.37 | convolution fusion | flops 905969664 | bytes 3801088 | tf_op jit(solution)/shard_map/bjpq,bjqr->bpr/dot_general | solution.py:27
  104.3 2.2 %fusion.26 = f32[2,256,128]{2,1,0:T(8,128)S(1)} fusion(f32[2,2,9,128,256]{3,4,2,1,0:T(8,128)S(1)} %select_bitcast_fusion, f32[2,2,9,128,128]{4,3,2,1,0:T(8,128)S(1)} %copy-done), kind=kOutput, calls=%fused_computation.36 | convolution fusion | flops 905969664 | bytes 3801088 | tf_op jit(solution)/shard_map/bjpq,bjqr->bpr/dot_general | solution.py:27
  106.6 2.2 %fusion.41 = f32[1,2,128,256]{2,3,1,0:T(8,128)S(1)} fusion(f32[2,256,128]{2,1,0:T(8,128)S(1)} %fusion.29, f32[2,2,9,128,256]{3,4,2,1,0:T(8,128)S(1)} %select_bitcast_fusion, f32[2,2,9,128,128]{4,3,2,1,0:T(8,128)S(1)} %copy-done), kind=kOutput, calls=%fused_computation.41 | convolution fusion | flops 906035200 | bytes 4063232 | tf_op jit(solution)/shard_map/bjpq,bjqr->bpr/dot_general | solution.py:27
  108.8 2.2 %fusion.47 = f32[1,2,128,256]{2,3,1,0:T(8,128)S(1)} fusion(f32[2,256,128]{2,1,0:T(8,128)S(1)} %fusion.26, f32[2,2,9,128,256]{3,4,2,1,0:T(8,128)S(1)} %select_bitcast_fusion, f32[2,2,9,128,128]{4,3,2,1,0:T(8,128)S(1)} %copy-done), kind=kOutput, calls=%fused_computation.43 | convolution fusion | flops 906035200 | bytes 4063232 | tf_op jit(solution)/shard_map/bjpq,bjqr->bpr/dot_general | solution.py:27
  111.0 6.4 %all-to-all-done.1 = f32[2,64,8,256]{3,2,0,1:T(8,128)} async-done(((f32[2,64,8,256]{3,2,0,1:T(8,128)}), f32[2,64,8,256]{3,2,0,1:T(8,128)}, u32[]{:S(2)}, u32[]{:S(2)}) %all-to-all-start.1) | async-done | bytes 1048608 | tf_op jit(solution)/shard_map/all_to_all | solution.py:60
  117.4 1.3 %copy.83 = f32[2,64,8,256]{3,2,1,0:T(8,128)S(1)} copy(f32[2,64,8,256]{3,2,0,1:T(8,128)} %all-to-all-done.1) | data formatting | bytes 2097152 | tf_op jit(solution)/shard_map/all_to_all | solution.py:60
  (55 shorter events, 18.7 us)
Async XLA Ops:
  0.0 4.9 %copy-start.1 = (f32[2,2,128,256]{3,2,1,0:T(8,128)S(1)}, f32[2,2,128,256]{3,2,1,0:T(8,128)}, u32[]{:S(2)}) copy-start(f32[2,2,128,256]{3,2,1,0:T(8,128)} %param.8) | copy-start | bytes 1572868
  0.0 4.9 %copy-start.3 = (f32[2,256,128]{2,1,0:T(8,128)S(1)}, f32[2,256,128]{2,1,0:T(8,128)}, u32[]{:S(2)}) copy-start(f32[2,256,128]{2,1,0:T(8,128)} %param.11) | copy-start | bytes 786436
  5.6 18.1 %copy-start.4 = (s32[64,32]{0,1:T(8,128)S(1)}, s32[64,32]{0,1:T(8,128)}, u32[]{:S(2)}) copy-start(s32[64,32]{0,1:T(8,128)} %param.14) | copy-start | bytes 24580
  7.0 39.6 %all-to-all-start = ((f32[2,2,256,256]{3,1,0,2:T(2,128)}), f32[2,2,256,256]{3,1,0,2:T(2,128)S(1)}, u32[]{:S(2)}, u32[]{:S(2)}) async-start(f32[2,2,256,256]{3,1,0,2:T(2,128)} %copy.69), calls=%async_computation | async-start | bytes 2097152 | tf_op jit(solution)/shard_map/all_to_all | solution.py:49
  18.5 70.0 %collective-permute-start.1 = (f32[2,2,128,256]{3,2,1,0:T(8,128)S(1)}, f32[2,2,128,256]{3,2,1,0:T(8,128)}, u32[]{:S(2)}, u32[]{:S(2)}) collective-permute-start(f32[2,2,128,256]{3,2,1,0:T(8,128)S(1)} %copy-done.1), channel_id=1, source_target_pairs={{1,0},{2,1},{3,2},{4,3},{5,4},{6,5},{7,6},{8,7},{9,8},{10,9},{11,1... | collective-permute-start | bytes 1572872 | tf_op jit(solution)/shard_map/ppermute | solution.py:17
  23.7 64.8 %collective-permute-start = (f32[2,2,128,256]{3,2,1,0:T(8,128)S(1)}, f32[2,2,128,256]{3,2,1,0:T(8,128)}, u32[]{:S(2)}, u32[]{:S(2)}) collective-permute-start(f32[2,2,128,256]{3,2,1,0:T(8,128)S(1)} %copy-done.1), channel_id=1, source_target_pairs={{0,1},{1,2},{2,3},{3,4},{4,5},{5,6},{6,7},{7,8},{8,9},{9,10},{10,1... | collective-permute-start | bytes 1572872 | tf_op jit(solution)/shard_map/ppermute | solution.py:15
  46.8 4.5 %copy-start.5 = (s32[64,32]{0,1:T(8,128)S(1)}, s32[64,32]{0,1:T(8,128)}, u32[]{:S(2)}) copy-start(s32[64,32]{0,1:T(8,128)} %param.13) | copy-start | bytes 24580
  46.8 4.6 %copy-start.6 = (f32[2,64,8]{1,2,0:T(8,128)S(1)}, f32[2,64,8]{1,2,0:T(8,128)}, u32[]{:S(2)}) copy-start(f32[2,64,8]{1,2,0:T(8,128)} %param.12) | copy-start | bytes 12292
  49.3 16.4 %collective-permute-start.2 = (f32[2,64,8,256]{3,1,2,0:T(8,128)}, f32[2,64,8,256]{3,1,2,0:T(8,128)}, u32[]{:S(2)}, u32[]{:S(2)}) collective-permute-start(f32[2,64,8,256]{3,1,2,0:T(8,128)} %all_to_all.27), channel_id=1, source_target_pairs={{0,32},{32,64},{64,96},{96,128},{128,160},{160,192},{192,224},{1,3... | collective-permute-start | bytes 3145736 | tf_op jit(solution)/shard_map/ppermute | solution.py:15
  59.4 16.3 %collective-permute-start.3 = (f32[2,64,8,256]{3,1,2,0:T(8,128)}, f32[2,64,8,256]{3,1,2,0:T(8,128)S(1)}, u32[]{:S(2)}, u32[]{:S(2)}) collective-permute-start(f32[2,64,8,256]{3,1,2,0:T(8,128)} %all_to_all.27), channel_id=1, source_target_pairs={{32,0},{64,32},{96,64},{128,96},{160,128},{192,160},{224,192},{33,... | collective-permute-start | bytes 3145736 | tf_op jit(solution)/shard_map/ppermute | solution.py:17
  80.9 7.5 %copy-start.7 = (s32[2,9]{1,0:T(2,128)S(1)}, s32[2,9]{1,0:T(2,128)}, u32[]{:S(2)}) copy-start(s32[2,9]{1,0:T(2,128)} %param.10) | copy-start | bytes 220
  82.5 34.9 %all-to-all-start.1 = ((f32[2,64,8,256]{3,2,0,1:T(8,128)}), f32[2,64,8,256]{3,2,0,1:T(8,128)}, u32[]{:S(2)}, u32[]{:S(2)}) async-start(f32[2,64,8,256]{3,2,0,1:T(8,128)} %copy.82), calls=%async_computation.1 | async-start | bytes 2097152 | tf_op jit(solution)/shard_map/all_to_all | solution.py:60
  98.9 3.1 %copy-start = (f32[2,2,9,128,128]{4,3,2,1,0:T(8,128)S(1)}, f32[2,2,9,128,128]{4,3,2,1,0:T(8,128)}, u32[]{:S(2)}) copy-start(f32[2,2,9,128,128]{4,3,2,1,0:T(8,128)} %param.9) | copy-start | bytes 7077892
  111.0 7.8 %copy-start.2 = (f32[2,128,256]{2,1,0:T(8,128)S(1)}, f32[2,128,256]{2,1,0:T(8,128)}, u32[]{:S(2)}) copy-start(f32[2,128,256]{2,1,0:T(8,128)} %param.15) | copy-start | bytes 786436
where the time goes:
time: 125 us; the launch traced here: 124 us
  waiting for transfers between devices  37.5 us (30%)
  starting transfers between devices  28.4 us (23%)
  local copies, waits for them, and re-layouts  28.2 us (23%)
  matrix products  24.6 us (20%)
  other arithmetic  4.77 us (4%)
    dot_general x16, matrix products, single(): return jnp.einsum(form, u, v, precision=lax.Precision.HIGHEST)  23.4 us
    all_to_all x1, waiting for transfers between devices, body(): lax.all_to_all(radiated, 'dir', split_axis=2, concat_axis=1, tiled=True)  22.6 us
    all_to_all x1, starting transfers between devices, body(): lax.all_to_all(radiated, 'dir', split_axis=2, concat_axis=1, tiled=True)  11.5 us
    ppermute x2, starting transfers between devices, extended(): lax.ppermute(head, axis, [((i + 1) % count, i) for i in range(ends)])  9.11 us
    gather x2, local copies, waits for them, and re-layouts, body(): sources = jnp.take(padded, near_index, axis=1)  9.07 us
    gather x2, local copies, waits for them, and re-layouts, body(): factors = jnp.take(translations, inter_shift, axis=1)  7.81 us
    ppermute x2, waiting for transfers between devices, extended(): lax.ppermute(head, axis, [((i + 1) % count, i) for i in range(ends)])  7.32 us
    all_to_all x1, waiting for transfers between devices, body(): lax.all_to_all(incoming, 'dir', split_axis=1, concat_axis=2, tiled=True)  6.41 us
  transfers between devices with their start and end apart: 6, of which 4 were waited for; matrix products, arithmetic and copies ran while one was open for 34% of the time, Pallas kernels for 0%

commit v1 on v0

v1 whole, which is shorter than its diff:
```python
import functools

import jax
import jax.numpy as jnp
from jax import lax
from jax.experimental import pallas as pl
from jax.experimental.pallas import tpu as pltpu
from jax.sharding import PartitionSpec as P

F32, BF16 = jnp.float32, jnp.bfloat16
VMEM = pltpu.MemorySpace.VMEM
SMEM = pltpu.MemorySpace.SMEM
MIB = 1 << 20


def split(x):
    high = x.astype(BF16)
    return high, (x - high.astype(F32)).astype(BF16)


def dot3(left, right, contract):
    def one(a, b):
        return lax.dot_general(a, b, (contract, ((), ())), preferred_element_type=F32)

    return one(left[0], right[0]) + (one(left[0], right[1]) + one(left[1], right[0]))


NN_FORM = ((1,), (0,))
NT_FORM = ((1,), (1,))


def pack_kernel(currents_ref, translations_ref, out_ref):
    devices, rows, lanes = out_ref.shape
    parts, boxes, _, illum = currents_ref.shape
    own = illum // devices
    for c in range(parts):
        for b in range(boxes):
            turned = currents_ref[c, b].T.reshape(devices, own, lanes)
            out_ref[:, pl.ds((c * boxes + b) * own, own), :] = turned
    table = jnp.concatenate([translations_ref[0], translations_ref[1]], axis=1)
    first = parts * boxes * own
    out_ref[:, first:, :] = jnp.broadcast_to(table[None], (devices, rows - first, lanes))


def near_kernel(index_ref, blocks_ref, own_ref, left_ref, right_ref, out_ref, high_ref, low_ref):
    boxes, entries = blocks_ref.shape[1], blocks_ref.shape[2]
    width = own_ref.shape[3]
    for place, ref in enumerate((left_ref, own_ref, right_ref)):
        for b in range(boxes):
            slot = place * boxes + b
            real, imag = split(ref[0, b]), split(ref[1, b])
            for store, x, y in ((high_ref, real[0], imag[0]), (low_ref, real[1], imag[1])):
                store[slot] = jnp.concatenate(
                    [jnp.concatenate([x, y], axis=1), jnp.concatenate([-y, x], axis=1)], axis=0
                )
    for b in range(boxes):

        def step(j, total):
            source = index_ref[b, j]
            block = split(jnp.concatenate([blocks_ref[0, b, j], blocks_ref[1, b, j]], axis=1))
            return total + dot3(block, (high_ref[source], low_ref[source]), NN_FORM)

        total = lax.fori_loop(0, entries, step, jnp.zeros((blocks_ref.shape[3], 2 * width), F32))
        out_ref[0, b] = total[:, :width]
        out_ref[1, b] = total[:, width:]


def radiate(block_ref, weights):
    devices, _, lanes = block_ref.shape
    real = block_ref[:, :16, :].reshape(devices * 16, lanes)
    imag = block_ref[:, 16:32, :].reshape(devices * 16, lanes)
    rows = jnp.concatenate([real, imag], axis=1)
    return dot3(split(rows), weights, NT_FORM)


def complex_rows(ref):
    real, imag = ref[0], ref[1]
    return jnp.concatenate(
        [jnp.concatenate([real, -imag], axis=1), jnp.concatenate([imag, real], axis=1)], axis=0
    )


def own_kernel(own_ref, aggregate_ref, radiated_ref, table_ref):
    boxes, sub, width = radiated_ref.shape
    radiated_ref[...] = radiate(own_ref, split(complex_rows(aggregate_ref))).reshape(boxes, sub, width)
    devices, rows, lanes = own_ref.shape
    table = own_ref[:, 32:, :].reshape(devices * (rows - 32), lanes).T
    half = lanes // 2
    wide = jnp.concatenate([table[:half], table[half:]], axis=1)
    table_ref[...] = jnp.broadcast_to(wide[:, None, :], table_ref.shape)


def far_kernel(
    source_ref, shift_ref, own_ref, table_ref, before_ref, after_ref, aggregate_ref, incoming_ref, radiated_ref
):
    boxes, sub, width = own_ref.shape
    entries = source_ref.shape[0]
    half = width // 2
    weights = split(complex_rows(aggregate_ref))
    radiated_ref[:boxes] = radiate(before_ref, weights).reshape(boxes, sub, width)
    radiated_ref[boxes : 2 * boxes] = own_ref[...]
    radiated_ref[2 * boxes :] = radiate(after_ref, weights).reshape(boxes, sub, width)

    def one_box(g, carry):
        real = jnp.zeros((sub, half), F32)
        imag = jnp.zeros((sub, half), F32)
        for i in range(entries):
            q, t = source_ref[i, g], shift_ref[i, g]
            xr, xi = radiated_ref[q, :, :half], radiated_ref[q, :, half:]
            tr, ti = table_ref[t, :, :half], table_ref[t, :, half:]
            real += tr * xr - ti * xi
            imag += tr * xi + ti * xr
        incoming_ref[g, :, :half] = real
        incoming_ref[g, :, half:] = imag
        return carry

    lax.fori_loop(0, boxes, one_box, 0)


def down_kernel(incoming_ref, disaggregate_ref, left_ref, right_ref, out_ref):
    boxes, sub, width = incoming_ref.shape
    far = dot3(
        split(incoming_ref[...].reshape(boxes * sub, width)), split(complex_rows(disaggregate_ref)), NT_FORM
    )
    devices, rows, lanes = out_ref.shape
    out_ref[:, : rows // 2, :] = far[:, :lanes].reshape(devices, rows // 2, lanes)
    out_ref[:, rows // 2 :, :] = far[:, lanes:].reshape(devices, rows // 2, lanes)


def join_kernel(far_ref, near_ref, out_ref):
    parts, boxes, lanes, illum = out_ref.shape
    devices = far_ref.shape[0]
    own = illum // devices
    for c in range(parts):
        for b in range(boxes):
            turned = far_ref[:, pl.ds((c * boxes + b) * own, own), :].reshape(illum, lanes)
            out_ref[c, b] = near_ref[c, b] + turned.T


def call(kernel, outs, kinds, scratch=(), limit=16, flops=0, name=None):
    specs = [pl.BlockSpec(memory_space=kind) for kind in kinds]

    def run(*args):
        moved = sum(a.size * 4 for a in args) + sum(o.size * 4 for o in jax.tree.leaves(outs))
        return pl.pallas_call(
            kernel,
            out_shape=outs,
            in_specs=specs,
            out_specs=jax.tree.map(lambda _: pl.BlockSpec(memory_space=VMEM), outs),
            scratch_shapes=list(scratch),
            compiler_params=pltpu.CompilerParams(vmem_limit_bytes=limit * MIB),
            cost_estimate=pl.CostEstimate(flops=flops, bytes_accessed=moved, transcendentals=0),
            name=name,
        )(*args)

    return run


def body(currents, near_blocks, near_index, aggregate, translations, inter_source, inter_shift, disaggregate):
    devices = lax.axis_size("dir")
    slabs = lax.axis_size("slab")
    parts, box_dev, unknowns, illum = currents.shape
    own = illum // devices
    directions = aggregate.shape[1]
    boxes = inter_source.shape[0]
    ops = translations.shape[1]
    ring = [(i, (i + 1) % devices) for i in range(devices)]
    line = [(i, i + 1) for i in range(slabs - 1)]
    rows = parts * box_dev * own
    packed = call(
        pack_kernel, jax.ShapeDtypeStruct((devices, rows + translations.shape[2], unknowns), F32), (VMEM, VMEM), name="pack"
    )(currents, jnp.transpose(translations, (0, 2, 1)))
    mine = lax.all_to_all(packed, "dir", 0, 0, tiled=True)
    before = lax.ppermute(mine, "slab", line)
    after = lax.ppermute(mine, "slab", [(j, i) for i, j in line])

    radiated, table = call(
        own_kernel,
        (
            jax.ShapeDtypeStruct((boxes, own, 2 * directions), F32),
            jax.ShapeDtypeStruct((ops, own, 2 * directions), F32),
        ),
        (VMEM, VMEM),
        flops=2 * 3 * 67_000_000,
        name="own",
    )(mine, aggregate)
    radiated, beside = lax.optimization_barrier((radiated, currents))
    left = lax.ppermute(beside, "dir", ring)
    right = lax.ppermute(beside, "dir", [(j, i) for i, j in ring])
    incoming = call(
        far_kernel,
        jax.ShapeDtypeStruct((boxes, own, 2 * directions), F32),
        (SMEM, SMEM) + (VMEM,) * 5,
        scratch=(pltpu.VMEM((3 * boxes, own, 2 * directions), F32),),
        limit=24,
        flops=2 * 3 * 200_000_000,
        name="far",
    )(inter_source.T, inter_shift.T, radiated, table, before, after, aggregate)
    far = call(
        down_kernel,
        jax.ShapeDtypeStruct((devices, rows, unknowns), F32),
        (VMEM, VMEM, pl.ANY, pl.ANY),
        flops=2 * 3 * 67_000_000,
        name="down",
    )(incoming, disaggregate, left, right)
    back = lax.all_to_all(far, "dir", 0, 0, tiled=True)

    near = call(
        near_kernel,
        jax.ShapeDtypeStruct(currents.shape, F32),
        (SMEM,) + (VMEM,) * 4,
        scratch=(
            pltpu.VMEM((3 * box_dev, 2 * unknowns, 2 * illum), BF16),
            pltpu.VMEM((3 * box_dev, 2 * unknowns, 2 * illum), BF16),
        ),
        limit=24,
        flops=2 * 3 * 302_000_000,
        name="near",
    )(near_index, near_blocks, currents, left, right)
    return call(join_kernel, jax.ShapeDtypeStruct(currents.shape, F32), (VMEM, VMEM), name="join")(back, near)


def solution(mesh):
    in_specs = (
        P(None, ("slab", "dir"), None, None),
        P(None, ("slab", "dir"), None, None, None),
        P(("slab", "dir"), None),
        P(),
        P(None, None, "dir"),
        P("slab", None),
        P("slab", None),
        P(),
    )
    out_specs = P(None, ("slab", "dir"), None, None)
    return jax.shard_map(body, mesh=mesh, in_specs=in_specs, out_specs=out_specs, check_vma=False)
```

time: 125 us -> 84.3 us (0.67)
  blocking collectives: 0 us -> 31.5 us
  local copies, waits for them, and re-layouts: 28.2 us -> 2.41 us
  matrix products: 24.6 us -> 0 us
  Pallas kernels: 0 us -> 18 us
  waiting for transfers between devices: 37.5 us -> 19.8 us
  starting transfers between devices: 28.4 us -> 12.2 us
  other arithmetic: 4.77 us -> 0 us
    all_to_all x0 -> x1, blocking collectives: none -> 31.5 us  [body(): mine = lax.all_to_all(packed, 'dir', 0, 0, tiled=True)]
    dot_general x17 -> x0, matrix products: 24.6 us -> none  [the longest x16 23.4 us: single(): return jnp.einsum(form, u, v, precision=lax.Precision.HIGHEST)]
    all_to_all x2 -> x1, waiting for transfers between devices: 29 us -> 9.53 us  [body(): back = lax.all_to_all(far, 'dir', 0, 0, tiled=True)]
    pallas_call x0 -> x6, Pallas kernels: none -> 18 us  [run(): pl.pallas_call(kernel, out_shape=outs, in_specs=specs, out_specs=jax.tree...]
    gather x4 -> x0, local copies, waits for them, and re-layouts: 16.9 us -> none  [the longest x2 9.07 us: body(): sources = jnp.take(padded, near_index, axis=1)]
    all_to_all x2 -> x1, starting transfers between devices: 17.4 us -> 5.77 us  [body(): back = lax.all_to_all(far, 'dir', 0, 0, tiled=True)]
    ppermute x4, starting transfers between devices: 11 us -> 6.42 us  [the longest x1 2.41 us: body(): before = lax.ppermute(mine, 'slab', line)]
    all_to_all x4 -> x0, local copies, waits for them, and re-layouts: 4.02 us -> none  [the longest x3 2.72 us: body(): lax.all_to_all(radiated, 'dir', split_axis=2, concat_axis=1, tiled=True)]
  transfers between devices with their start and end apart: 6 -> 5, of which waited for: 4 -> 4; matrix products, arithmetic and copies ran while one was open for 34% -> 0% of each run, Pallas kernels for 0% -> 17%
where the time goes in v1:
time: 84.3 us; the launch traced here: 84 us
  blocking collectives  31.5 us (37%)
  waiting for transfers between devices  19.8 us (23%)
  Pallas kernels  18 us (21%)
  starting transfers between devices  12.2 us (14%)
  local copies, waits for them, and re-layouts  2.41 us (3%)
    all_to_all x1, blocking collectives, body(): mine = lax.all_to_all(packed, 'dir', 0, 0, tiled=True)  31.5 us
    pallas_call x6, Pallas kernels, run(): pl.pallas_call(kernel, out_shape=outs, in_specs=specs, out_specs=jax.tree...  18 us
    all_to_all x1, waiting for transfers between devices, body(): back = lax.all_to_all(far, 'dir', 0, 0, tiled=True)  9.53 us
    all_to_all x1, starting transfers between devices, body(): back = lax.all_to_all(far, 'dir', 0, 0, tiled=True)  5.77 us
    ppermute x1, waiting for transfers between devices, body(): before = lax.ppermute(mine, 'slab', line)  3.82 us
    ppermute x1, waiting for transfers between devices, body(): left = lax.ppermute(beside, 'dir', ring)  3.5 us
    ppermute x1, waiting for transfers between devices, body(): after = lax.ppermute(mine, 'slab', [(j, i) for i, j in line])  2.92 us
    unnamed x14, local copies, waits for them, and re-layouts  2.41 us
  transfers between devices with their start and end apart: 5, of which 4 were waited for; matrix products, arithmetic and copies ran while one was open for 0% of the time, Pallas kernels for 17%

profile of v1, /device:TPU:2, one launch (start us, length us, event | category | flops | bytes accessed | tf_op | source)
XLA Modules:
  0.0 84.0 jit_solution(11061692673646229377)
XLA Ops:
  0.0 0.0 copy-start.4
  0.0 0.7 copy-done.4
  0.8 1.3 %pack.1 = f32[32,40,128]{2,1,0:T(8,128)S(1)} custom-call(f32[2,2,128,256]{3,2,1,0:T(8,128)} %own_ref.1, f32[2,8,64]{2,1,0:T(8,128)S(1)} %bitcast.5), custom_call_target="tpu_custom_call" | custom-call | bytes 1183744 | tf_op jit(solution)/shard_map/pack/pallas_call | solution.py:145
  2.0 31.5 %all_to_all.10.own_ref = f32[32,40,128]{2,1,0:T(8,128)S(1)} all-to-all(f32[32,40,128]{2,1,0:T(8,128)S(1)} %pack.1), channel_id=1, replica_groups=mesh['slab'=8,'dir'=32] {'dir'}, dimensions={0} | all-to-all | bytes 1310720 | tf_op jit(solution)/shard_map/all_to_all | solution.py:173
  33.5 1.9 %collective-permute-start.1 = (f32[32,40,128]{2,1,0:T(8,128)S(1)}, f32[32,40,128]{2,1,0:T(8,128)S(1)}, u32[]{:S(2)}, u32[]{:S(2)}) collective-permute-start(f32[32,40,128]{2,1,0:T(8,128)S(1)} %all_to_all.10.own_ref), channel_id=1, source_target_pairs={{32,0},{64,32},{96,64},{128,96},{160,128},{192,160},{224,192},{33,... | collective-permute-start | bytes 1966088 | tf_op jit(solution)/shard_map/ppermute | solution.py:175
  35.4 2.4 %collective-permute-start = (f32[32,40,128]{2,1,0:T(8,128)S(1)}, f32[32,40,128]{2,1,0:T(8,128)S(1)}, u32[]{:S(2)}, u32[]{:S(2)}) collective-permute-start(f32[32,40,128]{2,1,0:T(8,128)S(1)} %all_to_all.10.own_ref), channel_id=1, source_target_pairs={{0,32},{32,64},{64,96},{96,128},{128,160},{160,192},{192,224},{1,3... | collective-permute-start | bytes 1966088 | tf_op jit(solution)/shard_map/ppermute | solution.py:174
  37.8 0.0 copy-done
  37.8 0.6 own.1
  38.5 1.2 %collective-permute-start.3 = (f32[2,2,128,256]{3,2,1,0:T(8,128)}, f32[2,2,128,256]{3,2,1,0:T(8,128)S(1)}, u32[]{:S(2)}, u32[]{:S(2)}) collective-permute-start(f32[2,2,128,256]{3,2,1,0:T(8,128)} %own_ref.1), channel_id=1, source_target_pairs={{1,0},{2,1},{3,2},{4,3},{5,4},{6,5},{7,6},{8,7},{9,8},{10,9},{11,1... | collective-permute-start | bytes 1572872 | tf_op jit(solution)/shard_map/ppermute | solution.py:189
  39.7 0.9 %collective-permute-start.2 = (f32[2,2,128,256]{3,2,1,0:T(8,128)}, f32[2,2,128,256]{3,2,1,0:T(8,128)S(1)}, u32[]{:S(2)}, u32[]{:S(2)}) collective-permute-start(f32[2,2,128,256]{3,2,1,0:T(8,128)} %own_ref.1), channel_id=1, source_target_pairs={{0,1},{1,2},{2,3},{3,4},{4,5},{5,6},{6,7},{7,8},{8,9},{9,10},{10,1... | collective-permute-start | bytes 1572872 | tf_op jit(solution)/shard_map/ppermute | solution.py:188
  40.6 2.9 %collective-permute-done.1.after_ref = f32[32,40,128]{2,1,0:T(8,128)S(1)} collective-permute-done((f32[32,40,128]{2,1,0:T(8,128)S(1)}, f32[32,40,128]{2,1,0:T(8,128)S(1)}, u32[]{:S(2)}, u32[]{:S(2)}) %collective-permute-start.1) | collective-permute-done | bytes 655392 | tf_op jit(solution)/shard_map/ppermute | solution.py:175
  43.5 3.8 %collective-permute-done.before_ref = f32[32,40,128]{2,1,0:T(8,128)S(1)} collective-permute-done((f32[32,40,128]{2,1,0:T(8,128)S(1)}, f32[32,40,128]{2,1,0:T(8,128)S(1)}, u32[]{:S(2)}, u32[]{:S(2)}) %collective-permute-start) | collective-permute-done | bytes 655392 | tf_op jit(solution)/shard_map/ppermute | solution.py:174
  47.3 7.0 %far.1.incoming_ref = f32[64,8,512]{2,1,0:T(8,128)S(1)} custom-call(s32[32,64]{1,0:T(8,128)S(1)} %bitcast.3, s32[32,64]{1,0:T(8,128)S(1)} %bitcast.4, f32[64,8,512]{2,1,0:T(8,128)S(1)} %get-tuple-element.10.own_ref, f32[64,8,512]{2,1,0:T(8,128)S(1)} %get-tuple-element.11.table_ref, f32[32,40,128]{2,1,0:T(8,128)S(1)} %collective-permute-done.before_ref, ...), custom_call_target="tpu_custom_call" | custom-call | flops 1200000000 | bytes 4734976 | tf_op jit(solution)/shard_map/far/pallas_call | solution.py:145
  54.4 0.0 copy-start.6
  54.4 0.0 collective-permute-done.3.right_ref
  54.4 3.5 %collective-permute-done.2.left_ref = f32[2,2,128,256]{3,2,1,0:T(8,128)S(1)} collective-permute-done((f32[2,2,128,256]{3,2,1,0:T(8,128)}, f32[2,2,128,256]{3,2,1,0:T(8,128)S(1)}, u32[]{:S(2)}, u32[]{:S(2)}) %collective-permute-start.2) | collective-permute-done | bytes 524320 | tf_op jit(solution)/shard_map/ppermute | solution.py:188
  57.9 0.0 copy-done.1
  57.9 1.4 %down.1 = f32[32,32,128]{2,1,0:T(8,128)} custom-call(f32[64,8,512]{2,1,0:T(8,128)S(1)} %far.1.incoming_ref, f32[2,128,256]{2,1,0:T(8,128)S(1)} %copy-done.1, f32[2,2,128,256]{3,2,1,0:T(8,128)S(1)} %collective-permute-done.2.left_ref, f32[2,2,128,256]{3,2,1,0:T(8,128)S(1)} %collective-permute-done.3.right_ref), custom_call_target="tpu_custom_call" | custom-call | flops 402000000 | bytes 2883584 | tf_op jit(solution)/shard_map/down/pallas_call | solution.py:145
  59.3 5.8 %all-to-all-start.1 = ((f32[32,32,128]{2,1,0:T(8,128)}), f32[32,32,128]{2,1,0:T(8,128)S(1)}, u32[]{:S(2)}, u32[]{:S(2)}) async-start(f32[32,32,128]{2,1,0:T(8,128)} %down.1), calls=%async_computation.1 | async-start | bytes 1048576 | tf_op jit(solution)/shard_map/all_to_all | solution.py:206
  65.1 0.0 copy-start.5
  65.1 1.7 %copy-done.5 = f32[2,2,9,128,128]{4,3,2,1,0:T(8,128)S(1)} copy-done((f32[2,2,9,128,128]{4,3,2,1,0:T(8,128)S(1)}, f32[2,2,9,128,128]{4,3,2,1,0:T(8,128)}, u32[]{:S(2)}) %copy-start.5) | copy-done | bytes 2359320
  66.7 6.7 %near.1.near_ref = f32[2,2,128,256]{3,2,1,0:T(8,128)S(1)} custom-call(s32[2,9]{1,0:T(2,128)S(1)} %copy-done.6, f32[2,2,9,128,128]{4,3,2,1,0:T(8,128)S(1)} %copy-done.5, f32[2,2,128,256]{3,2,1,0:T(8,128)} %own_ref.1, f32[2,2,128,256]{3,2,1,0:T(8,128)S(1)} %collective-permute-done.2.left_ref, f32[2,2,128,256]{3,2,1,0:T(8,128)S(1)} %collective-permute-done.3.right_ref), custom_call_target="tpu_custom_call" | custom-call | flops 1812000000 | bytes 4456520 | tf_op jit(solution)/shard_map/near/pallas_call | solution.py:145
  73.4 9.5 %all-to-all-done.1.far_ref = f32[32,32,128]{2,1,0:T(8,128)S(1)} async-done(((f32[32,32,128]{2,1,0:T(8,128)}), f32[32,32,128]{2,1,0:T(8,128)S(1)}, u32[]{:S(2)}, u32[]{:S(2)}) %all-to-all-start.1) | async-done | bytes 524320 | tf_op jit(solution)/shard_map/all_to_all | solution.py:206
  83.0 1.0 %join.1 = f32[2,2,128,256]{3,2,1,0:T(8,128)} custom-call(f32[32,32,128]{2,1,0:T(8,128)S(1)} %all-to-all-done.1.far_ref, f32[2,2,128,256]{3,2,1,0:T(8,128)S(1)} %near.1.near_ref), custom_call_target="tpu_custom_call" | custom-call | bytes 1572864 | tf_op jit(solution)/shard_map/join/pallas_call | solution.py:145
  (7 shorter events, 0.0 us)
Async XLA Ops:
  0.0 37.8 %copy-start = (f32[2,256,128]{2,1,0:T(8,128)S(1)}, f32[2,256,128]{2,1,0:T(8,128)}, u32[]{:S(2)}) copy-start(f32[2,256,128]{2,1,0:T(8,128)} %aggregate_ref.3) | copy-start | bytes 786436
  0.0 47.3 %copy-start.3 = (s32[64,32]{0,1:T(8,128)S(1)}, s32[64,32]{0,1:T(8,128)}, u32[]{:S(2)}) copy-start(s32[64,32]{0,1:T(8,128)} %param.14) | copy-start | bytes 24580
  0.0 47.3 %copy-start.2 = (s32[64,32]{0,1:T(8,128)S(1)}, s32[64,32]{0,1:T(8,128)}, u32[]{:S(2)}) copy-start(s32[64,32]{0,1:T(8,128)} %param.13) | copy-start | bytes 24580
  0.0 0.7 copy-start.4
  33.5 10.0 %collective-permute-start.1 = (f32[32,40,128]{2,1,0:T(8,128)S(1)}, f32[32,40,128]{2,1,0:T(8,128)S(1)}, u32[]{:S(2)}, u32[]{:S(2)}) collective-permute-start(f32[32,40,128]{2,1,0:T(8,128)S(1)} %all_to_all.10.own_ref), channel_id=1, source_target_pairs={{32,0},{64,32},{96,64},{128,96},{160,128},{192,160},{224,192},{33,... | collective-permute-start | bytes 1966088 | tf_op jit(solution)/shard_map/ppermute | solution.py:175
  35.4 11.9 %collective-permute-start = (f32[32,40,128]{2,1,0:T(8,128)S(1)}, f32[32,40,128]{2,1,0:T(8,128)S(1)}, u32[]{:S(2)}, u32[]{:S(2)}) collective-permute-start(f32[32,40,128]{2,1,0:T(8,128)S(1)} %all_to_all.10.own_ref), channel_id=1, source_target_pairs={{0,32},{32,64},{64,96},{96,128},{128,160},{160,192},{192,224},{1,3... | collective-permute-start | bytes 1966088 | tf_op jit(solution)/shard_map/ppermute | solution.py:174
  38.5 15.9 %collective-permute-start.3 = (f32[2,2,128,256]{3,2,1,0:T(8,128)}, f32[2,2,128,256]{3,2,1,0:T(8,128)S(1)}, u32[]{:S(2)}, u32[]{:S(2)}) collective-permute-start(f32[2,2,128,256]{3,2,1,0:T(8,128)} %own_ref.1), channel_id=1, source_target_pairs={{1,0},{2,1},{3,2},{4,3},{5,4},{6,5},{7,6},{8,7},{9,8},{10,9},{11,1... | collective-permute-start | bytes 1572872 | tf_op jit(solution)/shard_map/ppermute | solution.py:189
  39.7 18.2 %collective-permute-start.2 = (f32[2,2,128,256]{3,2,1,0:T(8,128)}, f32[2,2,128,256]{3,2,1,0:T(8,128)S(1)}, u32[]{:S(2)}, u32[]{:S(2)}) collective-permute-start(f32[2,2,128,256]{3,2,1,0:T(8,128)} %own_ref.1), channel_id=1, source_target_pairs={{0,1},{1,2},{2,3},{3,4},{4,5},{5,6},{6,7},{7,8},{8,9},{9,10},{10,1... | collective-permute-start | bytes 1572872 | tf_op jit(solution)/shard_map/ppermute | solution.py:188
  47.3 10.6 %copy-start.1 = (f32[2,128,256]{2,1,0:T(8,128)S(1)}, f32[2,128,256]{2,1,0:T(8,128)}, u32[]{:S(2)}) copy-start(f32[2,128,256]{2,1,0:T(8,128)} %disaggregate_ref.1) | copy-start | bytes 786436
  54.4 10.7 %copy-start.6 = (s32[2,9]{1,0:T(2,128)S(1)}, s32[2,9]{1,0:T(2,128)}, u32[]{:S(2)}) copy-start(s32[2,9]{1,0:T(2,128)} %index_ref.1) | copy-start | bytes 220
  59.3 23.7 %all-to-all-start.1 = ((f32[32,32,128]{2,1,0:T(8,128)}), f32[32,32,128]{2,1,0:T(8,128)S(1)}, u32[]{:S(2)}, u32[]{:S(2)}) async-start(f32[32,32,128]{2,1,0:T(8,128)} %down.1), calls=%async_computation.1 | async-start | bytes 1048576 | tf_op jit(solution)/shard_map/all_to_all | solution.py:206
  65.1 1.7 %copy-start.5 = (f32[2,2,9,128,128]{4,3,2,1,0:T(8,128)S(1)}, f32[2,2,9,128,128]{4,3,2,1,0:T(8,128)}, u32[]{:S(2)}) copy-start(f32[2,2,9,128,128]{4,3,2,1,0:T(8,128)} %blocks_ref.1) | copy-start | bytes 7077892

commit v2 on v1

v2 whole, which is shorter than its diff:
```python
import functools

import jax
import jax.numpy as jnp
from jax import lax
from jax.experimental import pallas as pl
from jax.experimental.pallas import tpu as pltpu
from jax.sharding import PartitionSpec as P

F32, BF16 = jnp.float32, jnp.bfloat16
VMEM = pltpu.MemorySpace.VMEM
SMEM = pltpu.MemorySpace.SMEM
MIB = 1 << 20
RE_IM_ROWS = 32
GROUP = 4


def split(x):
    high = x.astype(BF16)
    return high, (x - high.astype(F32)).astype(BF16)


def dot3(left, right, contract):
    def one(a, b):
        return lax.dot_general(a, b, (contract, ((), ())), preferred_element_type=F32)

    return one(left[0], right[0]) + (one(left[0], right[1]) + one(left[1], right[0]))


NN_FORM = ((1,), (0,))
NT_FORM = ((1,), (1,))


def pack_kernel(currents_ref, translations_ref, out_ref):
    devices, rows, lanes = out_ref.shape
    parts, boxes, _, illum = currents_ref.shape
    own = illum // devices
    for c in range(parts):
        for b in range(boxes):
            turned = currents_ref[c, b].T.reshape(devices, own, lanes)
            out_ref[:, pl.ds((c * boxes + b) * own, own), :] = turned
    table = jnp.concatenate([translations_ref[0], translations_ref[1]], axis=1)
    first = parts * boxes * own
    out_ref[:, first:, :] = jnp.broadcast_to(table[None], (devices, rows - first, lanes))


def near_kernel(index_ref, blocks_ref, own_ref, left_ref, right_ref, out_ref, high_ref, low_ref):
    boxes, entries = blocks_ref.shape[1], blocks_ref.shape[2]
    width = own_ref.shape[3]
    for place, ref in enumerate((left_ref, own_ref, right_ref)):
        for b in range(boxes):
            slot = place * boxes + b
            real, imag = split(ref[0, b]), split(ref[1, b])
            for store, x, y in ((high_ref, real[0], imag[0]), (low_ref, real[1], imag[1])):
                store[slot] = jnp.concatenate(
                    [jnp.concatenate([x, y], axis=1), jnp.concatenate([-y, x], axis=1)], axis=0
                )
    for b in range(boxes):

        def step(j, total):
            source = index_ref[b, j]
            block = split(jnp.concatenate([blocks_ref[0, b, j], blocks_ref[1, b, j]], axis=1))
            return total + dot3(block, (high_ref[source], low_ref[source]), NN_FORM)

        total = lax.fori_loop(0, entries, step, jnp.zeros((blocks_ref.shape[3], 2 * width), F32))
        out_ref[0, b] = total[:, :width]
        out_ref[1, b] = total[:, width:]


def radiate(block_ref, weights):
    devices, rows, lanes = block_ref.shape
    half = RE_IM_ROWS // 2
    real = block_ref[:, :half, :].reshape(devices * half, lanes)
    imag = block_ref[:, half : 2 * half, :].reshape(devices * half, lanes)
    return dot3(split(jnp.concatenate([real, imag], axis=1)), weights, NT_FORM)


def complex_rows(ref):
    real, imag = ref[0], ref[1]
    return jnp.concatenate(
        [jnp.concatenate([real, -imag], axis=1), jnp.concatenate([imag, real], axis=1)], axis=0
    )


def plan_kernel(source_ref, shift_ref, first_ref, source2_ref, shift2_ref, count_ref):
    entries, boxes = source_ref.shape
    odd = lax.axis_index("slab") % 2
    source, shift = source_ref[...], shift_ref[...]
    part, place = source // boxes, source % boxes
    away = part == 2 * odd
    first_ref[...] = jnp.where(part == 1, place, jnp.where(away, 2 * boxes, boxes + place))
    one = away.astype(jnp.int32)
    position = jnp.zeros((1, boxes), jnp.int32)
    row = lax.broadcasted_iota(jnp.int32, (entries, boxes), 0)
    moved_source = jnp.zeros((entries, boxes), jnp.int32)
    moved_shift = jnp.zeros((entries, boxes), jnp.int32)
    for i in range(entries):
        here = (row == position) & (one[i : i + 1] == 1)
        moved_source = jnp.where(here, place[i : i + 1], moved_source)
        moved_shift = jnp.where(here, shift[i : i + 1], moved_shift)
        position = position + one[i : i + 1]
    source2_ref[...] = jnp.where(row < position, moved_source, boxes)
    shift2_ref[...] = moved_shift
    count_ref[...] = jnp.broadcast_to((position + (GROUP - 1)) // GROUP, count_ref.shape)


def own_kernel(own_ref, aggregate_ref, disaggregate_ref, radiated_ref, table_ref, up0_ref, up1_ref, down0_ref, down1_ref):
    boxes, sub, width = radiated_ref.shape
    up = split(complex_rows(aggregate_ref))
    up0_ref[...], up1_ref[...] = up
    down0_ref[...], down1_ref[...] = split(complex_rows(disaggregate_ref))
    radiated_ref[...] = radiate(own_ref, up).reshape(boxes, sub, width)
    devices, rows, lanes = own_ref.shape
    table = own_ref[:, RE_IM_ROWS:, :].reshape(devices * (rows - RE_IM_ROWS), lanes).T
    half = lanes // 2
    wide = jnp.concatenate([table[:half], table[half:]], axis=1)
    table_ref[...] = jnp.broadcast_to(wide[:, None, :], table_ref.shape)


def add_entry(total, radiated_ref, q, table_ref, t):
    half = table_ref.shape[2] // 2
    xr, xi = radiated_ref[q, :, :half], radiated_ref[q, :, half:]
    tr, ti = table_ref[t, :, :half], table_ref[t, :, half:]
    return total[0] + (tr * xr - ti * xi), total[1] + (tr * xi + ti * xr)


def mid_kernel(
    source_ref, shift_ref, own_ref, table_ref, block_ref, up0_ref, up1_ref, out_ref, radiated_ref
):
    boxes, sub, width = own_ref.shape
    half = width // 2
    radiated_ref[:boxes] = own_ref[...]
    radiated_ref[boxes : 2 * boxes] = radiate(block_ref, (up0_ref[...], up1_ref[...])).reshape(boxes, sub, width)
    radiated_ref[2 * boxes] = jnp.zeros((sub, width), F32)

    def one_box(g, carry):
        total = (jnp.zeros((sub, half), F32), jnp.zeros((sub, half), F32))
        for i in range(source_ref.shape[0]):
            total = add_entry(total, radiated_ref, source_ref[i, g], table_ref, shift_ref[i, g])
        out_ref[g, :, :half], out_ref[g, :, half:] = total
        return carry

    lax.fori_loop(0, boxes, one_box, 0)


def far_kernel(
    source_ref, shift_ref, count_ref, mid_ref, table_ref, block_ref, up0_ref, up1_ref, down0_ref, down1_ref,
    out_ref, radiated_ref, incoming_ref,
):
    boxes, sub, width = mid_ref.shape
    half = width // 2
    radiated_ref[:boxes] = radiate(block_ref, (up0_ref[...], up1_ref[...])).reshape(boxes, sub, width)
    radiated_ref[boxes] = jnp.zeros((sub, width), F32)

    def one_box(g, carry):
        def group(n, total):
            for i in range(GROUP):
                e = n * GROUP + i
                total = add_entry(total, radiated_ref, source_ref[e, g], table_ref, shift_ref[e, g])
            return total

        total = lax.fori_loop(0, count_ref[0, g], group, (mid_ref[g, :, :half], mid_ref[g, :, half:]))
        incoming_ref[g, :, :half], incoming_ref[g, :, half:] = total
        return carry

    lax.fori_loop(0, boxes, one_box, 0)
    far = dot3(split(incoming_ref[...].reshape(boxes * sub, width)), (down0_ref[...], down1_ref[...]), NT_FORM)
    devices, rows, lanes = out_ref.shape
    out_ref[:, : rows // 2, :] = far[:, :lanes].reshape(devices, rows // 2, lanes)
    out_ref[:, rows // 2 :, :] = far[:, lanes:].reshape(devices, rows // 2, lanes)


def join_kernel(far_ref, near_ref, out_ref):
    parts, boxes, lanes, illum = out_ref.shape
    devices = far_ref.shape[0]
    own = illum // devices
    for c in range(parts):
        for b in range(boxes):
            turned = far_ref[:, pl.ds((c * boxes + b) * own, own), :].reshape(illum, lanes)
            out_ref[c, b] = near_ref[c, b] + turned.T


def call(kernel, outs, kinds, scratch=(), limit=16, micros=1, name=None):
    specs = [pl.BlockSpec(memory_space=kind) for kind in kinds]

    def run(*args):
        return pl.pallas_call(
            kernel,
            out_shape=outs,
            in_specs=specs,
            out_specs=jax.tree.map(lambda _: pl.BlockSpec(memory_space=VMEM), outs),
            scratch_shapes=list(scratch),
            compiler_params=pltpu.CompilerParams(vmem_limit_bytes=limit * MIB),
            cost_estimate=pl.CostEstimate(flops=micros * 1_000_000_000, bytes_accessed=0, transcendentals=0),
            name=name,
        )(*args)

    return run


def shape(*dims, kind=F32):
    return jax.ShapeDtypeStruct(dims, kind)


def body(currents, near_blocks, near_index, aggregate, translations, inter_source, inter_shift, disaggregate):
    devices = lax.axis_size("dir")
    slabs = lax.axis_size("slab")
    parts, box_dev, unknowns, illum = currents.shape
    own = illum // devices
    width = 2 * aggregate.shape[1]
    boxes, entries = inter_source.shape
    ops = translations.shape[1]
    rows = parts * box_dev * own
    ring = [(i, (i + 1) % devices) for i in range(devices)]
    pairs_of = [[(i, i + 1) for i in range(start, slabs - 1, 2)] for start in (0, 1)]
    same, cross = [p + [(j, i) for i, j in p] for p in pairs_of]

    packed = call(pack_kernel, shape(devices, rows + translations.shape[2], unknowns), (VMEM, VMEM), name="pack")(
        currents, jnp.transpose(translations, (0, 2, 1))
    )
    mine = lax.all_to_all(packed, "dir", 0, 0, tiled=True)
    index = shape(entries, boxes, kind=jnp.int32)
    first, source2, shift2, count = call(
        plan_kernel, (index, index, index, shape(8, boxes, kind=jnp.int32)), (VMEM, VMEM), name="plan"
    )(inter_source.T, inter_shift.T)
    mine, beside, first, source2, shift2, count = lax.optimization_barrier(
        (mine, currents, first, source2, shift2, count)
    )
    sent = mine[:, :rows]
    from_cross = lax.ppermute(sent, "slab", cross)
    from_same = lax.ppermute(sent, "slab", same)
    left = lax.ppermute(beside, "dir", ring)
    right = lax.ppermute(beside, "dir", [(j, i) for i, j in ring])
    field = shape(boxes, own, width)
    up, down = shape(width, 2 * unknowns, kind=BF16), shape(2 * unknowns, width, kind=BF16)
    radiated, table, up0, up1, down0, down1 = call(
        own_kernel, (field, shape(ops, own, width), up, up, down, down), (VMEM,) * 3, name="own"
    )(mine, aggregate, disaggregate)
    partial = call(
        mid_kernel,
        field,
        (SMEM, SMEM) + (VMEM,) * 5,
        scratch=(pltpu.VMEM((2 * boxes + 1, own, width), F32),),
        micros=6,
        name="mid",
    )(first, inter_shift.T, radiated, table, from_same, up0, up1)
    far = call(
        far_kernel,
        shape(devices, rows, unknowns),
        (SMEM,) * 3 + (VMEM,) * 7,
        scratch=(pltpu.VMEM((boxes + 1, own, width), F32), pltpu.VMEM((boxes, own, width), F32)),
        micros=5,
        name="far",
    )(source2, shift2, count, partial, table, from_cross, up0, up1, down0, down1)
    back = lax.all_to_all(far, "dir", 0, 0, tiled=True)

    stack = pltpu.VMEM((3 * box_dev, 2 * unknowns, 2 * illum), BF16)
    near = call(
        near_kernel, shape(*currents.shape), (SMEM,) + (VMEM,) * 4, scratch=(stack, stack), micros=20, name="near"
    )(near_index, near_blocks, currents, left, right)
    return call(join_kernel, shape(*currents.shape), (VMEM, VMEM), name="join")(back, near)


def solution(mesh):
    in_specs = (
        P(None, ("slab", "dir"), None, None),
        P(None, ("slab", "dir"), None, None, None),
        P(("slab", "dir"), None),
        P(),
        P(None, None, "dir"),
        P("slab", None),
        P("slab", None),
        P(),
    )
    out_specs = P(None, ("slab", "dir"), None, None)
    return jax.shard_map(body, mesh=mesh, in_specs=in_specs, out_specs=out_specs, check_vma=False)
```

time: 84.3 us -> 83.5 us (level)
  blocking collectives: 31.5 us -> 0 us
  starting transfers between devices: 12.2 us -> 23.4 us
  waiting for transfers between devices: 19.8 us -> 30.8 us
  Pallas kernels: 18 us -> 25 us
  local copies, waits for them, and re-layouts: 2.41 us -> 3.65 us
    all_to_all x1 -> x0, blocking collectives: 31.5 us -> none  [body(): mine = lax.all_to_all(packed, 'dir', 0, 0, tiled=True)]
    all_to_all x0 -> x1, waiting for transfers between devices: none -> 19.9 us  [body(): mine = lax.all_to_all(packed, 'dir', 0, 0, tiled=True)]
    all_to_all x0 -> x1, starting transfers between devices: none -> 11.5 us  [body(): mine = lax.all_to_all(packed, 'dir', 0, 0, tiled=True)]
    pallas_call x6 -> x7, Pallas kernels: 18 us -> 25 us  [run(): pl.pallas_call(kernel, out_shape=outs, in_specs=specs, out_specs=jax.tree...]
    ppermute x2, waiting for transfers between devices: 6.74 us -> 0.01 us  [the longest x1 0.01 us: body(): from_same = lax.ppermute(sent, 'slab', same)]
    ppermute x1, waiting for transfers between devices: 3.5 us -> 0.01 us  [body(): left = lax.ppermute(beside, 'dir', ring)]
    ppermute x1, starting transfers between devices: 1.22 us -> 4.12 us  [body(): right = lax.ppermute(beside, 'dir', [(j, i) for i, j in ring])]
    all_to_all x1, starting transfers between devices: 5.77 us -> 3.89 us  [body(): back = lax.all_to_all(far, 'dir', 0, 0, tiled=True)]
  transfers between devices with their start and end apart: 5 -> 6, of which waited for: 4 -> 2; matrix products, arithmetic and copies ran while one was open for 0% -> 0% of each run, Pallas kernels for 17% -> 28%
where the time goes in v2:
time: 83.5 us; the launch traced here: 83.1 us
  waiting for transfers between devices  30.8 us (37%)
  Pallas kernels  25 us (30%)
  starting transfers between devices  23.4 us (28%)
  local copies, waits for them, and re-layouts  3.65 us (4%)
    pallas_call x7, Pallas kernels, run(): pl.pallas_call(kernel, out_shape=outs, in_specs=specs, out_specs=jax.tree...  25 us
    all_to_all x1, waiting for transfers between devices, body(): mine = lax.all_to_all(packed, 'dir', 0, 0, tiled=True)  19.9 us
    all_to_all x1, starting transfers between devices, body(): mine = lax.all_to_all(packed, 'dir', 0, 0, tiled=True)  11.5 us
    all_to_all x1, waiting for transfers between devices, body(): back = lax.all_to_all(far, 'dir', 0, 0, tiled=True)  10.9 us
    ppermute x1, starting transfers between devices, body(): right = lax.ppermute(beside, 'dir', [(j, i) for i, j in ring])  4.12 us
    all_to_all x1, starting transfers between devices, body(): back = lax.all_to_all(far, 'dir', 0, 0, tiled=True)  3.89 us
    unnamed x22, local copies, waits for them, and re-layouts  3.6 us
    ppermute x1, starting transfers between devices, body(): from_cross = lax.ppermute(sent, 'slab', cross)  2.53 us
  transfers between devices with their start and end apart: 6, of which 2 were waited for; matrix products, arithmetic and copies ran while one was open for 0% of the time, Pallas kernels for 28%

profile of v2, /device:TPU:2, one launch (start us, length us, event | category | flops | bytes accessed | tf_op | source)
XLA Modules:
  0.0 83.1 jit_solution(7759371499702539293)
XLA Ops:
  0.0 1.0 %copy-done.1 = f32[2,2,128,256]{3,2,1,0:T(8,128)S(1)} copy-done((f32[2,2,128,256]{3,2,1,0:T(8,128)S(1)}, f32[2,2,128,256]{3,2,1,0:T(8,128)}, u32[]{:S(2)}) %copy-start.1) | copy-done | bytes 524312
  1.0 0.7 copy-done.7
  1.7 1.1 %pack.1 = f32[32,40,128]{2,1,0:T(8,128)} custom-call(f32[2,2,128,256]{3,2,1,0:T(8,128)S(1)} %copy-done.1, f32[2,8,64]{2,1,0:T(8,128)S(1)} %bitcast.6), custom_call_target="tpu_custom_call" | custom-call | flops 1000000000 | tf_op jit(solution)/shard_map/pack/pallas_call | solution.py:187
  2.8 11.5 %all-to-all-start = ((f32[32,40,128]{2,1,0:T(8,128)}), f32[32,40,128]{2,1,0:T(8,128)S(1)}, u32[]{:S(2)}, u32[]{:S(2)}) async-start(f32[32,40,128]{2,1,0:T(8,128)} %pack.1), calls=%async_computation | async-start | bytes 1310720 | tf_op jit(solution)/shard_map/all_to_all | solution.py:221
  14.3 0.0 copy-start.3
  14.3 0.0 copy-start.4
  14.4 0.2 plan.1
  14.6 19.9 %all-to-all-done.own_ref = f32[32,40,128]{2,1,0:T(8,128)S(1)} async-done(((f32[32,40,128]{2,1,0:T(8,128)}), f32[32,40,128]{2,1,0:T(8,128)S(1)}, u32[]{:S(2)}, u32[]{:S(2)}) %all-to-all-start) | async-done | bytes 655392 | tf_op jit(solution)/shard_map/all_to_all | solution.py:221
  34.5 0.1 slice.3
  34.6 0.1 collective-permute-start
  34.7 2.5 %collective-permute-start.1 = (f32[32,32,128]{2,1,0:T(8,128)S(1)}, f32[32,32,128]{2,1,0:T(8,128)S(1)}, u32[]{:S(2)}, u32[]{:S(2)}) collective-permute-start(f32[32,32,128]{2,1,0:T(8,128)S(1)} %slice.3), channel_id=1, source_target_pairs={{32,64},{96,128},{160,192},{64,32},{128,96},{192,160},{33,65},{97,... | collective-permute-start | bytes 1572872 | tf_op jit(solution)/shard_map/ppermute | solution.py:230
  37.2 1.3 %collective-permute-start.2 = (f32[2,2,128,256]{3,2,1,0:T(8,128)S(1)}, f32[2,2,128,256]{3,2,1,0:T(8,128)}, u32[]{:S(2)}, u32[]{:S(2)}) collective-permute-start(f32[2,2,128,256]{3,2,1,0:T(8,128)S(1)} %copy-done.2), channel_id=1, source_target_pairs={{0,1},{1,2},{2,3},{3,4},{4,5},{5,6},{6,7},{7,8},{8,9},{9,10},{10,1... | collective-permute-start | bytes 1572872 | tf_op jit(solution)/shard_map/ppermute | solution.py:232
  38.5 4.1 %collective-permute-start.3 = (f32[2,2,128,256]{3,2,1,0:T(8,128)S(1)}, f32[2,2,128,256]{3,2,1,0:T(8,128)}, u32[]{:S(2)}, u32[]{:S(2)}) collective-permute-start(f32[2,2,128,256]{3,2,1,0:T(8,128)S(1)} %copy-done.2), channel_id=1, source_target_pairs={{1,0},{2,1},{3,2},{4,3},{5,4},{6,5},{7,6},{8,7},{9,8},{10,9},{11,1... | collective-permute-start | bytes 1572872 | tf_op jit(solution)/shard_map/ppermute | solution.py:233
  42.6 0.7 own.1
  43.4 6.7 %mid.1.mid_ref = f32[64,8,512]{2,1,0:T(8,128)S(1)} custom-call(s32[32,64]{1,0:T(8,128)S(1)} %get-tuple-element.28.source_ref, s32[32,64]{1,0:T(8,128)S(1)} %bitcast.5, f32[64,8,512]{2,1,0:T(8,128)S(1)} %get-tuple-element.30.own_ref, f32[64,8,512]{2,1,0:T(8,128)S(1)} %get-tuple-element.31.table_ref, f32[32,32,128]{2,1,0:T(8,128)S(1)} %collective-permute-done.block_ref, ...), custom_call_target="tpu_custom_call" | custom-call | flops 6000000000 | tf_op jit(solution)/shard_map/mid/pallas_call | solution.py:187
  50.1 0.0 copy-start
  50.1 0.0 copy-start.8
  50.1 8.5 %far.1 = f32[32,32,128]{2,1,0:T(8,128)} custom-call(s32[32,64]{1,0:T(8,128)S(1)} %get-tuple-element.25.source_ref, s32[32,64]{1,0:T(8,128)S(1)} %get-tuple-element.26.shift_ref, s32[8,64]{1,0:T(8,128)S(1)} %get-tuple-element.27.count_ref, f32[64,8,512]{2,1,0:T(8,128)S(1)} %mid.1.mid_ref, f32[64,8,512]{2,1,0:T(8,128)S(1)} %get-tuple-element.31.table_ref, ...), custom_call_target="tpu_custom_call" | custom-call | flops 5000000000 | tf_op jit(solution)/shard_map/far/pallas_call | solution.py:187
  58.6 3.9 %all-to-all-start.1 = ((f32[32,32,128]{2,1,0:T(8,128)}), f32[32,32,128]{2,1,0:T(8,128)S(1)}, u32[]{:S(2)}, u32[]{:S(2)}) async-start(f32[32,32,128]{2,1,0:T(8,128)} %far.1), calls=%async_computation.1 | async-start | bytes 1048576 | tf_op jit(solution)/shard_map/all_to_all | solution.py:255
  62.6 6.8 %near.1.near_ref = f32[2,2,128,256]{3,2,1,0:T(8,128)S(1)} custom-call(s32[2,9]{1,0:T(2,128)S(1)} %copy-done.8, f32[2,2,9,128,128]{4,3,2,1,0:T(8,128)S(1)} %copy-done, f32[2,2,128,256]{3,2,1,0:T(8,128)S(1)} %copy-done.2, f32[2,2,128,256]{3,2,1,0:T(8,128)} %collective-permute-done.2.left_ref, f32[2,2,128,256]{3,2,1,0:T(8,128)} %collective-permute-done.3.right_ref), custom_call_target="tpu_custom_call" | custom-call | flops 20000000000 | tf_op jit(solution)/shard_map/near/pallas_call | solution.py:187
  69.4 0.8 copy-done.9
  70.2 10.9 %all-to-all-done.1.far_ref = f32[32,32,128]{2,1,0:T(8,128)S(1)} async-done(((f32[32,32,128]{2,1,0:T(8,128)}), f32[32,32,128]{2,1,0:T(8,128)S(1)}, u32[]{:S(2)}, u32[]{:S(2)}) %all-to-all-start.1) | async-done | bytes 524320 | tf_op jit(solution)/shard_map/all_to_all | solution.py:255
  81.0 1.0 %copy-done.10 = f32[2,2,128,256]{3,2,1,0:T(8,128)S(1)} copy-done((f32[2,2,128,256]{3,2,1,0:T(8,128)S(1)}, f32[2,2,128,256]{3,2,1,0:T(8,128)}, u32[]{:S(2)}) %copy-start.10) | copy-done | bytes 524312
  82.1 1.0 %join.1 = f32[2,2,128,256]{3,2,1,0:T(8,128)} custom-call(f32[32,32,128]{2,1,0:T(8,128)S(1)} %all-to-all-done.1.far_ref, f32[2,2,128,256]{3,2,1,0:T(8,128)S(1)} %copy-done.10), custom_call_target="tpu_custom_call" | custom-call | flops 1000000000 | tf_op jit(solution)/shard_map/join/pallas_call | solution.py:187
  (18 shorter events, 0.0 us)
Async XLA Ops:
  0.0 1.0 %copy-start.1 = (f32[2,2,128,256]{3,2,1,0:T(8,128)S(1)}, f32[2,2,128,256]{3,2,1,0:T(8,128)}, u32[]{:S(2)}) copy-start(f32[2,2,128,256]{3,2,1,0:T(8,128)} %own_ref.1) | copy-start | bytes 1572868
  1.0 0.7 copy-start.7
  1.7 12.6 %copy-start.5 = (s32[64,32]{0,1:T(8,128)S(1)}, s32[64,32]{0,1:T(8,128)}, u32[]{:S(2)}) copy-start(s32[64,32]{0,1:T(8,128)} %param.13) | copy-start | bytes 24580
  1.7 12.6 %copy-start.6 = (s32[64,32]{0,1:T(8,128)S(1)}, s32[64,32]{0,1:T(8,128)}, u32[]{:S(2)}) copy-start(s32[64,32]{0,1:T(8,128)} %param.14) | copy-start | bytes 24580
  2.8 31.7 %all-to-all-start = ((f32[32,40,128]{2,1,0:T(8,128)}), f32[32,40,128]{2,1,0:T(8,128)S(1)}, u32[]{:S(2)}, u32[]{:S(2)}) async-start(f32[32,40,128]{2,1,0:T(8,128)} %pack.1), calls=%async_computation | async-start | bytes 1310720 | tf_op jit(solution)/shard_map/all_to_all | solution.py:221
  14.3 22.9 %copy-start.2 = (f32[2,2,128,256]{3,2,1,0:T(8,128)S(1)}, f32[2,2,128,256]{3,2,1,0:T(8,128)}, u32[]{:S(2)}) copy-start(f32[2,2,128,256]{3,2,1,0:T(8,128)} %own_ref.1) | copy-start | bytes 1572868
  14.3 28.3 %copy-start.3 = (f32[2,256,128]{2,1,0:T(8,128)S(1)}, f32[2,256,128]{2,1,0:T(8,128)}, u32[]{:S(2)}) copy-start(f32[2,256,128]{2,1,0:T(8,128)} %aggregate_ref.1) | copy-start | bytes 786436
  14.3 28.3 %copy-start.4 = (f32[2,128,256]{2,1,0:T(8,128)S(1)}, f32[2,128,256]{2,1,0:T(8,128)}, u32[]{:S(2)}) copy-start(f32[2,128,256]{2,1,0:T(8,128)} %disaggregate_ref.1) | copy-start | bytes 786436
  34.6 8.8 %collective-permute-start = (f32[32,32,128]{2,1,0:T(8,128)S(1)}, f32[32,32,128]{2,1,0:T(8,128)S(1)}, u32[]{:S(2)}, u32[]{:S(2)}) collective-permute-start(f32[32,32,128]{2,1,0:T(8,128)S(1)} %slice.3), channel_id=1, source_target_pairs={{0,32},{64,96},{128,160},{192,224},{32,0},{96,64},{160,128},{224,1... | collective-permute-start | bytes 1572872 | tf_op jit(solution)/shard_map/ppermute | solution.py:231
  34.7 15.4 %collective-permute-start.1 = (f32[32,32,128]{2,1,0:T(8,128)S(1)}, f32[32,32,128]{2,1,0:T(8,128)S(1)}, u32[]{:S(2)}, u32[]{:S(2)}) collective-permute-start(f32[32,32,128]{2,1,0:T(8,128)S(1)} %slice.3), channel_id=1, source_target_pairs={{32,64},{96,128},{160,192},{64,32},{128,96},{192,160},{33,65},{97,... | collective-permute-start | bytes 1572872 | tf_op jit(solution)/shard_map/ppermute | solution.py:230
  37.2 25.3 %collective-permute-start.2 = (f32[2,2,128,256]{3,2,1,0:T(8,128)S(1)}, f32[2,2,128,256]{3,2,1,0:T(8,128)}, u32[]{:S(2)}, u32[]{:S(2)}) collective-permute-start(f32[2,2,128,256]{3,2,1,0:T(8,128)S(1)} %copy-done.2), channel_id=1, source_target_pairs={{0,1},{1,2},{2,3},{3,4},{4,5},{5,6},{6,7},{7,8},{8,9},{9,10},{10,1... | collective-permute-start | bytes 1572872 | tf_op jit(solution)/shard_map/ppermute | solution.py:232
  38.5 24.0 %collective-permute-start.3 = (f32[2,2,128,256]{3,2,1,0:T(8,128)S(1)}, f32[2,2,128,256]{3,2,1,0:T(8,128)}, u32[]{:S(2)}, u32[]{:S(2)}) collective-permute-start(f32[2,2,128,256]{3,2,1,0:T(8,128)S(1)} %copy-done.2), channel_id=1, source_target_pairs={{1,0},{2,1},{3,2},{4,3},{5,4},{6,5},{7,6},{8,7},{9,8},{10,9},{11,1... | collective-permute-start | bytes 1572872 | tf_op jit(solution)/shard_map/ppermute | solution.py:233
  50.1 12.5 %copy-start = (f32[2,2,9,128,128]{4,3,2,1,0:T(8,128)S(1)}, f32[2,2,9,128,128]{4,3,2,1,0:T(8,128)}, u32[]{:S(2)}) copy-start(f32[2,2,9,128,128]{4,3,2,1,0:T(8,128)} %blocks_ref.1) | copy-start | bytes 7077892
  50.1 12.5 %copy-start.8 = (s32[2,9]{1,0:T(2,128)S(1)}, s32[2,9]{1,0:T(2,128)}, u32[]{:S(2)}) copy-start(s32[2,9]{1,0:T(2,128)} %index_ref.1) | copy-start | bytes 220
  58.6 22.4 %all-to-all-start.1 = ((f32[32,32,128]{2,1,0:T(8,128)}), f32[32,32,128]{2,1,0:T(8,128)S(1)}, u32[]{:S(2)}, u32[]{:S(2)}) async-start(f32[32,32,128]{2,1,0:T(8,128)} %far.1), calls=%async_computation.1 | async-start | bytes 1048576 | tf_op jit(solution)/shard_map/all_to_all | solution.py:255
  69.4 0.8 copy-start.9
  81.0 1.0 %copy-start.10 = (f32[2,2,128,256]{3,2,1,0:T(8,128)S(1)}, f32[2,2,128,256]{3,2,1,0:T(8,128)}, u32[]{:S(2)}) copy-start(f32[2,2,128,256]{3,2,1,0:T(8,128)} %copy-done.9) | copy-start | bytes 1572868

commit v3 on v2

--- a/solution.py
+++ b/solution.py
@@ -12,7 +12,8 @@
 SMEM = pltpu.MemorySpace.SMEM
 MIB = 1 << 20
 RE_IM_ROWS = 32
-GROUP = 4
+EARLY, LATE = 24, 14
+LIST_ROWS = 8
 
 
 def split(x):
@@ -82,26 +83,30 @@
     )
 
 
-def plan_kernel(source_ref, shift_ref, first_ref, source2_ref, shift2_ref, count_ref):
+def plan_kernel(source_ref, shift_ref, early_ref, late_ref):
     entries, boxes = source_ref.shape
     odd = lax.axis_index("slab") % 2
     source, shift = source_ref[...], shift_ref[...]
     part, place = source // boxes, source % boxes
     away = part == 2 * odd
-    first_ref[...] = jnp.where(part == 1, place, jnp.where(away, 2 * boxes, boxes + place))
-    one = away.astype(jnp.int32)
-    position = jnp.zeros((1, boxes), jnp.int32)
     row = lax.broadcasted_iota(jnp.int32, (entries, boxes), 0)
-    moved_source = jnp.zeros((entries, boxes), jnp.int32)
-    moved_shift = jnp.zeros((entries, boxes), jnp.int32)
-    for i in range(entries):
-        here = (row == position) & (one[i : i + 1] == 1)
-        moved_source = jnp.where(here, place[i : i + 1], moved_source)
-        moved_shift = jnp.where(here, shift[i : i + 1], moved_shift)
-        position = position + one[i : i + 1]
-    source2_ref[...] = jnp.where(row < position, moved_source, boxes)
-    shift2_ref[...] = moved_shift
-    count_ref[...] = jnp.broadcast_to((position + (GROUP - 1)) // GROUP, count_ref.shape)
+    for ref, chosen, where, zeros in (
+        (early_ref, jnp.logical_not(away), jnp.where(part == 1, place, boxes + place), 2 * boxes),
+        (late_ref, away, place, boxes),
+    ):
+        one = chosen.astype(jnp.int32)
+        count = jnp.zeros((1, boxes), jnp.int32)
+        front_where = jnp.full((entries, boxes), zeros, jnp.int32)
+        front_shift = jnp.zeros((entries, boxes), jnp.int32)
+        for i in range(entries):
+            here = (row == count) & (one[i : i + 1] == 1)
+            front_where = jnp.where(here, where[i : i + 1], front_where)
+            front_shift = jnp.where(here, shift[i : i + 1], front_shift)
+            count = count + one[i : i + 1]
+        ref[...] = jnp.zeros(ref.shape, jnp.int32)
+        ref[:entries, :boxes] = front_where
+        ref[entries : 2 * entries, :boxes] = front_shift
+        ref[2 * entries :, :boxes] = jnp.broadcast_to(count, (ref.shape[0] - 2 * entries, boxes))
 
 
 def own_kernel(own_ref, aggregate_ref, disaggregate_ref, radiated_ref, table_ref, up0_ref, up1_ref, down0_ref, down1_ref):
@@ -117,53 +122,68 @@
     table_ref[...] = jnp.broadcast_to(wide[:, None, :], table_ref.shape)
 
 
-def add_entry(total, radiated_ref, q, table_ref, t):
+def add_entries(list_ref, g, numbers, total, radiated_ref, table_ref):
+    entries = list_ref.shape[0] // 2 - LIST_ROWS // 2
     half = table_ref.shape[2] // 2
-    xr, xi = radiated_ref[q, :, :half], radiated_ref[q, :, half:]
-    tr, ti = table_ref[t, :, :half], table_ref[t, :, half:]
-    return total[0] + (tr * xr - ti * xi), total[1] + (tr * xi + ti * xr)
+    real, imag = total
+    for n in numbers:
+        q, t = list_ref[n, g], list_ref[entries + n, g]
+        xr, xi = radiated_ref[q, :, :half], radiated_ref[q, :, half:]
+        tr, ti = table_ref[t, :, :half], table_ref[t, :, half:]
+        real, imag = real + (tr * xr - ti * xi), imag + (tr * xi + ti * xr)
+    return real, imag
+
+
+def add_all(list_ref, fixed, start, out_ref, radiated_ref, table_ref):
+    entries = list_ref.shape[0] // 2 - LIST_ROWS // 2
+    half = table_ref.shape[2] // 2
+
+    def one_box(g, carry):
+        total = add_entries(list_ref, g, range(fixed), start(g), radiated_ref, table_ref)
+        out_ref[g, :, :half], out_ref[g, :, half:] = total
+        count = list_ref[2 * entries, g]
+
+        @pl.when(count > fixed)
+        def _():
+            def rest(n, total):
+                return add_entries(list_ref, g, (n,), total, radiated_ref, table_ref)
+
+            both = lax.fori_loop(fixed, count, rest, (out_ref[g, :, :half], out_ref[g, :, half:]))
+            out_ref[g, :, :half], out_ref[g, :, half:] = both
+
+        return carry
+
+    lax.fori_loop(0, out_ref.shape[0], one_box, 0)
 
 
 def mid_kernel(
-    source_ref, shift_ref, own_ref, table_ref, block_ref, up0_ref, up1_ref, out_ref, radiated_ref
+    lists_ref, own_ref, table_ref, block_ref, up0_ref, up1_ref, out_ref, radiated_ref, list_ref, sem
 ):
+    staged = pltpu.make_async_copy(lists_ref, list_ref, sem)
+    staged.start()
     boxes, sub, width = own_ref.shape
-    half = width // 2
     radiated_ref[:boxes] = own_ref[...]
     radiated_ref[boxes : 2 * boxes] = radiate(block_ref, (up0_ref[...], up1_ref[...])).reshape(boxes, sub, width)
     radiated_ref[2 * boxes] = jnp.zeros((sub, width), F32)
-
-    def one_box(g, carry):
-        total = (jnp.zeros((sub, half), F32), jnp.zeros((sub, half), F32))
-        for i in range(source_ref.shape[0]):
-            total = add_entry(total, radiated_ref, source_ref[i, g], table_ref, shift_ref[i, g])
-        out_ref[g, :, :half], out_ref[g, :, half:] = total
-        return carry
-
-    lax.fori_loop(0, boxes, one_box, 0)
+    staged.wait()
+    nothing = jnp.zeros((sub, width // 2), F32)
+    add_all(list_ref, EARLY, lambda g: (nothing, nothing), out_ref, radiated_ref, table_ref)
 
 
 def far_kernel(
-    source_ref, shift_ref, count_ref, mid_ref, table_ref, block_ref, up0_ref, up1_ref, down0_ref, down1_ref,
-    out_ref, radiated_ref, incoming_ref,
+    lists_ref, mid_ref, table_ref, block_ref, up0_ref, up1_ref, down0_ref, down1_ref, out_ref, radiated_ref,
+    incoming_ref, list_ref, sem,
 ):
+    staged = pltpu.make_async_copy(lists_ref, list_ref, sem)
+    staged.start()
     boxes, sub, width = mid_ref.shape
     half = width // 2
     radiated_ref[:boxes] = radiate(block_ref, (up0_ref[...], up1_ref[...])).reshape(boxes, sub, width)
     radiated_ref[boxes] = jnp.zeros((sub, width), F32)
-
-    def one_box(g, carry):
-        def group(n, total):
-            for i in range(GROUP):
-                e = n * GROUP + i
-                total = add_entry(total, radiated_ref, source_ref[e, g], table_ref, shift_ref[e, g])
-            return total
-
-        total = lax.fori_loop(0, count_ref[0, g], group, (mid_ref[g, :, :half], mid_ref[g, :, half:]))
-        incoming_ref[g, :, :half], incoming_ref[g, :, half:] = total
-        return carry
-
-    lax.fori_loop(0, boxes, one_box, 0)
+    staged.wait()
+    add_all(
+        list_ref, LATE, lambda g: (mid_ref[g, :, :half], mid_ref[g, :, half:]), incoming_ref, radiated_ref, table_ref
+    )
     far = dot3(split(incoming_ref[...].reshape(boxes * sub, width)), (down0_ref[...], down1_ref[...]), NT_FORM)
     devices, rows, lanes = out_ref.shape
     out_ref[:, : rows // 2, :] = far[:, :lanes].reshape(devices, rows // 2, lanes)
@@ -219,13 +239,9 @@
         currents, jnp.transpose(translations, (0, 2, 1))
     )
     mine = lax.all_to_all(packed, "dir", 0, 0, tiled=True)
-    index = shape(entries, boxes, kind=jnp.int32)
-    first, source2, shift2, count = call(
-        plan_kernel, (index, index, index, shape(8, boxes, kind=jnp.int32)), (VMEM, VMEM), name="plan"
-    )(inter_source.T, inter_shift.T)
-    mine, beside, first, source2, shift2, count = lax.optimization_barrier(
-        (mine, currents, first, source2, shift2, count)
-    )
+    lists = shape(2 * entries + LIST_ROWS, 128, kind=jnp.int32)
+    early, late = call(plan_kernel, (lists, lists), (VMEM, VMEM), name="plan")(inter_source.T, inter_shift.T)
+    mine, beside, early, late = lax.optimization_barrier((mine, currents, early, late))
     sent = mine[:, :rows]
     from_cross = lax.ppermute(sent, "slab", cross)
     from_same = lax.ppermute(sent, "slab", same)
@@ -236,22 +252,23 @@
     radiated, table, up0, up1, down0, down1 = call(
         own_kernel, (field, shape(ops, own, width), up, up, down, down), (VMEM,) * 3, name="own"
     )(mine, aggregate, disaggregate)
+    staging = (pltpu.SMEM(lists.shape, jnp.int32), pltpu.SemaphoreType.DMA)
     partial = call(
         mid_kernel,
         field,
-        (SMEM, SMEM) + (VMEM,) * 5,
-        scratch=(pltpu.VMEM((2 * boxes + 1, own, width), F32),),
+        (VMEM,) * 6,
+        scratch=(pltpu.VMEM((2 * boxes + 1, own, width), F32), *staging),
         micros=6,
         name="mid",
-    )(first, inter_shift.T, radiated, table, from_same, up0, up1)
+    )(early, radiated, table, from_same, up0, up1)
     far = call(
         far_kernel,
         shape(devices, rows, unknowns),
-        (SMEM,) * 3 + (VMEM,) * 7,
-        scratch=(pltpu.VMEM((boxes + 1, own, width), F32), pltpu.VMEM((boxes, own, width), F32)),
+        (VMEM,) * 8,
+        scratch=(pltpu.VMEM((boxes + 1, own, width), F32), pltpu.VMEM((boxes, own, width), F32), *staging),
         micros=5,
         name="far",
-    )(source2, shift2, count, partial, table, from_cross, up0, up1, down0, down1)
+    )(late, partial, table, from_cross, up0, up1, down0, down1)
     back = lax.all_to_all(far, "dir", 0, 0, tiled=True)
 
     stack = pltpu.VMEM((3 * box_dev, 2 * unknowns, 2 * illum), BF16)

time: 83.5 us -> 80.6 us (0.965)
  Pallas kernels: 25 us -> 22.3 us
    pallas_call x7, Pallas kernels: 25 us -> 22.3 us  [run(): pl.pallas_call(kernel, out_shape=outs, in_specs=specs, out_specs=jax.tree...]
  transfers between devices with their start and end apart: 6 -> 6, of which waited for: 2 -> 2; matrix products, arithmetic and copies ran while one was open for 0% -> 0% of each run, Pallas kernels for 28% -> 25%
where the time goes in v3:
time: 80.6 us; the launch traced here: 80 us
  waiting for transfers between devices  30.4 us (38%)
  starting transfers between devices  23.4 us (29%)
  Pallas kernels  22.3 us (28%)
  local copies, waits for them, and re-layouts  3.65 us (5%)
    pallas_call x7, Pallas kernels, run(): pl.pallas_call(kernel, out_shape=outs, in_specs=specs, out_specs=jax.tree...  22.3 us
    all_to_all x1, waiting for transfers between devices, body(): mine = lax.all_to_all(packed, 'dir', 0, 0, tiled=True)  19.8 us
    all_to_all x1, starting transfers between devices, body(): mine = lax.all_to_all(packed, 'dir', 0, 0, tiled=True)  11.5 us
    all_to_all x1, waiting for transfers between devices, body(): back = lax.all_to_all(far, 'dir', 0, 0, tiled=True)  10.6 us
    ppermute x1, starting transfers between devices, body(): right = lax.ppermute(beside, 'dir', [(j, i) for i, j in ring])  4.12 us
    all_to_all x1, starting transfers between devices, body(): back = lax.all_to_all(far, 'dir', 0, 0, tiled=True)  3.91 us
    unnamed x22, local copies, waits for them, and re-layouts  3.6 us
    ppermute x1, starting transfers between devices, body(): from_cross = lax.ppermute(sent, 'slab', cross)  2.53 us
  transfers between devices with their start and end apart: 6, of which 2 were waited for; matrix products, arithmetic and copies ran while one was open for 0% of the time, Pallas kernels for 25%

profile of v3, /device:TPU:2, one launch (start us, length us, event | category | flops | bytes accessed | tf_op | source)
XLA Modules:
  0.0 80.0 jit_solution(11332021360524912963)
XLA Ops:
  0.0 1.0 %copy-done.1 = f32[2,2,128,256]{3,2,1,0:T(8,128)S(1)} copy-done((f32[2,2,128,256]{3,2,1,0:T(8,128)S(1)}, f32[2,2,128,256]{3,2,1,0:T(8,128)}, u32[]{:S(2)}) %copy-start.1) | copy-done | bytes 524312
  1.0 0.7 copy-done.7
  1.7 1.1 %pack.1 = f32[32,40,128]{2,1,0:T(8,128)} custom-call(f32[2,2,128,256]{3,2,1,0:T(8,128)S(1)} %copy-done.1, f32[2,8,64]{2,1,0:T(8,128)S(1)} %bitcast.5), custom_call_target="tpu_custom_call" | custom-call | flops 1000000000 | tf_op jit(solution)/shard_map/pack/pallas_call | solution.py:207
  2.8 11.5 %all-to-all-start = ((f32[32,40,128]{2,1,0:T(8,128)}), f32[32,40,128]{2,1,0:T(8,128)S(1)}, u32[]{:S(2)}, u32[]{:S(2)}) async-start(f32[32,40,128]{2,1,0:T(8,128)} %pack.1), calls=%async_computation | async-start | bytes 1310720 | tf_op jit(solution)/shard_map/all_to_all | solution.py:241
  14.3 0.0 copy-start.2
  14.3 0.0 copy-start.3
  14.3 0.0 copy-start.4
  14.4 0.3 plan.1
  14.7 19.8 %all-to-all-done.own_ref = f32[32,40,128]{2,1,0:T(8,128)S(1)} async-done(((f32[32,40,128]{2,1,0:T(8,128)}), f32[32,40,128]{2,1,0:T(8,128)S(1)}, u32[]{:S(2)}, u32[]{:S(2)}) %all-to-all-start) | async-done | bytes 655392 | tf_op jit(solution)/shard_map/all_to_all | solution.py:241
  34.5 0.1 slice.3
  34.6 0.1 collective-permute-start
  34.7 2.5 %collective-permute-start.1 = (f32[32,32,128]{2,1,0:T(8,128)S(1)}, f32[32,32,128]{2,1,0:T(8,128)S(1)}, u32[]{:S(2)}, u32[]{:S(2)}) collective-permute-start(f32[32,32,128]{2,1,0:T(8,128)S(1)} %slice.3), channel_id=1, source_target_pairs={{32,64},{96,128},{160,192},{64,32},{128,96},{192,160},{33,65},{97,... | collective-permute-start | bytes 1572872 | tf_op jit(solution)/shard_map/ppermute | solution.py:246
  37.2 1.3 %collective-permute-start.2 = (f32[2,2,128,256]{3,2,1,0:T(8,128)S(1)}, f32[2,2,128,256]{3,2,1,0:T(8,128)}, u32[]{:S(2)}, u32[]{:S(2)}) collective-permute-start(f32[2,2,128,256]{3,2,1,0:T(8,128)S(1)} %copy-done.2), channel_id=1, source_target_pairs={{0,1},{1,2},{2,3},{3,4},{4,5},{5,6},{6,7},{7,8},{8,9},{9,10},{10,1... | collective-permute-start | bytes 1572872 | tf_op jit(solution)/shard_map/ppermute | solution.py:248
  38.5 4.1 %collective-permute-start.3 = (f32[2,2,128,256]{3,2,1,0:T(8,128)S(1)}, f32[2,2,128,256]{3,2,1,0:T(8,128)}, u32[]{:S(2)}, u32[]{:S(2)}) collective-permute-start(f32[2,2,128,256]{3,2,1,0:T(8,128)S(1)} %copy-done.2), channel_id=1, source_target_pairs={{1,0},{2,1},{3,2},{4,3},{5,4},{6,5},{7,6},{8,7},{9,8},{10,9},{11,1... | collective-permute-start | bytes 1572872 | tf_op jit(solution)/shard_map/ppermute | solution.py:249
  42.6 0.7 own.1
  43.4 6.2 %mid.1.mid_ref = f32[64,8,512]{2,1,0:T(8,128)S(1)} custom-call(s32[72,128]{1,0:T(8,128)S(1)} %get-tuple-element.20.lists_ref, f32[64,8,512]{2,1,0:T(8,128)S(1)} %get-tuple-element.22.own_ref, f32[64,8,512]{2,1,0:T(8,128)S(1)} %get-tuple-element.23.table_ref, f32[32,32,128]{2,1,0:T(8,128)S(1)} %collective-permute-done.block_ref, ...), custom_call_target="tpu_custom_call" | custom-call | flops 6000000000 | tf_op jit(solution)/shard_map/mid/pallas_call | solution.py:207
  49.7 0.0 copy-start.8
  49.7 6.2 %far.1 = f32[32,32,128]{2,1,0:T(8,128)} custom-call(s32[72,128]{1,0:T(8,128)S(1)} %get-tuple-element.19.lists_ref, f32[64,8,512]{2,1,0:T(8,128)S(1)} %mid.1.mid_ref, f32[64,8,512]{2,1,0:T(8,128)S(1)} %get-tuple-element.23.table_ref, f32[32,32,128]{2,1,0:T(8,128)S(1)} %collective-permute-done.1.block_ref, bf16[512,256]{1,0:T(8,128)(2,1)S(1)} %get-tuple-element.24.up0_ref, ...), custom_call_target="tpu_custom_call" | custom-call | flops 5000000000 | tf_op jit(solution)/shard_map/far/pallas_call | solution.py:207
  55.9 3.9 %all-to-all-start.1 = ((f32[32,32,128]{2,1,0:T(8,128)}), f32[32,32,128]{2,1,0:T(8,128)S(1)}, u32[]{:S(2)}, u32[]{:S(2)}) async-start(f32[32,32,128]{2,1,0:T(8,128)} %far.1), calls=%async_computation.1 | async-start | bytes 1048576 | tf_op jit(solution)/shard_map/all_to_all | solution.py:272
  59.9 6.8 %near.1.near_ref = f32[2,2,128,256]{3,2,1,0:T(8,128)S(1)} custom-call(s32[2,9]{1,0:T(2,128)S(1)} %copy-done.8, f32[2,2,9,128,128]{4,3,2,1,0:T(8,128)S(1)} %copy-done, f32[2,2,128,256]{3,2,1,0:T(8,128)S(1)} %copy-done.2, f32[2,2,128,256]{3,2,1,0:T(8,128)} %collective-permute-done.2.left_ref, f32[2,2,128,256]{3,2,1,0:T(8,128)} %collective-permute-done.3.right_ref), custom_call_target="tpu_custom_call" | custom-call | flops 20000000000 | tf_op jit(solution)/shard_map/near/pallas_call | solution.py:207
  66.7 0.8 copy-done.9
  67.4 10.6 %all-to-all-done.1.far_ref = f32[32,32,128]{2,1,0:T(8,128)S(1)} async-done(((f32[32,32,128]{2,1,0:T(8,128)}), f32[32,32,128]{2,1,0:T(8,128)S(1)}, u32[]{:S(2)}, u32[]{:S(2)}) %all-to-all-start.1) | async-done | bytes 524320 | tf_op jit(solution)/shard_map/all_to_all | solution.py:272
  78.0 1.0 %copy-done.10 = f32[2,2,128,256]{3,2,1,0:T(8,128)S(1)} copy-done((f32[2,2,128,256]{3,2,1,0:T(8,128)S(1)}, f32[2,2,128,256]{3,2,1,0:T(8,128)}, u32[]{:S(2)}) %copy-start.10) | copy-done | bytes 524312
  79.0 1.0 %join.1 = f32[2,2,128,256]{3,2,1,0:T(8,128)} custom-call(f32[32,32,128]{2,1,0:T(8,128)S(1)} %all-to-all-done.1.far_ref, f32[2,2,128,256]{3,2,1,0:T(8,128)S(1)} %copy-done.10), custom_call_target="tpu_custom_call" | custom-call | flops 1000000000 | tf_op jit(solution)/shard_map/join/pallas_call | solution.py:207
  (18 shorter events, 0.0 us)
Async XLA Ops:
  0.0 1.0 %copy-start.1 = (f32[2,2,128,256]{3,2,1,0:T(8,128)S(1)}, f32[2,2,128,256]{3,2,1,0:T(8,128)}, u32[]{:S(2)}) copy-start(f32[2,2,128,256]{3,2,1,0:T(8,128)} %own_ref.1) | copy-start | bytes 1572868
  1.0 0.7 copy-start.7
  1.7 12.6 %copy-start.5 = (s32[64,32]{0,1:T(8,128)S(1)}, s32[64,32]{0,1:T(8,128)}, u32[]{:S(2)}) copy-start(s32[64,32]{0,1:T(8,128)} %param.13) | copy-start | bytes 24580
  1.7 12.6 %copy-start.6 = (s32[64,32]{0,1:T(8,128)S(1)}, s32[64,32]{0,1:T(8,128)}, u32[]{:S(2)}) copy-start(s32[64,32]{0,1:T(8,128)} %param.14) | copy-start | bytes 24580
  2.8 31.7 %all-to-all-start = ((f32[32,40,128]{2,1,0:T(8,128)}), f32[32,40,128]{2,1,0:T(8,128)S(1)}, u32[]{:S(2)}, u32[]{:S(2)}) async-start(f32[32,40,128]{2,1,0:T(8,128)} %pack.1), calls=%async_computation | async-start | bytes 1310720 | tf_op jit(solution)/shard_map/all_to_all | solution.py:241
  14.3 22.9 %copy-start.2 = (f32[2,2,128,256]{3,2,1,0:T(8,128)S(1)}, f32[2,2,128,256]{3,2,1,0:T(8,128)}, u32[]{:S(2)}) copy-start(f32[2,2,128,256]{3,2,1,0:T(8,128)} %own_ref.1) | copy-start | bytes 1572868
  14.3 28.3 %copy-start.3 = (f32[2,256,128]{2,1,0:T(8,128)S(1)}, f32[2,256,128]{2,1,0:T(8,128)}, u32[]{:S(2)}) copy-start(f32[2,256,128]{2,1,0:T(8,128)} %aggregate_ref.1) | copy-start | bytes 786436
  14.3 28.3 %copy-start.4 = (f32[2,128,256]{2,1,0:T(8,128)S(1)}, f32[2,128,256]{2,1,0:T(8,128)}, u32[]{:S(2)}) copy-start(f32[2,128,256]{2,1,0:T(8,128)} %disaggregate_ref.1) | copy-start | bytes 786436
  34.6 8.8 %collective-permute-start = (f32[32,32,128]{2,1,0:T(8,128)S(1)}, f32[32,32,128]{2,1,0:T(8,128)S(1)}, u32[]{:S(2)}, u32[]{:S(2)}) collective-permute-start(f32[32,32,128]{2,1,0:T(8,128)S(1)} %slice.3), channel_id=1, source_target_pairs={{0,32},{64,96},{128,160},{192,224},{32,0},{96,64},{160,128},{224,1... | collective-permute-start | bytes 1572872 | tf_op jit(solution)/shard_map/ppermute | solution.py:247
  34.7 15.0 %collective-permute-start.1 = (f32[32,32,128]{2,1,0:T(8,128)S(1)}, f32[32,32,128]{2,1,0:T(8,128)S(1)}, u32[]{:S(2)}, u32[]{:S(2)}) collective-permute-start(f32[32,32,128]{2,1,0:T(8,128)S(1)} %slice.3), channel_id=1, source_target_pairs={{32,64},{96,128},{160,192},{64,32},{128,96},{192,160},{33,65},{97,... | collective-permute-start | bytes 1572872 | tf_op jit(solution)/shard_map/ppermute | solution.py:246
  37.2 22.6 %collective-permute-start.2 = (f32[2,2,128,256]{3,2,1,0:T(8,128)S(1)}, f32[2,2,128,256]{3,2,1,0:T(8,128)}, u32[]{:S(2)}, u32[]{:S(2)}) collective-permute-start(f32[2,2,128,256]{3,2,1,0:T(8,128)S(1)} %copy-done.2), channel_id=1, source_target_pairs={{0,1},{1,2},{2,3},{3,4},{4,5},{5,6},{6,7},{7,8},{8,9},{9,10},{10,1... | collective-permute-start | bytes 1572872 | tf_op jit(solution)/shard_map/ppermute | solution.py:248
  38.5 21.3 %collective-permute-start.3 = (f32[2,2,128,256]{3,2,1,0:T(8,128)S(1)}, f32[2,2,128,256]{3,2,1,0:T(8,128)}, u32[]{:S(2)}, u32[]{:S(2)}) collective-permute-start(f32[2,2,128,256]{3,2,1,0:T(8,128)S(1)} %copy-done.2), channel_id=1, source_target_pairs={{1,0},{2,1},{3,2},{4,3},{5,4},{6,5},{7,6},{8,7},{9,8},{10,9},{11,1... | collective-permute-start | bytes 1572872 | tf_op jit(solution)/shard_map/ppermute | solution.py:249
  49.6 10.2 %copy-start = (f32[2,2,9,128,128]{4,3,2,1,0:T(8,128)S(1)}, f32[2,2,9,128,128]{4,3,2,1,0:T(8,128)}, u32[]{:S(2)}) copy-start(f32[2,2,9,128,128]{4,3,2,1,0:T(8,128)} %blocks_ref.1) | copy-start | bytes 7077892
  49.7 10.2 %copy-start.8 = (s32[2,9]{1,0:T(2,128)S(1)}, s32[2,9]{1,0:T(2,128)}, u32[]{:S(2)}) copy-start(s32[2,9]{1,0:T(2,128)} %index_ref.1) | copy-start | bytes 220
  55.9 22.1 %all-to-all-start.1 = ((f32[32,32,128]{2,1,0:T(8,128)}), f32[32,32,128]{2,1,0:T(8,128)S(1)}, u32[]{:S(2)}, u32[]{:S(2)}) async-start(f32[32,32,128]{2,1,0:T(8,128)} %far.1), calls=%async_computation.1 | async-start | bytes 1048576 | tf_op jit(solution)/shard_map/all_to_all | solution.py:272
  66.7 0.8 copy-start.9
  78.0 1.0 %copy-start.10 = (f32[2,2,128,256]{3,2,1,0:T(8,128)S(1)}, f32[2,2,128,256]{3,2,1,0:T(8,128)}, u32[]{:S(2)}) copy-start(f32[2,2,128,256]{3,2,1,0:T(8,128)} %copy-done.9) | copy-start | bytes 1572868

commit v4 on v3

--- a/solution.py
+++ b/solution.py
@@ -10,10 +10,12 @@
 F32, BF16 = jnp.float32, jnp.bfloat16
 VMEM = pltpu.MemorySpace.VMEM
 SMEM = pltpu.MemorySpace.SMEM
+ANY = pl.ANY
 MIB = 1 << 20
 RE_IM_ROWS = 32
-EARLY, LATE = 24, 14
+EARLY, LATE = 26, 14
 LIST_ROWS = 8
+FULL = 63
 
 
 def split(x):
@@ -32,17 +34,30 @@
 NT_FORM = ((1,), (1,))
 
 
-def pack_kernel(currents_ref, translations_ref, out_ref):
+def pack_kernel(currents_ref, translations_ref, out_ref, block_ref, table_ref, packed_ref, in_sem, out_sem):
     devices, rows, lanes = out_ref.shape
     parts, boxes, _, illum = currents_ref.shape
     own = illum // devices
-    for c in range(parts):
-        for b in range(boxes):
-            turned = currents_ref[c, b].T.reshape(devices, own, lanes)
-            out_ref[:, pl.ds((c * boxes + b) * own, own), :] = turned
-    table = jnp.concatenate([translations_ref[0], translations_ref[1]], axis=1)
-    first = parts * boxes * own
-    out_ref[:, first:, :] = jnp.broadcast_to(table[None], (devices, rows - first, lanes))
+    pieces = [(c, b) for c in range(parts) for b in range(boxes)]
+    last = len(pieces)
+    loads = [pltpu.make_async_copy(currents_ref.at[c, b], block_ref.at[n], in_sem.at[n]) for n, (c, b) in enumerate(pieces)]
+    loads.append(pltpu.make_async_copy(translations_ref, table_ref, in_sem.at[last]))
+    stores = [
+        pltpu.make_async_copy(packed_ref.at[:, pl.ds(n * own, own), :], out_ref.at[:, pl.ds(n * own, own), :], out_sem.at[n])
+        for n in range(last + 1)
+    ]
+    for load in loads:
+        load.start()
+    for n in range(last):
+        loads[n].wait()
+        packed_ref[:, n * own : (n + 1) * own, :] = block_ref[n].T.reshape(devices, own, lanes)
+        stores[n].start()
+    loads[last].wait()
+    table = jnp.concatenate([table_ref[0], table_ref[1]], axis=1)
+    packed_ref[:, last * own :, :] = jnp.broadcast_to(table[None], (devices, own, lanes))
+    stores[last].start()
+    for store in stores:
+        store.wait()
 
 
 def near_kernel(index_ref, blocks_ref, own_ref, left_ref, right_ref, out_ref, high_ref, low_ref):
@@ -141,6 +156,9 @@
     def one_box(g, carry):
         total = add_entries(list_ref, g, range(fixed), start(g), radiated_ref, table_ref)
         out_ref[g, :, :half], out_ref[g, :, half:] = total
+        return carry
+
+    def beyond(g, carry):
         count = list_ref[2 * entries, g]
 
         @pl.when(count > fixed)
@@ -153,7 +171,8 @@
 
         return carry
 
-    lax.fori_loop(0, out_ref.shape[0], one_box, 0)
+    lax.fori_loop(0, out_ref.shape[0], one_box, 0, unroll=2)
+    lax.fori_loop(0, out_ref.shape[0], beyond, 0)
 
 
 def mid_kernel(
@@ -190,17 +209,29 @@
     out_ref[:, rows // 2 :, :] = far[:, lanes:].reshape(devices, rows // 2, lanes)
 
 
-def join_kernel(far_ref, near_ref, out_ref):
+def join_kernel(far_ref, near_ref, out_ref, rows_ref, block_ref, sum_ref, far_sem, near_sem, out_sem):
     parts, boxes, lanes, illum = out_ref.shape
     devices = far_ref.shape[0]
     own = illum // devices
-    for c in range(parts):
-        for b in range(boxes):
-            turned = far_ref[:, pl.ds((c * boxes + b) * own, own), :].reshape(illum, lanes)
-            out_ref[c, b] = near_ref[c, b] + turned.T
-
-
-def call(kernel, outs, kinds, scratch=(), limit=16, micros=1, name=None):
+    pieces = [(c, b) for c in range(parts) for b in range(boxes)]
+    loads = []
+    for n, (c, b) in enumerate(pieces):
+        loads.append(pltpu.make_async_copy(far_ref.at[:, pl.ds(n * own, own), :], rows_ref.at[n], far_sem.at[n]))
+        loads.append(pltpu.make_async_copy(near_ref.at[c, b], block_ref.at[n], near_sem.at[n]))
+    stores = [pltpu.make_async_copy(sum_ref.at[n], out_ref.at[c, b], out_sem.at[n]) for n, (c, b) in enumerate(pieces)]
+    for load in loads:
+        load.start()
+    for n in range(len(pieces)):
+        loads[2 * n].wait()
+        turned = rows_ref[n].reshape(illum, lanes).T
+        loads[2 * n + 1].wait()
+        sum_ref[n] = block_ref[n] + turned
+        stores[n].start()
+    for store in stores:
+        store.wait()
+
+
+def call(kernel, outs, kinds, scratch=(), limit=16, micros=1, name=None, out_kind=VMEM):
     specs = [pl.BlockSpec(memory_space=kind) for kind in kinds]
 
     def run(*args):
@@ -208,7 +239,7 @@
             kernel,
             out_shape=outs,
             in_specs=specs,
-            out_specs=jax.tree.map(lambda _: pl.BlockSpec(memory_space=VMEM), outs),
+            out_specs=jax.tree.map(lambda _: pl.BlockSpec(memory_space=out_kind), outs),
             scratch_shapes=list(scratch),
             compiler_params=pltpu.CompilerParams(vmem_limit_bytes=limit * MIB),
             cost_estimate=pl.CostEstimate(flops=micros * 1_000_000_000, bytes_accessed=0, transcendentals=0),
@@ -235,9 +266,25 @@
     pairs_of = [[(i, i + 1) for i in range(start, slabs - 1, 2)] for start in (0, 1)]
     same, cross = [p + [(j, i) for i, j in p] for p in pairs_of]
 
-    packed = call(pack_kernel, shape(devices, rows + translations.shape[2], unknowns), (VMEM, VMEM), name="pack")(
-        currents, jnp.transpose(translations, (0, 2, 1))
-    )
+    turned = jnp.transpose(translations, (0, 2, 1))
+    pieces = parts * box_dev
+    blocks = pltpu.VMEM((pieces, unknowns, illum), F32)
+    whole = shape(devices, rows + turned.shape[1], unknowns)
+    packed = call(
+        pack_kernel,
+        whole,
+        (ANY, ANY),
+        scratch=(
+            blocks,
+            pltpu.VMEM(turned.shape, F32),
+            pltpu.VMEM(whole.shape, F32),
+            pltpu.SemaphoreType.DMA((pieces + 1,)),
+            pltpu.SemaphoreType.DMA((pieces + 1,)),
+        ),
+        limit=FULL,
+        name="pack",
+        out_kind=ANY,
+    )(currents, turned)
     mine = lax.all_to_all(packed, "dir", 0, 0, tiled=True)
     lists = shape(2 * entries + LIST_ROWS, 128, kind=jnp.int32)
     early, late = call(plan_kernel, (lists, lists), (VMEM, VMEM), name="plan")(inter_source.T, inter_shift.T)
@@ -275,7 +322,15 @@
     near = call(
         near_kernel, shape(*currents.shape), (SMEM,) + (VMEM,) * 4, scratch=(stack, stack), micros=20, name="near"
     )(near_index, near_blocks, currents, left, right)
-    return call(join_kernel, shape(*currents.shape), (VMEM, VMEM), name="join")(back, near)
+    return call(
+        join_kernel,
+        shape(*currents.shape),
+        (ANY, ANY),
+        scratch=(pltpu.VMEM((pieces, devices, own, unknowns), F32), blocks, blocks, *(pltpu.SemaphoreType.DMA((pieces,)),) * 3),
+        limit=FULL,
+        name="join",
+        out_kind=ANY,
+    )(back, near)
 
 
 def solution(mesh):

time: 80.6 us -> 81.9 us (1.016)
  Pallas kernels: 22.3 us -> 25.7 us
  local copies, waits for them, and re-layouts: 3.65 us -> 0.89 us
    pallas_call x7, Pallas kernels: 22.3 us -> 25.7 us  [run(): pl.pallas_call(kernel, out_shape=outs, in_specs=specs, out_specs=jax.tree...]
    unnamed x22 -> x16, local copies, waits for them, and re-layouts: 3.6 us -> 0.84 us
  transfers between devices with their start and end apart: 6 -> 6, of which waited for: 2 -> 2; matrix products, arithmetic and copies ran while one was open for 0% -> 0% of each run, Pallas kernels for 25% -> 26%
where the time goes in v4:
time: 81.9 us; the launch traced here: 81.6 us
  waiting for transfers between devices  30.6 us (37%)
  Pallas kernels  25.7 us (31%)
  starting transfers between devices  24.2 us (30%)
  local copies, waits for them, and re-layouts  0.89 us (1%)
    pallas_call x7, Pallas kernels, run(): pl.pallas_call(kernel, out_shape=outs, in_specs=specs, out_specs=jax.tree...  25.7 us
    all_to_all x1, waiting for transfers between devices, body(): mine = lax.all_to_all(packed, 'dir', 0, 0, tiled=True)  19.8 us
    all_to_all x1, starting transfers between devices, body(): mine = lax.all_to_all(packed, 'dir', 0, 0, tiled=True)  11.5 us
    all_to_all x1, waiting for transfers between devices, body(): back = lax.all_to_all(far, 'dir', 0, 0, tiled=True)  10.8 us
    all_to_all x1, starting transfers between devices, body(): back = lax.all_to_all(far, 'dir', 0, 0, tiled=True)  4.64 us
    ppermute x1, starting transfers between devices, body(): right = lax.ppermute(beside, 'dir', [(j, i) for i, j in ring])  4.12 us
    ppermute x1, starting transfers between devices, body(): from_cross = lax.ppermute(sent, 'slab', cross)  2.53 us
  transfers between devices with their start and end apart: 6, of which 2 were waited for; matrix products, arithmetic and copies ran while one was open for 0% of the time, Pallas kernels for 26%

profile of v4, /device:TPU:2, one launch (start us, length us, event | category | flops | bytes accessed | tf_op | source)
XLA Modules:
  0.0 81.6 jit_solution(4562335284468463224)
XLA Ops:
  0.0 2.2 %pack.1 = f32[32,40,128]{2,1,0:T(8,128)} custom-call(f32[2,2,128,256]{3,2,1,0:T(8,128)} %own_ref.1, f32[2,8,64]{2,1,0:T(8,128)} %bitcast.5), custom_call_target="tpu_custom_call" | custom-call | flops 1000000000 | tf_op jit(solution)/shard_map/pack/pallas_call | solution.py:238
  2.2 11.5 %all-to-all-start = ((f32[32,40,128]{2,1,0:T(8,128)}), f32[32,40,128]{2,1,0:T(8,128)S(1)}, u32[]{:S(2)}, u32[]{:S(2)}) async-start(f32[32,40,128]{2,1,0:T(8,128)} %pack.1), calls=%async_computation | async-start | bytes 1310720 | tf_op jit(solution)/shard_map/all_to_all | solution.py:288
  13.7 0.0 copy-start.1
  13.7 0.0 copy-start.2
  13.7 0.0 copy-start.3
  13.8 0.3 plan.1
  14.1 19.8 %all-to-all-done.own_ref = f32[32,40,128]{2,1,0:T(8,128)S(1)} async-done(((f32[32,40,128]{2,1,0:T(8,128)}), f32[32,40,128]{2,1,0:T(8,128)S(1)}, u32[]{:S(2)}, u32[]{:S(2)}) %all-to-all-start) | async-done | bytes 655392 | tf_op jit(solution)/shard_map/all_to_all | solution.py:288
  33.9 0.1 slice.3
  34.0 0.1 collective-permute-start
  34.1 2.5 %collective-permute-start.1 = (f32[32,32,128]{2,1,0:T(8,128)S(1)}, f32[32,32,128]{2,1,0:T(8,128)S(1)}, u32[]{:S(2)}, u32[]{:S(2)}) collective-permute-start(f32[32,32,128]{2,1,0:T(8,128)S(1)} %slice.3), channel_id=1, source_target_pairs={{32,64},{96,128},{160,192},{64,32},{128,96},{192,160},{33,65},{97,... | collective-permute-start | bytes 1572872 | tf_op jit(solution)/shard_map/ppermute | solution.py:293
  36.6 1.3 %collective-permute-start.2 = (f32[2,2,128,256]{3,2,1,0:T(8,128)S(1)}, f32[2,2,128,256]{3,2,1,0:T(8,128)S(1)}, u32[]{:S(2)}, u32[]{:S(2)}) collective-permute-start(f32[2,2,128,256]{3,2,1,0:T(8,128)S(1)} %copy-done.1), channel_id=1, source_target_pairs={{0,1},{1,2},{2,3},{3,4},{4,5},{5,6},{6,7},{7,8},{8,9},{9,10},{10,1... | collective-permute-start | bytes 1572872 | tf_op jit(solution)/shard_map/ppermute | solution.py:295
  37.9 4.1 %collective-permute-start.3 = (f32[2,2,128,256]{3,2,1,0:T(8,128)S(1)}, f32[2,2,128,256]{3,2,1,0:T(8,128)}, u32[]{:S(2)}, u32[]{:S(2)}) collective-permute-start(f32[2,2,128,256]{3,2,1,0:T(8,128)S(1)} %copy-done.1), channel_id=1, source_target_pairs={{1,0},{2,1},{3,2},{4,3},{5,4},{6,5},{7,6},{8,7},{9,8},{10,9},{11,1... | collective-permute-start | bytes 1572872 | tf_op jit(solution)/shard_map/ppermute | solution.py:296
  42.0 0.8 own.1
  42.8 0.0 collective-permute-done.block_ref
  42.8 6.9 %mid.1.mid_ref = f32[64,8,512]{2,1,0:T(8,128)S(1)} custom-call(s32[72,128]{1,0:T(8,128)S(1)} %get-tuple-element.20.lists_ref, f32[64,8,512]{2,1,0:T(8,128)S(1)} %get-tuple-element.22.own_ref, f32[64,8,512]{2,1,0:T(8,128)S(1)} %get-tuple-element.23.table_ref, f32[32,32,128]{2,1,0:T(8,128)S(1)} %collective-permute-done.block_ref, ...), custom_call_target="tpu_custom_call" | custom-call | flops 6000000000 | tf_op jit(solution)/shard_map/mid/pallas_call | solution.py:238
  49.7 0.0 collective-permute-done.1.block_ref
  49.7 0.0 copy-start
  49.7 0.0 copy-start.6
  49.7 6.7 %far.1 = f32[32,32,128]{2,1,0:T(8,128)} custom-call(s32[72,128]{1,0:T(8,128)S(1)} %get-tuple-element.19.lists_ref, f32[64,8,512]{2,1,0:T(8,128)S(1)} %mid.1.mid_ref, f32[64,8,512]{2,1,0:T(8,128)S(1)} %get-tuple-element.23.table_ref, f32[32,32,128]{2,1,0:T(8,128)S(1)} %collective-permute-done.1.block_ref, bf16[512,256]{1,0:T(8,128)(2,1)S(1)} %get-tuple-element.24.up0_ref, ...), custom_call_target="tpu_custom_call" | custom-call | flops 5000000000 | tf_op jit(solution)/shard_map/far/pallas_call | solution.py:238
  56.4 4.6 %all-to-all-start.1 = ((f32[32,32,128]{2,1,0:T(8,128)}), f32[32,32,128]{2,1,0:T(8,128)}, u32[]{:S(2)}, u32[]{:S(2)}) async-start(f32[32,32,128]{2,1,0:T(8,128)} %far.1), calls=%async_computation.1 | async-start | bytes 1048576 | tf_op jit(solution)/shard_map/all_to_all | solution.py:319
  61.1 6.7 %near.1.near_ref = f32[2,2,128,256]{3,2,1,0:T(8,128)S(1)} custom-call(s32[2,9]{1,0:T(2,128)S(1)} %copy-done.6, f32[2,2,9,128,128]{4,3,2,1,0:T(8,128)S(1)} %copy-done, f32[2,2,128,256]{3,2,1,0:T(8,128)S(1)} %copy-done.1, f32[2,2,128,256]{3,2,1,0:T(8,128)S(1)} %collective-permute-done.2.left_ref, f32[2,2,128,256]{3,2,1,0:T(8,128)} %collective-permute-done.3.right_ref), custom_call_target="tpu_custom_call" | custom-call | flops 20000000000 | tf_op jit(solution)/shard_map/near/pallas_call | solution.py:238
  67.8 0.8 copy-done.7
  68.6 10.8 %all-to-all-done.1.far_ref = f32[32,32,128]{2,1,0:T(8,128)} async-done(((f32[32,32,128]{2,1,0:T(8,128)}), f32[32,32,128]{2,1,0:T(8,128)}, u32[]{:S(2)}, u32[]{:S(2)}) %all-to-all-start.1) | async-done | bytes 524320 | tf_op jit(solution)/shard_map/all_to_all | solution.py:319
  79.4 2.1 %join.1 = f32[2,2,128,256]{3,2,1,0:T(8,128)} custom-call(f32[32,32,128]{2,1,0:T(8,128)} %all-to-all-done.1.far_ref, f32[2,2,128,256]{3,2,1,0:T(8,128)} %copy-done.7), custom_call_target="tpu_custom_call" | custom-call | flops 1000000000 | tf_op jit(solution)/shard_map/join/pallas_call | solution.py:238
  (12 shorter events, 0.0 us)
Async XLA Ops:
  0.0 13.7 %copy-start.4 = (s32[64,32]{0,1:T(8,128)S(1)}, s32[64,32]{0,1:T(8,128)}, u32[]{:S(2)}) copy-start(s32[64,32]{0,1:T(8,128)} %param.13) | copy-start | bytes 24580
  0.0 13.7 %copy-start.5 = (s32[64,32]{0,1:T(8,128)S(1)}, s32[64,32]{0,1:T(8,128)}, u32[]{:S(2)}) copy-start(s32[64,32]{0,1:T(8,128)} %param.14) | copy-start | bytes 24580
  2.2 31.7 %all-to-all-start = ((f32[32,40,128]{2,1,0:T(8,128)}), f32[32,40,128]{2,1,0:T(8,128)S(1)}, u32[]{:S(2)}, u32[]{:S(2)}) async-start(f32[32,40,128]{2,1,0:T(8,128)} %pack.1), calls=%async_computation | async-start | bytes 1310720 | tf_op jit(solution)/shard_map/all_to_all | solution.py:288
  13.7 22.9 %copy-start.1 = (f32[2,2,128,256]{3,2,1,0:T(8,128)S(1)}, f32[2,2,128,256]{3,2,1,0:T(8,128)}, u32[]{:S(2)}) copy-start(f32[2,2,128,256]{3,2,1,0:T(8,128)} %own_ref.1) | copy-start | bytes 1572868
  13.7 28.3 %copy-start.2 = (f32[2,256,128]{2,1,0:T(8,128)S(1)}, f32[2,256,128]{2,1,0:T(8,128)}, u32[]{:S(2)}) copy-start(f32[2,256,128]{2,1,0:T(8,128)} %aggregate_ref.1) | copy-start | bytes 786436
  13.7 28.3 %copy-start.3 = (f32[2,128,256]{2,1,0:T(8,128)S(1)}, f32[2,128,256]{2,1,0:T(8,128)}, u32[]{:S(2)}) copy-start(f32[2,128,256]{2,1,0:T(8,128)} %disaggregate_ref.1) | copy-start | bytes 786436
  34.0 8.8 %collective-permute-start = (f32[32,32,128]{2,1,0:T(8,128)S(1)}, f32[32,32,128]{2,1,0:T(8,128)S(1)}, u32[]{:S(2)}, u32[]{:S(2)}) collective-permute-start(f32[32,32,128]{2,1,0:T(8,128)S(1)} %slice.3), channel_id=1, source_target_pairs={{0,32},{64,96},{128,160},{192,224},{32,0},{96,64},{160,128},{224,1... | collective-permute-start | bytes 1572872 | tf_op jit(solution)/shard_map/ppermute | solution.py:294
  34.1 15.6 %collective-permute-start.1 = (f32[32,32,128]{2,1,0:T(8,128)S(1)}, f32[32,32,128]{2,1,0:T(8,128)S(1)}, u32[]{:S(2)}, u32[]{:S(2)}) collective-permute-start(f32[32,32,128]{2,1,0:T(8,128)S(1)} %slice.3), channel_id=1, source_target_pairs={{32,64},{96,128},{160,192},{64,32},{128,96},{192,160},{33,65},{97,... | collective-permute-start | bytes 1572872 | tf_op jit(solution)/shard_map/ppermute | solution.py:293
  36.6 24.5 %collective-permute-start.2 = (f32[2,2,128,256]{3,2,1,0:T(8,128)S(1)}, f32[2,2,128,256]{3,2,1,0:T(8,128)S(1)}, u32[]{:S(2)}, u32[]{:S(2)}) collective-permute-start(f32[2,2,128,256]{3,2,1,0:T(8,128)S(1)} %copy-done.1), channel_id=1, source_target_pairs={{0,1},{1,2},{2,3},{3,4},{4,5},{5,6},{6,7},{7,8},{8,9},{9,10},{10,1... | collective-permute-start | bytes 1572872 | tf_op jit(solution)/shard_map/ppermute | solution.py:295
  37.9 23.2 %collective-permute-start.3 = (f32[2,2,128,256]{3,2,1,0:T(8,128)S(1)}, f32[2,2,128,256]{3,2,1,0:T(8,128)}, u32[]{:S(2)}, u32[]{:S(2)}) collective-permute-start(f32[2,2,128,256]{3,2,1,0:T(8,128)S(1)} %copy-done.1), channel_id=1, source_target_pairs={{1,0},{2,1},{3,2},{4,3},{5,4},{6,5},{7,6},{8,7},{9,8},{10,9},{11,1... | collective-permute-start | bytes 1572872 | tf_op jit(solution)/shard_map/ppermute | solution.py:296
  49.7 11.4 %copy-start = (f32[2,2,9,128,128]{4,3,2,1,0:T(8,128)S(1)}, f32[2,2,9,128,128]{4,3,2,1,0:T(8,128)}, u32[]{:S(2)}) copy-start(f32[2,2,9,128,128]{4,3,2,1,0:T(8,128)} %blocks_ref.1) | copy-start | bytes 7077892
  49.7 11.4 %copy-start.6 = (s32[2,9]{1,0:T(2,128)S(1)}, s32[2,9]{1,0:T(2,128)}, u32[]{:S(2)}) copy-start(s32[2,9]{1,0:T(2,128)} %index_ref.1) | copy-start | bytes 220
  56.4 23.0 %all-to-all-start.1 = ((f32[32,32,128]{2,1,0:T(8,128)}), f32[32,32,128]{2,1,0:T(8,128)}, u32[]{:S(2)}, u32[]{:S(2)}) async-start(f32[32,32,128]{2,1,0:T(8,128)} %far.1), calls=%async_computation.1 | async-start | bytes 1048576 | tf_op jit(solution)/shard_map/all_to_all | solution.py:319
  67.8 0.8 copy-start.7

commit v5 on v4

--- a/solution.py
+++ b/solution.py
@@ -13,7 +13,7 @@
 ANY = pl.ANY
 MIB = 1 << 20
 RE_IM_ROWS = 32
-EARLY, LATE = 26, 14
+EARLY, LATE = 25, 15
 LIST_ROWS = 8
 FULL = 63
 
@@ -105,9 +105,12 @@
     part, place = source // boxes, source % boxes
     away = part == 2 * odd
     row = lax.broadcasted_iota(jnp.int32, (entries, boxes), 0)
-    for ref, chosen, where, zeros in (
-        (early_ref, jnp.logical_not(away), jnp.where(part == 1, place, boxes + place), 2 * boxes),
-        (late_ref, away, place, boxes),
+    across = [lax.broadcasted_iota(jnp.int32, (boxes, boxes), n) for n in range(2)]
+    before, same = (across[1] < across[0]).astype(F32), (across[1] == across[0]).astype(F32)
+    slot = lax.broadcasted_iota(jnp.int32, (boxes, early_ref.shape[1]), 1).astype(F32)
+    for ref, fixed, chosen, where, zeros in (
+        (early_ref, EARLY, jnp.logical_not(away), jnp.where(part == 1, place, boxes + place), 2 * boxes),
+        (late_ref, LATE, away, place, boxes),
     ):
         one = chosen.astype(jnp.int32)
         count = jnp.zeros((1, boxes), jnp.int32)
@@ -121,7 +124,15 @@
         ref[...] = jnp.zeros(ref.shape, jnp.int32)
         ref[:entries, :boxes] = front_where
         ref[entries : 2 * entries, :boxes] = front_shift
-        ref[2 * entries :, :boxes] = jnp.broadcast_to(count, (ref.shape[0] - 2 * entries, boxes))
+        ref[2 * entries : 2 * entries + 1, :boxes] = count
+        more = jnp.broadcast_to((count > fixed).astype(F32), (8, boxes))
+        rank = lax.dot_general(before, more, (NT_FORM, ((), ())), preferred_element_type=F32)[:, :1]
+        flag = lax.dot_general(same, more, (NT_FORM, ((), ())), preferred_element_type=F32)[:, :1]
+        box = lax.broadcasted_iota(jnp.int32, slot.shape, 0).astype(F32)
+        chosen_box = jnp.where((slot == rank) & (flag > 0.5), box, 0.0)
+        ref[2 * entries + 1 : 2 * entries + 2, :] = jnp.sum(chosen_box, axis=0, keepdims=True).astype(jnp.int32)
+        total = jnp.sum(more, axis=1, keepdims=True)[:1]
+        ref[2 * entries + 2 : 2 * entries + 3, :] = jnp.broadcast_to(total, (1, ref.shape[1])).astype(jnp.int32)
 
 
 def own_kernel(own_ref, aggregate_ref, disaggregate_ref, radiated_ref, table_ref, up0_ref, up1_ref, down0_ref, down1_ref):
@@ -158,21 +169,18 @@
         out_ref[g, :, :half], out_ref[g, :, half:] = total
         return carry
 
-    def beyond(g, carry):
-        count = list_ref[2 * entries, g]
-
-        @pl.when(count > fixed)
-        def _():
-            def rest(n, total):
-                return add_entries(list_ref, g, (n,), total, radiated_ref, table_ref)
-
-            both = lax.fori_loop(fixed, count, rest, (out_ref[g, :, :half], out_ref[g, :, half:]))
-            out_ref[g, :, :half], out_ref[g, :, half:] = both
-
+    def beyond(place, carry):
+        g = list_ref[2 * entries + 1, place]
+
+        def rest(n, total):
+            return add_entries(list_ref, g, (n,), total, radiated_ref, table_ref)
+
+        both = lax.fori_loop(fixed, list_ref[2 * entries, g], rest, (out_ref[g, :, :half], out_ref[g, :, half:]))
+        out_ref[g, :, :half], out_ref[g, :, half:] = both
         return carry
 
-    lax.fori_loop(0, out_ref.shape[0], one_box, 0, unroll=2)
-    lax.fori_loop(0, out_ref.shape[0], beyond, 0)
+    lax.fori_loop(0, out_ref.shape[0], one_box, 0, unroll=4)
+    lax.fori_loop(0, list_ref[2 * entries + 2, 0], beyond, 0)
 
 
 def mid_kernel(
@@ -214,19 +222,22 @@
     devices = far_ref.shape[0]
     own = illum // devices
     pieces = [(c, b) for c in range(parts) for b in range(boxes)]
-    loads = []
-    for n, (c, b) in enumerate(pieces):
-        loads.append(pltpu.make_async_copy(far_ref.at[:, pl.ds(n * own, own), :], rows_ref.at[n], far_sem.at[n]))
-        loads.append(pltpu.make_async_copy(near_ref.at[c, b], block_ref.at[n], near_sem.at[n]))
+    halves = [pl.ds(h * (devices // 2), devices // 2) for h in range(2)]
+    arrive = [pltpu.make_async_copy(far_ref.at[half], rows_ref.at[half], far_sem.at[h]) for h, half in enumerate(halves)]
+    loads = [pltpu.make_async_copy(near_ref.at[c, b], block_ref.at[n], near_sem.at[n]) for n, (c, b) in enumerate(pieces)]
     stores = [pltpu.make_async_copy(sum_ref.at[n], out_ref.at[c, b], out_sem.at[n]) for n, (c, b) in enumerate(pieces)]
-    for load in loads:
-        load.start()
-    for n in range(len(pieces)):
-        loads[2 * n].wait()
-        turned = rows_ref[n].reshape(illum, lanes).T
-        loads[2 * n + 1].wait()
-        sum_ref[n] = block_ref[n] + turned
-        stores[n].start()
+    for copy in arrive + loads:
+        copy.start()
+    for h, half in enumerate(halves):
+        arrive[h].wait()
+        columns = slice(h * (illum // 2), (h + 1) * (illum // 2))
+        for n in range(len(pieces)):
+            turned = rows_ref[half, n * own : (n + 1) * own, :].reshape(illum // 2, lanes).T
+            if h == 0:
+                loads[n].wait()
+            sum_ref[n, :, columns] = block_ref[n, :, columns] + turned
+            if h == 1:
+                stores[n].start()
     for store in stores:
         store.wait()
 
@@ -235,6 +246,7 @@
     specs = [pl.BlockSpec(memory_space=kind) for kind in kinds]
 
     def run(*args):
+        moved = 4 * sum(a.size for a in (*args, *jax.tree.leaves(outs)))
         return pl.pallas_call(
             kernel,
             out_shape=outs,
@@ -242,7 +254,7 @@
             out_specs=jax.tree.map(lambda _: pl.BlockSpec(memory_space=out_kind), outs),
             scratch_shapes=list(scratch),
             compiler_params=pltpu.CompilerParams(vmem_limit_bytes=limit * MIB),
-            cost_estimate=pl.CostEstimate(flops=micros * 1_000_000_000, bytes_accessed=0, transcendentals=0),
+            cost_estimate=pl.CostEstimate(flops=micros * 1_000_000_000, bytes_accessed=moved, transcendentals=0),
             name=name,
         )(*args)
 
@@ -326,7 +338,14 @@
         join_kernel,
         shape(*currents.shape),
         (ANY, ANY),
-        scratch=(pltpu.VMEM((pieces, devices, own, unknowns), F32), blocks, blocks, *(pltpu.SemaphoreType.DMA((pieces,)),) * 3),
+        scratch=(
+            pltpu.VMEM(far.shape, F32),
+            blocks,
+            blocks,
+            pltpu.SemaphoreType.DMA((2,)),
+            pltpu.SemaphoreType.DMA((pieces,)),
+            pltpu.SemaphoreType.DMA((pieces,)),
+        ),
         limit=FULL,
         name="join",
         out_kind=ANY,

time: 81.9 us -> 80.2 us (0.979)
  Pallas kernels: 25.7 us -> 23.8 us
    pallas_call x7, Pallas kernels: 25.7 us -> 23.8 us  [run(): pl.pallas_call(kernel, out_shape=outs, in_specs=specs, out_specs=jax.tree...]
  transfers between devices with their start and end apart: 6 -> 6, of which waited for: 2 -> 2; matrix products, arithmetic and copies ran while one was open for 0% -> 0% of each run, Pallas kernels for 26% -> 24%
where the time goes in v5:
time: 80.2 us; the launch traced here: 79.4 us
  waiting for transfers between devices  30.3 us (38%)
  starting transfers between devices  24.2 us (30%)
  Pallas kernels  23.8 us (30%)
  local copies, waits for them, and re-layouts  0.89 us (1%)
    pallas_call x7, Pallas kernels, run(): pl.pallas_call(kernel, out_shape=outs, in_specs=specs, out_specs=jax.tree...  23.8 us
    all_to_all x1, waiting for transfers between devices, body(): mine = lax.all_to_all(packed, 'dir', 0, 0, tiled=True)  19.7 us
    all_to_all x1, starting transfers between devices, body(): mine = lax.all_to_all(packed, 'dir', 0, 0, tiled=True)  11.5 us
    all_to_all x1, waiting for transfers between devices, body(): back = lax.all_to_all(far, 'dir', 0, 0, tiled=True)  10.5 us
    all_to_all x1, starting transfers between devices, body(): back = lax.all_to_all(far, 'dir', 0, 0, tiled=True)  4.64 us
    ppermute x1, starting transfers between devices, body(): right = lax.ppermute(beside, 'dir', [(j, i) for i, j in ring])  4.12 us
    ppermute x1, starting transfers between devices, body(): from_cross = lax.ppermute(sent, 'slab', cross)  2.53 us
  transfers between devices with their start and end apart: 6, of which 2 were waited for; matrix products, arithmetic and copies ran while one was open for 0% of the time, Pallas kernels for 24%

profile of v5, /device:TPU:2, one launch (start us, length us, event | category | flops | bytes accessed | tf_op | source)
XLA Modules:
  0.0 79.4 jit_solution(9090205765626095069)
XLA Ops:
  0.0 2.2 %pack.1 = f32[32,40,128]{2,1,0:T(8,128)} custom-call(f32[2,2,128,256]{3,2,1,0:T(8,128)} %own_ref.1, f32[2,8,64]{2,1,0:T(8,128)} %bitcast.5), custom_call_target="tpu_custom_call" | custom-call | flops 1000000000 | bytes 1183744 | tf_op jit(solution)/shard_map/pack/pallas_call | solution.py:250
  2.2 11.5 %all-to-all-start = ((f32[32,40,128]{2,1,0:T(8,128)}), f32[32,40,128]{2,1,0:T(8,128)S(1)}, u32[]{:S(2)}, u32[]{:S(2)}) async-start(f32[32,40,128]{2,1,0:T(8,128)} %pack.1), calls=%async_computation | async-start | bytes 1310720 | tf_op jit(solution)/shard_map/all_to_all | solution.py:300
  13.7 0.0 copy-start.1
  13.7 0.0 copy-start.2
  13.7 0.0 copy-start.3
  13.8 0.4 plan.1
  14.2 19.7 %all-to-all-done.own_ref = f32[32,40,128]{2,1,0:T(8,128)S(1)} async-done(((f32[32,40,128]{2,1,0:T(8,128)}), f32[32,40,128]{2,1,0:T(8,128)S(1)}, u32[]{:S(2)}, u32[]{:S(2)}) %all-to-all-start) | async-done | bytes 655392 | tf_op jit(solution)/shard_map/all_to_all | solution.py:300
  33.9 0.1 slice.3
  34.0 0.1 collective-permute-start
  34.1 2.5 %collective-permute-start.1 = (f32[32,32,128]{2,1,0:T(8,128)S(1)}, f32[32,32,128]{2,1,0:T(8,128)S(1)}, u32[]{:S(2)}, u32[]{:S(2)}) collective-permute-start(f32[32,32,128]{2,1,0:T(8,128)S(1)} %slice.3), channel_id=1, source_target_pairs={{32,64},{96,128},{160,192},{64,32},{128,96},{192,160},{33,65},{97,... | collective-permute-start | bytes 1572872 | tf_op jit(solution)/shard_map/ppermute | solution.py:305
  36.6 1.3 %collective-permute-start.2 = (f32[2,2,128,256]{3,2,1,0:T(8,128)S(1)}, f32[2,2,128,256]{3,2,1,0:T(8,128)S(1)}, u32[]{:S(2)}, u32[]{:S(2)}) collective-permute-start(f32[2,2,128,256]{3,2,1,0:T(8,128)S(1)} %copy-done.1), channel_id=1, source_target_pairs={{0,1},{1,2},{2,3},{3,4},{4,5},{5,6},{6,7},{7,8},{8,9},{9,10},{10,1... | collective-permute-start | bytes 1572872 | tf_op jit(solution)/shard_map/ppermute | solution.py:307
  37.9 4.1 %collective-permute-start.3 = (f32[2,2,128,256]{3,2,1,0:T(8,128)S(1)}, f32[2,2,128,256]{3,2,1,0:T(8,128)}, u32[]{:S(2)}, u32[]{:S(2)}) collective-permute-start(f32[2,2,128,256]{3,2,1,0:T(8,128)S(1)} %copy-done.1), channel_id=1, source_target_pairs={{1,0},{2,1},{3,2},{4,3},{5,4},{6,5},{7,6},{8,7},{9,8},{10,9},{11,1... | collective-permute-start | bytes 1572872 | tf_op jit(solution)/shard_map/ppermute | solution.py:308
  42.0 0.8 own.1
  42.8 0.0 collective-permute-done.block_ref
  42.8 5.6 %mid.1.mid_ref = f32[64,8,512]{2,1,0:T(8,128)S(1)} custom-call(s32[72,128]{1,0:T(8,128)S(1)} %get-tuple-element.20.lists_ref, f32[64,8,512]{2,1,0:T(8,128)S(1)} %get-tuple-element.22.own_ref, f32[64,8,512]{2,1,0:T(8,128)S(1)} %get-tuple-element.23.table_ref, f32[32,32,128]{2,1,0:T(8,128)S(1)} %collective-permute-done.block_ref, ...), custom_call_target="tpu_custom_call" | custom-call | flops 6000000000 | bytes 4755456 | tf_op jit(solution)/shard_map/mid/pallas_call | solution.py:250
  48.4 0.0 collective-permute-done.1.block_ref
  48.4 0.0 copy-start
  48.5 0.0 copy-start.6
  48.5 5.7 %far.1 = f32[32,32,128]{2,1,0:T(8,128)} custom-call(s32[72,128]{1,0:T(8,128)S(1)} %get-tuple-element.19.lists_ref, f32[64,8,512]{2,1,0:T(8,128)S(1)} %mid.1.mid_ref, f32[64,8,512]{2,1,0:T(8,128)S(1)} %get-tuple-element.23.table_ref, f32[32,32,128]{2,1,0:T(8,128)S(1)} %collective-permute-done.1.block_ref, bf16[512,256]{1,0:T(8,128)(2,1)S(1)} %get-tuple-element.24.up0_ref, ...), custom_call_target="tpu_custom_call" | custom-call | flops 5000000000 | bytes 5279744 | tf_op jit(solution)/shard_map/far/pallas_call | solution.py:250
  54.2 4.6 %all-to-all-start.1 = ((f32[32,32,128]{2,1,0:T(8,128)}), f32[32,32,128]{2,1,0:T(8,128)}, u32[]{:S(2)}, u32[]{:S(2)}) async-start(f32[32,32,128]{2,1,0:T(8,128)} %far.1), calls=%async_computation.1 | async-start | bytes 1048576 | tf_op jit(solution)/shard_map/all_to_all | solution.py:331
  58.9 6.7 %near.1.near_ref = f32[2,2,128,256]{3,2,1,0:T(8,128)S(1)} custom-call(s32[2,9]{1,0:T(2,128)S(1)} %copy-done.6, f32[2,2,9,128,128]{4,3,2,1,0:T(8,128)S(1)} %copy-done, f32[2,2,128,256]{3,2,1,0:T(8,128)S(1)} %copy-done.1, f32[2,2,128,256]{3,2,1,0:T(8,128)S(1)} %collective-permute-done.2.left_ref, f32[2,2,128,256]{3,2,1,0:T(8,128)} %collective-permute-done.3.right_ref), custom_call_target="tpu_custom_call" | custom-call | flops 20000000000 | bytes 4456520 | tf_op jit(solution)/shard_map/near/pallas_call | solution.py:250
  65.6 0.8 %copy-done.7 = f32[2,2,128,256]{3,2,1,0:T(8,128)} copy-done((f32[2,2,128,256]{3,2,1,0:T(8,128)}, f32[2,2,128,256]{3,2,1,0:T(8,128)S(1)}, u32[]{:S(2)}) %copy-start.7) | copy-done | bytes 524312
  66.4 10.5 %all-to-all-done.1.far_ref = f32[32,32,128]{2,1,0:T(8,128)} async-done(((f32[32,32,128]{2,1,0:T(8,128)}), f32[32,32,128]{2,1,0:T(8,128)}, u32[]{:S(2)}, u32[]{:S(2)}) %all-to-all-start.1) | async-done | bytes 524320 | tf_op jit(solution)/shard_map/all_to_all | solution.py:331
  76.9 2.5 %join.1 = f32[2,2,128,256]{3,2,1,0:T(8,128)} custom-call(f32[32,32,128]{2,1,0:T(8,128)} %all-to-all-done.1.far_ref, f32[2,2,128,256]{3,2,1,0:T(8,128)} %copy-done.7), custom_call_target="tpu_custom_call" | custom-call | flops 1000000000 | bytes 1572864 | tf_op jit(solution)/shard_map/join/pallas_call | solution.py:250
  (12 shorter events, 0.0 us)
Async XLA Ops:
  0.0 13.7 %copy-start.4 = (s32[64,32]{0,1:T(8,128)S(1)}, s32[64,32]{0,1:T(8,128)}, u32[]{:S(2)}) copy-start(s32[64,32]{0,1:T(8,128)} %param.13) | copy-start | bytes 24580
  0.0 13.7 %copy-start.5 = (s32[64,32]{0,1:T(8,128)S(1)}, s32[64,32]{0,1:T(8,128)}, u32[]{:S(2)}) copy-start(s32[64,32]{0,1:T(8,128)} %param.14) | copy-start | bytes 24580
  2.2 31.7 %all-to-all-start = ((f32[32,40,128]{2,1,0:T(8,128)}), f32[32,40,128]{2,1,0:T(8,128)S(1)}, u32[]{:S(2)}, u32[]{:S(2)}) async-start(f32[32,40,128]{2,1,0:T(8,128)} %pack.1), calls=%async_computation | async-start | bytes 1310720 | tf_op jit(solution)/shard_map/all_to_all | solution.py:300
  13.7 22.9 %copy-start.1 = (f32[2,2,128,256]{3,2,1,0:T(8,128)S(1)}, f32[2,2,128,256]{3,2,1,0:T(8,128)}, u32[]{:S(2)}) copy-start(f32[2,2,128,256]{3,2,1,0:T(8,128)} %own_ref.1) | copy-start | bytes 1572868
  13.7 28.3 %copy-start.2 = (f32[2,256,128]{2,1,0:T(8,128)S(1)}, f32[2,256,128]{2,1,0:T(8,128)}, u32[]{:S(2)}) copy-start(f32[2,256,128]{2,1,0:T(8,128)} %aggregate_ref.1) | copy-start | bytes 786436
  13.7 28.3 %copy-start.3 = (f32[2,128,256]{2,1,0:T(8,128)S(1)}, f32[2,128,256]{2,1,0:T(8,128)}, u32[]{:S(2)}) copy-start(f32[2,128,256]{2,1,0:T(8,128)} %disaggregate_ref.1) | copy-start | bytes 786436
  34.0 8.8 %collective-permute-start = (f32[32,32,128]{2,1,0:T(8,128)S(1)}, f32[32,32,128]{2,1,0:T(8,128)S(1)}, u32[]{:S(2)}, u32[]{:S(2)}) collective-permute-start(f32[32,32,128]{2,1,0:T(8,128)S(1)} %slice.3), channel_id=1, source_target_pairs={{0,32},{64,96},{128,160},{192,224},{32,0},{96,64},{160,128},{224,1... | collective-permute-start | bytes 1572872 | tf_op jit(solution)/shard_map/ppermute | solution.py:306
  34.1 14.4 %collective-permute-start.1 = (f32[32,32,128]{2,1,0:T(8,128)S(1)}, f32[32,32,128]{2,1,0:T(8,128)S(1)}, u32[]{:S(2)}, u32[]{:S(2)}) collective-permute-start(f32[32,32,128]{2,1,0:T(8,128)S(1)} %slice.3), channel_id=1, source_target_pairs={{32,64},{96,128},{160,192},{64,32},{128,96},{192,160},{33,65},{97,... | collective-permute-start | bytes 1572872 | tf_op jit(solution)/shard_map/ppermute | solution.py:305
  36.6 22.2 %collective-permute-start.2 = (f32[2,2,128,256]{3,2,1,0:T(8,128)S(1)}, f32[2,2,128,256]{3,2,1,0:T(8,128)S(1)}, u32[]{:S(2)}, u32[]{:S(2)}) collective-permute-start(f32[2,2,128,256]{3,2,1,0:T(8,128)S(1)} %copy-done.1), channel_id=1, source_target_pairs={{0,1},{1,2},{2,3},{3,4},{4,5},{5,6},{6,7},{7,8},{8,9},{9,10},{10,1... | collective-permute-start | bytes 1572872 | tf_op jit(solution)/shard_map/ppermute | solution.py:307
  37.9 20.9 %collective-permute-start.3 = (f32[2,2,128,256]{3,2,1,0:T(8,128)S(1)}, f32[2,2,128,256]{3,2,1,0:T(8,128)}, u32[]{:S(2)}, u32[]{:S(2)}) collective-permute-start(f32[2,2,128,256]{3,2,1,0:T(8,128)S(1)} %copy-done.1), channel_id=1, source_target_pairs={{1,0},{2,1},{3,2},{4,3},{5,4},{6,5},{7,6},{8,7},{9,8},{10,9},{11,1... | collective-permute-start | bytes 1572872 | tf_op jit(solution)/shard_map/ppermute | solution.py:308
  48.4 10.4 %copy-start = (f32[2,2,9,128,128]{4,3,2,1,0:T(8,128)S(1)}, f32[2,2,9,128,128]{4,3,2,1,0:T(8,128)}, u32[]{:S(2)}) copy-start(f32[2,2,9,128,128]{4,3,2,1,0:T(8,128)} %blocks_ref.1) | copy-start | bytes 7077892
  48.5 10.4 %copy-start.6 = (s32[2,9]{1,0:T(2,128)S(1)}, s32[2,9]{1,0:T(2,128)}, u32[]{:S(2)}) copy-start(s32[2,9]{1,0:T(2,128)} %index_ref.1) | copy-start | bytes 220
  54.2 22.8 %all-to-all-start.1 = ((f32[32,32,128]{2,1,0:T(8,128)}), f32[32,32,128]{2,1,0:T(8,128)}, u32[]{:S(2)}, u32[]{:S(2)}) async-start(f32[32,32,128]{2,1,0:T(8,128)} %far.1), calls=%async_computation.1 | async-start | bytes 1048576 | tf_op jit(solution)/shard_map/all_to_all | solution.py:331
  65.6 0.8 %copy-start.7 = (f32[2,2,128,256]{3,2,1,0:T(8,128)}, f32[2,2,128,256]{3,2,1,0:T(8,128)S(1)}, u32[]{:S(2)}) copy-start(f32[2,2,128,256]{3,2,1,0:T(8,128)S(1)} %near.1.near_ref) | copy-start | bytes 1572868

commit v6 on v5

--- a/solution.py
+++ b/solution.py
@@ -217,27 +217,15 @@
     out_ref[:, rows // 2 :, :] = far[:, lanes:].reshape(devices, rows // 2, lanes)
 
 
-def join_kernel(far_ref, near_ref, out_ref, rows_ref, block_ref, sum_ref, far_sem, near_sem, out_sem):
+def join_kernel(far_ref, near_ref, out_ref, sum_ref, sem):
     parts, boxes, lanes, illum = out_ref.shape
-    devices = far_ref.shape[0]
-    own = illum // devices
-    pieces = [(c, b) for c in range(parts) for b in range(boxes)]
-    halves = [pl.ds(h * (devices // 2), devices // 2) for h in range(2)]
-    arrive = [pltpu.make_async_copy(far_ref.at[half], rows_ref.at[half], far_sem.at[h]) for h, half in enumerate(halves)]
-    loads = [pltpu.make_async_copy(near_ref.at[c, b], block_ref.at[n], near_sem.at[n]) for n, (c, b) in enumerate(pieces)]
-    stores = [pltpu.make_async_copy(sum_ref.at[n], out_ref.at[c, b], out_sem.at[n]) for n, (c, b) in enumerate(pieces)]
-    for copy in arrive + loads:
-        copy.start()
-    for h, half in enumerate(halves):
-        arrive[h].wait()
-        columns = slice(h * (illum // 2), (h + 1) * (illum // 2))
-        for n in range(len(pieces)):
-            turned = rows_ref[half, n * own : (n + 1) * own, :].reshape(illum // 2, lanes).T
-            if h == 0:
-                loads[n].wait()
-            sum_ref[n, :, columns] = block_ref[n, :, columns] + turned
-            if h == 1:
-                stores[n].start()
+    own = illum // far_ref.shape[0]
+    stores = []
+    for n, (c, b) in enumerate((c, b) for c in range(parts) for b in range(boxes)):
+        turned = far_ref[:, n * own : (n + 1) * own, :].reshape(illum, lanes).T
+        sum_ref[n] = near_ref[c, b] + turned
+        stores.append(pltpu.make_async_copy(sum_ref.at[n], out_ref.at[c, b], sem.at[n]))
+        stores[n].start()
     for store in stores:
         store.wait()
 
@@ -337,16 +325,9 @@
     return call(
         join_kernel,
         shape(*currents.shape),
-        (ANY, ANY),
-        scratch=(
-            pltpu.VMEM(far.shape, F32),
-            blocks,
-            blocks,
-            pltpu.SemaphoreType.DMA((2,)),
-            pltpu.SemaphoreType.DMA((pieces,)),
-            pltpu.SemaphoreType.DMA((pieces,)),
-        ),
-        limit=FULL,
+        (VMEM, VMEM),
+        scratch=(blocks, pltpu.SemaphoreType.DMA((pieces,))),
+        micros=0,
         name="join",
         out_kind=ANY,
     )(back, near)

time: 80.2 us -> 77.8 us (0.970)
  Pallas kernels: 23.8 us -> 22.6 us
  local copies, waits for them, and re-layouts: 0.89 us -> 0.08 us
    pallas_call x7, Pallas kernels: 23.8 us -> 22.6 us  [run(): pl.pallas_call(kernel, out_shape=outs, in_specs=specs, out_specs=jax.tree...]
    unnamed x16 -> x12, local copies, waits for them, and re-layouts: 0.84 us -> 0.03 us
  transfers between devices with their start and end apart: 6 -> 6, of which waited for: 2 -> 2; matrix products, arithmetic and copies ran while one was open for 0% -> 0% of each run, Pallas kernels for 24% -> 25%
where the time goes in v6:
time: 77.8 us; the launch traced here: 77.2 us
  waiting for transfers between devices  30.9 us (40%)
  starting transfers between devices  23.5 us (30%)
  Pallas kernels  22.6 us (29%)
    pallas_call x7, Pallas kernels, run(): pl.pallas_call(kernel, out_shape=outs, in_specs=specs, out_specs=jax.tree...  22.6 us
    all_to_all x1, waiting for transfers between devices, body(): mine = lax.all_to_all(packed, 'dir', 0, 0, tiled=True)  19.7 us
    all_to_all x1, starting transfers between devices, body(): mine = lax.all_to_all(packed, 'dir', 0, 0, tiled=True)  11.5 us
    all_to_all x1, waiting for transfers between devices, body(): back = lax.all_to_all(far, 'dir', 0, 0, tiled=True)  11.2 us
    ppermute x1, starting transfers between devices, body(): right = lax.ppermute(beside, 'dir', [(j, i) for i, j in ring])  4.12 us
    all_to_all x1, starting transfers between devices, body(): back = lax.all_to_all(far, 'dir', 0, 0, tiled=True)  3.9 us
    ppermute x1, starting transfers between devices, body(): from_cross = lax.ppermute(sent, 'slab', cross)  2.53 us
  transfers between devices with their start and end apart: 6, of which 2 were waited for; matrix products, arithmetic and copies ran while one was open for 0% of the time, Pallas kernels for 25%

profile of v6, /device:TPU:2, one launch (start us, length us, event | category | flops | bytes accessed | tf_op | source)
XLA Modules:
  0.0 77.2 jit_solution(5175240747789234123)
XLA Ops:
  0.0 2.2 %pack.1 = f32[32,40,128]{2,1,0:T(8,128)} custom-call(f32[2,2,128,256]{3,2,1,0:T(8,128)} %own_ref.1, f32[2,8,64]{2,1,0:T(8,128)} %bitcast.5), custom_call_target="tpu_custom_call" | custom-call | flops 1000000000 | bytes 1183744 | tf_op jit(solution)/shard_map/pack/pallas_call | solution.py:238
  2.2 11.5 %all-to-all-start = ((f32[32,40,128]{2,1,0:T(8,128)}), f32[32,40,128]{2,1,0:T(8,128)S(1)}, u32[]{:S(2)}, u32[]{:S(2)}) async-start(f32[32,40,128]{2,1,0:T(8,128)} %pack.1), calls=%async_computation | async-start | bytes 1310720 | tf_op jit(solution)/shard_map/all_to_all | solution.py:288
  13.7 0.0 copy-start.1
  13.7 0.0 copy-start.2
  13.7 0.4 plan.1
  14.1 19.7 %all-to-all-done.own_ref = f32[32,40,128]{2,1,0:T(8,128)S(1)} async-done(((f32[32,40,128]{2,1,0:T(8,128)}), f32[32,40,128]{2,1,0:T(8,128)S(1)}, u32[]{:S(2)}, u32[]{:S(2)}) %all-to-all-start) | async-done | bytes 655392 | tf_op jit(solution)/shard_map/all_to_all | solution.py:288
  33.9 0.1 slice.3
  33.9 0.1 collective-permute-start
  34.0 2.5 %collective-permute-start.1 = (f32[32,32,128]{2,1,0:T(8,128)S(1)}, f32[32,32,128]{2,1,0:T(8,128)S(1)}, u32[]{:S(2)}, u32[]{:S(2)}) collective-permute-start(f32[32,32,128]{2,1,0:T(8,128)S(1)} %slice.3), channel_id=1, source_target_pairs={{32,64},{96,128},{160,192},{64,32},{128,96},{192,160},{33,65},{97,... | collective-permute-start | bytes 1572872 | tf_op jit(solution)/shard_map/ppermute | solution.py:293
  36.6 1.3 %collective-permute-start.2 = (f32[2,2,128,256]{3,2,1,0:T(8,128)}, f32[2,2,128,256]{3,2,1,0:T(8,128)}, u32[]{:S(2)}, u32[]{:S(2)}) collective-permute-start(f32[2,2,128,256]{3,2,1,0:T(8,128)} %own_ref.1), channel_id=1, source_target_pairs={{0,1},{1,2},{2,3},{3,4},{4,5},{5,6},{6,7},{7,8},{8,9},{9,10},{10,1... | collective-permute-start | bytes 1572872 | tf_op jit(solution)/shard_map/ppermute | solution.py:295
  37.9 4.1 %collective-permute-start.3 = (f32[2,2,128,256]{3,2,1,0:T(8,128)}, f32[2,2,128,256]{3,2,1,0:T(8,128)}, u32[]{:S(2)}, u32[]{:S(2)}) collective-permute-start(f32[2,2,128,256]{3,2,1,0:T(8,128)} %own_ref.1), channel_id=1, source_target_pairs={{1,0},{2,1},{3,2},{4,3},{5,4},{6,5},{7,6},{8,7},{9,8},{10,9},{11,1... | collective-permute-start | bytes 1572872 | tf_op jit(solution)/shard_map/ppermute | solution.py:296
  42.0 0.8 own.1
  42.8 0.0 collective-permute-done.block_ref
  42.8 5.5 %mid.1.mid_ref = f32[64,8,512]{2,1,0:T(8,128)S(1)} custom-call(s32[72,128]{1,0:T(8,128)S(1)} %get-tuple-element.20.lists_ref, f32[64,8,512]{2,1,0:T(8,128)S(1)} %get-tuple-element.22.own_ref, f32[64,8,512]{2,1,0:T(8,128)S(1)} %get-tuple-element.23.table_ref, f32[32,32,128]{2,1,0:T(8,128)S(1)} %collective-permute-done.block_ref, ...), custom_call_target="tpu_custom_call" | custom-call | flops 6000000000 | bytes 4755456 | tf_op jit(solution)/shard_map/mid/pallas_call | solution.py:238
  48.3 0.0 collective-permute-done.1.block_ref
  48.3 0.0 copy-start
  48.4 0.0 copy-start.5
  48.4 5.8 %far.1 = f32[32,32,128]{2,1,0:T(8,128)} custom-call(s32[72,128]{1,0:T(8,128)S(1)} %get-tuple-element.19.lists_ref, f32[64,8,512]{2,1,0:T(8,128)S(1)} %mid.1.mid_ref, f32[64,8,512]{2,1,0:T(8,128)S(1)} %get-tuple-element.23.table_ref, f32[32,32,128]{2,1,0:T(8,128)S(1)} %collective-permute-done.1.block_ref, bf16[512,256]{1,0:T(8,128)(2,1)S(1)} %get-tuple-element.24.up0_ref, ...), custom_call_target="tpu_custom_call" | custom-call | flops 5000000000 | bytes 5279744 | tf_op jit(solution)/shard_map/far/pallas_call | solution.py:238
  54.2 3.9 %all-to-all-start.1 = ((f32[32,32,128]{2,1,0:T(8,128)}), f32[32,32,128]{2,1,0:T(8,128)S(1)}, u32[]{:S(2)}, u32[]{:S(2)}) async-start(f32[32,32,128]{2,1,0:T(8,128)} %far.1), calls=%async_computation.1 | async-start | bytes 1048576 | tf_op jit(solution)/shard_map/all_to_all | solution.py:319
  58.1 0.0 collective-permute-done.2.left_ref
  58.1 0.0 collective-permute-done.3.right_ref
  58.1 7.0 %near.1.near_ref = f32[2,2,128,256]{3,2,1,0:T(8,128)S(1)} custom-call(s32[2,9]{1,0:T(2,128)S(1)} %copy-done.5, f32[2,2,9,128,128]{4,3,2,1,0:T(8,128)S(1)} %copy-done, f32[2,2,128,256]{3,2,1,0:T(8,128)} %own_ref.1, f32[2,2,128,256]{3,2,1,0:T(8,128)} %collective-permute-done.2.left_ref, f32[2,2,128,256]{3,2,1,0:T(8,128)} %collective-permute-done.3.right_ref), custom_call_target="tpu_custom_call" | custom-call | flops 20000000000 | bytes 4456520 | tf_op jit(solution)/shard_map/near/pallas_call | solution.py:238
  65.1 11.2 %all-to-all-done.1.far_ref = f32[32,32,128]{2,1,0:T(8,128)S(1)} async-done(((f32[32,32,128]{2,1,0:T(8,128)}), f32[32,32,128]{2,1,0:T(8,128)S(1)}, u32[]{:S(2)}, u32[]{:S(2)}) %all-to-all-start.1) | async-done | bytes 524320 | tf_op jit(solution)/shard_map/all_to_all | solution.py:319
  76.3 0.9 %join.1 = f32[2,2,128,256]{3,2,1,0:T(8,128)} custom-call(f32[32,32,128]{2,1,0:T(8,128)S(1)} %all-to-all-done.1.far_ref, f32[2,2,128,256]{3,2,1,0:T(8,128)S(1)} %near.1.near_ref), custom_call_target="tpu_custom_call" | custom-call | bytes 1572864 | tf_op jit(solution)/shard_map/join/pallas_call | solution.py:238
  (8 shorter events, 0.0 us)
Async XLA Ops:
  0.0 13.7 %copy-start.3 = (s32[64,32]{0,1:T(8,128)S(1)}, s32[64,32]{0,1:T(8,128)}, u32[]{:S(2)}) copy-start(s32[64,32]{0,1:T(8,128)} %param.13) | copy-start | bytes 24580
  0.0 13.7 %copy-start.4 = (s32[64,32]{0,1:T(8,128)S(1)}, s32[64,32]{0,1:T(8,128)}, u32[]{:S(2)}) copy-start(s32[64,32]{0,1:T(8,128)} %param.14) | copy-start | bytes 24580
  2.2 31.7 %all-to-all-start = ((f32[32,40,128]{2,1,0:T(8,128)}), f32[32,40,128]{2,1,0:T(8,128)S(1)}, u32[]{:S(2)}, u32[]{:S(2)}) async-start(f32[32,40,128]{2,1,0:T(8,128)} %pack.1), calls=%async_computation | async-start | bytes 1310720 | tf_op jit(solution)/shard_map/all_to_all | solution.py:288
  13.7 28.3 %copy-start.1 = (f32[2,256,128]{2,1,0:T(8,128)S(1)}, f32[2,256,128]{2,1,0:T(8,128)}, u32[]{:S(2)}) copy-start(f32[2,256,128]{2,1,0:T(8,128)} %aggregate_ref.1) | copy-start | bytes 786436
  13.7 28.3 %copy-start.2 = (f32[2,128,256]{2,1,0:T(8,128)S(1)}, f32[2,128,256]{2,1,0:T(8,128)}, u32[]{:S(2)}) copy-start(f32[2,128,256]{2,1,0:T(8,128)} %disaggregate_ref.1) | copy-start | bytes 786436
  33.9 8.8 %collective-permute-start = (f32[32,32,128]{2,1,0:T(8,128)S(1)}, f32[32,32,128]{2,1,0:T(8,128)S(1)}, u32[]{:S(2)}, u32[]{:S(2)}) collective-permute-start(f32[32,32,128]{2,1,0:T(8,128)S(1)} %slice.3), channel_id=1, source_target_pairs={{0,32},{64,96},{128,160},{192,224},{32,0},{96,64},{160,128},{224,1... | collective-permute-start | bytes 1572872 | tf_op jit(solution)/shard_map/ppermute | solution.py:294
  34.0 14.3 %collective-permute-start.1 = (f32[32,32,128]{2,1,0:T(8,128)S(1)}, f32[32,32,128]{2,1,0:T(8,128)S(1)}, u32[]{:S(2)}, u32[]{:S(2)}) collective-permute-start(f32[32,32,128]{2,1,0:T(8,128)S(1)} %slice.3), channel_id=1, source_target_pairs={{32,64},{96,128},{160,192},{64,32},{128,96},{192,160},{33,65},{97,... | collective-permute-start | bytes 1572872 | tf_op jit(solution)/shard_map/ppermute | solution.py:293
  36.6 21.5 %collective-permute-start.2 = (f32[2,2,128,256]{3,2,1,0:T(8,128)}, f32[2,2,128,256]{3,2,1,0:T(8,128)}, u32[]{:S(2)}, u32[]{:S(2)}) collective-permute-start(f32[2,2,128,256]{3,2,1,0:T(8,128)} %own_ref.1), channel_id=1, source_target_pairs={{0,1},{1,2},{2,3},{3,4},{4,5},{5,6},{6,7},{7,8},{8,9},{9,10},{10,1... | collective-permute-start | bytes 1572872 | tf_op jit(solution)/shard_map/ppermute | solution.py:295
  37.9 20.2 %collective-permute-start.3 = (f32[2,2,128,256]{3,2,1,0:T(8,128)}, f32[2,2,128,256]{3,2,1,0:T(8,128)}, u32[]{:S(2)}, u32[]{:S(2)}) collective-permute-start(f32[2,2,128,256]{3,2,1,0:T(8,128)} %own_ref.1), channel_id=1, source_target_pairs={{1,0},{2,1},{3,2},{4,3},{5,4},{6,5},{7,6},{8,7},{9,8},{10,9},{11,1... | collective-permute-start | bytes 1572872 | tf_op jit(solution)/shard_map/ppermute | solution.py:296
  48.3 9.8 %copy-start = (f32[2,2,9,128,128]{4,3,2,1,0:T(8,128)S(1)}, f32[2,2,9,128,128]{4,3,2,1,0:T(8,128)}, u32[]{:S(2)}) copy-start(f32[2,2,9,128,128]{4,3,2,1,0:T(8,128)} %blocks_ref.1) | copy-start | bytes 7077892
  48.4 9.8 %copy-start.5 = (s32[2,9]{1,0:T(2,128)S(1)}, s32[2,9]{1,0:T(2,128)}, u32[]{:S(2)}) copy-start(s32[2,9]{1,0:T(2,128)} %index_ref.1) | copy-start | bytes 220
  54.2 22.2 %all-to-all-start.1 = ((f32[32,32,128]{2,1,0:T(8,128)}), f32[32,32,128]{2,1,0:T(8,128)S(1)}, u32[]{:S(2)}, u32[]{:S(2)}) async-start(f32[32,32,128]{2,1,0:T(8,128)} %far.1), calls=%async_computation.1 | async-start | bytes 1048576 | tf_op jit(solution)/shard_map/all_to_all | solution.py:319

commit v7 on v6

--- a/solution.py
+++ b/solution.py
@@ -34,17 +34,16 @@
 NT_FORM = ((1,), (1,))
 
 
-def pack_kernel(currents_ref, translations_ref, out_ref, block_ref, table_ref, packed_ref, in_sem, out_sem):
+def pack_kernel(currents_ref, out_ref, block_ref, packed_ref, in_sem, out_sem):
     devices, rows, lanes = out_ref.shape
     parts, boxes, _, illum = currents_ref.shape
     own = illum // devices
     pieces = [(c, b) for c in range(parts) for b in range(boxes)]
     last = len(pieces)
     loads = [pltpu.make_async_copy(currents_ref.at[c, b], block_ref.at[n], in_sem.at[n]) for n, (c, b) in enumerate(pieces)]
-    loads.append(pltpu.make_async_copy(translations_ref, table_ref, in_sem.at[last]))
     stores = [
         pltpu.make_async_copy(packed_ref.at[:, pl.ds(n * own, own), :], out_ref.at[:, pl.ds(n * own, own), :], out_sem.at[n])
-        for n in range(last + 1)
+        for n in range(last)
     ]
     for load in loads:
         load.start()
@@ -52,10 +51,6 @@
         loads[n].wait()
         packed_ref[:, n * own : (n + 1) * own, :] = block_ref[n].T.reshape(devices, own, lanes)
         stores[n].start()
-    loads[last].wait()
-    table = jnp.concatenate([table_ref[0], table_ref[1]], axis=1)
-    packed_ref[:, last * own :, :] = jnp.broadcast_to(table[None], (devices, own, lanes))
-    stores[last].start()
     for store in stores:
         store.wait()
 
@@ -135,14 +130,17 @@
         ref[2 * entries + 2 : 2 * entries + 3, :] = jnp.broadcast_to(total, (1, ref.shape[1])).astype(jnp.int32)
 
 
-def own_kernel(own_ref, aggregate_ref, disaggregate_ref, radiated_ref, table_ref, up0_ref, up1_ref, down0_ref, down1_ref):
+def own_kernel(own_ref, tables_ref, aggregate_ref, disaggregate_ref, radiated_ref, table_ref, up0_ref, up1_ref, down0_ref, down1_ref):
     boxes, sub, width = radiated_ref.shape
     up = split(complex_rows(aggregate_ref))
     up0_ref[...], up1_ref[...] = up
     down0_ref[...], down1_ref[...] = split(complex_rows(disaggregate_ref))
     radiated_ref[...] = radiate(own_ref, up).reshape(boxes, sub, width)
-    devices, rows, lanes = own_ref.shape
-    table = own_ref[:, RE_IM_ROWS:, :].reshape(devices * (rows - RE_IM_ROWS), lanes).T
+    devices, lanes = own_ref.shape[0], tables_ref.shape[1]
+    rows = tables_ref.shape[0] // devices
+    me = lax.axis_index("dir")
+    ordered = [tables_ref[pl.ds(pl.multiple_of((me ^ d) * rows, rows), rows), :] for d in range(devices)]
+    table = jnp.concatenate(ordered, axis=0).T
     half = lanes // 2
     wide = jnp.concatenate([table[:half], table[half:]], axis=1)
     table_ref[...] = jnp.broadcast_to(wide[:, None, :], table_ref.shape)
@@ -253,6 +251,19 @@
     return jax.ShapeDtypeStruct(dims, kind)
 
 
+def gathered(block, devices):
+    step = 1
+    while step < devices:
+        count = min(4, devices // step)
+        blocks = [block]
+        for p in range(1, count):
+            pairs = [(i, i ^ (p * step)) for i in range(devices)]
+            blocks.append(lax.ppermute(block, "dir", pairs))
+        block = jnp.concatenate(blocks, axis=0)
+        step *= count
+    return block
+
+
 def body(currents, near_blocks, near_index, aggregate, translations, inter_source, inter_shift, disaggregate):
     devices = lax.axis_size("dir")
     slabs = lax.axis_size("slab")
@@ -266,39 +277,37 @@
     pairs_of = [[(i, i + 1) for i in range(start, slabs - 1, 2)] for start in (0, 1)]
     same, cross = [p + [(j, i) for i, j in p] for p in pairs_of]
 
-    turned = jnp.transpose(translations, (0, 2, 1))
     pieces = parts * box_dev
     blocks = pltpu.VMEM((pieces, unknowns, illum), F32)
-    whole = shape(devices, rows + turned.shape[1], unknowns)
+    whole = shape(devices, rows, unknowns)
     packed = call(
         pack_kernel,
         whole,
-        (ANY, ANY),
+        (ANY,),
         scratch=(
             blocks,
-            pltpu.VMEM(turned.shape, F32),
             pltpu.VMEM(whole.shape, F32),
-            pltpu.SemaphoreType.DMA((pieces + 1,)),
-            pltpu.SemaphoreType.DMA((pieces + 1,)),
+            pltpu.SemaphoreType.DMA((pieces,)),
+            pltpu.SemaphoreType.DMA((pieces,)),
         ),
         limit=FULL,
         name="pack",
         out_kind=ANY,
-    )(currents, turned)
+    )(currents)
     mine = lax.all_to_all(packed, "dir", 0, 0, tiled=True)
+    tables = gathered(jnp.transpose(translations, (2, 0, 1)).reshape(-1, parts * ops), devices)
     lists = shape(2 * entries + LIST_ROWS, 128, kind=jnp.int32)
     early, late = call(plan_kernel, (lists, lists), (VMEM, VMEM), name="plan")(inter_source.T, inter_shift.T)
-    mine, beside, early, late = lax.optimization_barrier((mine, currents, early, late))
-    sent = mine[:, :rows]
-    from_cross = lax.ppermute(sent, "slab", cross)
-    from_same = lax.ppermute(sent, "slab", same)
+    mine, beside, early, late, tables = lax.optimization_barrier((mine, currents, early, late, tables))
+    from_cross = lax.ppermute(mine, "slab", cross)
+    from_same = lax.ppermute(mine, "slab", same)
     left = lax.ppermute(beside, "dir", ring)
     right = lax.ppermute(beside, "dir", [(j, i) for i, j in ring])
     field = shape(boxes, own, width)
     up, down = shape(width, 2 * unknowns, kind=BF16), shape(2 * unknowns, width, kind=BF16)
     radiated, table, up0, up1, down0, down1 = call(
-        own_kernel, (field, shape(ops, own, width), up, up, down, down), (VMEM,) * 3, name="own"
-    )(mine, aggregate, disaggregate)
+        own_kernel, (field, shape(ops, own, width), up, up, down, down), (VMEM,) * 4, name="own"
+    )(mine, tables, aggregate, disaggregate)
     staging = (pltpu.SMEM(lists.shape, jnp.int32), pltpu.SemaphoreType.DMA)
     partial = call(
         mid_kernel,

time: 77.8 us -> 85 us (1.093)
  starting transfers between devices: 23.5 us -> 35.5 us
  waiting for transfers between devices: 30.9 us -> 26.2 us
    all_to_all x1, waiting for transfers between devices: 19.7 us -> 0.01 us  [body(): mine = lax.all_to_all(packed, 'dir', 0, 0, tiled=True)]
    ppermute x2 -> x9, waiting for transfers between devices: 0.01 us -> 14.9 us  [the longest x7 14.9 us: gathered(): blocks.append(lax.ppermute(block, 'dir', pairs))]
    ppermute x2 -> x9, starting transfers between devices: 2.63 us -> 14.8 us  [the longest x7 12.2 us: gathered(): blocks.append(lax.ppermute(block, 'dir', pairs))]
    all_to_all x1, starting transfers between devices: 3.9 us -> 6.93 us  [body(): back = lax.all_to_all(far, 'dir', 0, 0, tiled=True)]
    ppermute x1, starting transfers between devices: 4.12 us -> 2.01 us  [body(): right = lax.ppermute(beside, 'dir', [(j, i) for i, j in ring])]
    ppermute x1, starting transfers between devices: 1.31 us -> 0.09 us  [body(): left = lax.ppermute(beside, 'dir', ring)]
  transfers between devices with their start and end apart: 6 -> 13, of which waited for: 2 -> 6; matrix products, arithmetic and copies ran while one was open for 0% -> 0% of each run, Pallas kernels for 25% -> 23%
where the time goes in v7:
time: 85 us; the launch traced here: 84.6 us
  starting transfers between devices  35.5 us (42%)
  waiting for transfers between devices  26.2 us (31%)
  Pallas kernels  22.6 us (27%)
    pallas_call x7, Pallas kernels, run(): pl.pallas_call(kernel, out_shape=outs, in_specs=specs, out_specs=jax.tree...  22.6 us
    ppermute x7, waiting for transfers between devices, gathered(): blocks.append(lax.ppermute(block, 'dir', pairs))  14.9 us
    ppermute x7, starting transfers between devices, gathered(): blocks.append(lax.ppermute(block, 'dir', pairs))  12.2 us
    all_to_all x1, starting transfers between devices, body(): mine = lax.all_to_all(packed, 'dir', 0, 0, tiled=True)  11.6 us
    all_to_all x1, waiting for transfers between devices, body(): back = lax.all_to_all(far, 'dir', 0, 0, tiled=True)  11.2 us
    all_to_all x1, starting transfers between devices, body(): back = lax.all_to_all(far, 'dir', 0, 0, tiled=True)  6.93 us
    ppermute x1, starting transfers between devices, body(): from_cross = lax.ppermute(mine, 'slab', cross)  2.53 us
    ppermute x1, starting transfers between devices, body(): right = lax.ppermute(beside, 'dir', [(j, i) for i, j in ring])  2.01 us
  transfers between devices with their start and end apart: 13, of which 6 were waited for; matrix products, arithmetic and copies ran while one was open for 0% of the time, Pallas kernels for 23%

profile of v7, /device:TPU:2, one launch (start us, length us, event | category | flops | bytes accessed | tf_op | source)
XLA Modules:
  0.0 84.6 jit_solution(17199071048690703496)
XLA Ops:
  0.0 2.1 %pack.1 = f32[32,32,128]{2,1,0:T(8,128)} custom-call(f32[2,2,128,256]{3,2,1,0:T(8,128)} %own_ref.1), custom_call_target="tpu_custom_call" | custom-call | flops 1000000000 | bytes 1048576 | tf_op jit(solution)/shard_map/pack/pallas_call | solution.py:236
  2.1 11.6 %all-to-all-start = ((f32[32,32,128]{2,1,0:T(8,128)}), f32[32,32,128]{2,1,0:T(8,128)S(1)}, u32[]{:S(2)}, u32[]{:S(2)}) async-start(f32[32,32,128]{2,1,0:T(8,128)} %pack.1), calls=%async_computation | async-start | bytes 1048576 | tf_op jit(solution)/shard_map/all_to_all | solution.py:297
  13.8 1.8 %collective-permute-start = (f32[8,128]{1,0:T(8,128)S(1)}, f32[8,128]{1,0:T(8,128)S(1)}, u32[]{:S(2)}, u32[]{:S(2)}) collective-permute-start(f32[8,128]{1,0:T(8,128)S(1)} %reshape.3), channel_id=1, source_target_pairs={{0,1},{1,0},{2,3},{3,2},{4,5},{5,4},{6,7},{7,6},{8,9},{9,8},{10,11... | collective-permute-start | bytes 12296 | tf_op jit(solution)/shard_map/ppermute | solution.py:261
  15.7 2.7 %collective-permute-start.1 = (f32[8,128]{1,0:T(8,128)S(1)}, f32[8,128]{1,0:T(8,128)S(1)}, u32[]{:S(2)}, u32[]{:S(2)}) collective-permute-start(f32[8,128]{1,0:T(8,128)S(1)} %reshape.3), channel_id=1, source_target_pairs={{0,2},{1,3},{2,0},{3,1},{4,6},{5,7},{6,4},{7,5},{8,10},{9,11},{10,... | collective-permute-start | bytes 12296 | tf_op jit(solution)/shard_map/ppermute | solution.py:261
  18.3 0.2 collective-permute-start.2
  18.6 2.4 %collective-permute-done.1 = f32[8,128]{1,0:T(8,128)S(1)} collective-permute-done((f32[8,128]{1,0:T(8,128)S(1)}, f32[8,128]{1,0:T(8,128)S(1)}, u32[]{:S(2)}, u32[]{:S(2)}) %collective-permute-start.1) | collective-permute-done | bytes 4128 | tf_op jit(solution)/shard_map/ppermute | solution.py:261
  21.0 2.2 %collective-permute-done.2 = f32[8,128]{1,0:T(8,128)S(1)} collective-permute-done((f32[8,128]{1,0:T(8,128)S(1)}, f32[8,128]{1,0:T(8,128)S(1)}, u32[]{:S(2)}, u32[]{:S(2)}) %collective-permute-start.2) | collective-permute-done | bytes 4128 | tf_op jit(solution)/shard_map/ppermute | solution.py:261
  23.2 1.5 %collective-permute-start.3 = (f32[32,128]{1,0:T(8,128)S(1)}, f32[32,128]{1,0:T(8,128)S(1)}, u32[]{:S(2)}, u32[]{:S(2)}) collective-permute-start(f32[32,128]{1,0:T(8,128)S(1)} %get-tuple-element.39), channel_id=1, source_target_pairs={{0,4},{1,5},{2,6},{3,7},{4,0},{5,1},{6,2},{7,3},{8,12},{9,13},{10,... | collective-permute-start | bytes 49160 | tf_op jit(solution)/shard_map/ppermute | solution.py:261
  24.7 2.3 %collective-permute-start.4 = (f32[32,128]{1,0:T(8,128)S(1)}, f32[32,128]{1,0:T(8,128)S(1)}, u32[]{:S(2)}, u32[]{:S(2)}) collective-permute-start(f32[32,128]{1,0:T(8,128)S(1)} %get-tuple-element.39), channel_id=1, source_target_pairs={{0,8},{1,9},{2,10},{3,11},{4,12},{5,13},{6,14},{7,15},{8,0},{9,1},... | collective-permute-start | bytes 49160 | tf_op jit(solution)/shard_map/ppermute | solution.py:261
  27.0 0.5 collective-permute-start.5
  27.6 2.0 %collective-permute-done.4 = f32[32,128]{1,0:T(8,128)S(1)} collective-permute-done((f32[32,128]{1,0:T(8,128)S(1)}, f32[32,128]{1,0:T(8,128)S(1)}, u32[]{:S(2)}, u32[]{:S(2)}) %collective-permute-start.4) | collective-permute-done | bytes 16416 | tf_op jit(solution)/shard_map/ppermute | solution.py:261
  29.6 3.0 %collective-permute-done.5 = f32[32,128]{1,0:T(8,128)S(1)} collective-permute-done((f32[32,128]{1,0:T(8,128)S(1)}, f32[32,128]{1,0:T(8,128)S(1)}, u32[]{:S(2)}, u32[]{:S(2)}) %collective-permute-start.5) | collective-permute-done | bytes 16416 | tf_op jit(solution)/shard_map/ppermute | solution.py:261
  32.6 3.1 %collective-permute-start.6 = (f32[128,128]{1,0:T(8,128)S(1)}, f32[128,128]{1,0:T(8,128)S(1)}, u32[]{:S(2)}, u32[]{:S(2)}) collective-permute-start(f32[128,128]{1,0:T(8,128)S(1)} %get-tuple-element.31), channel_id=1, source_target_pairs={{0,16},{1,17},{2,18},{3,19},{4,20},{5,21},{6,22},{7,23},{8,24},{9,... | collective-permute-start | bytes 196616 | tf_op jit(solution)/shard_map/ppermute | solution.py:261
  35.7 0.4 plan.1
  36.1 5.4 %collective-permute-done.6 = f32[128,128]{1,0:T(8,128)S(1)} collective-permute-done((f32[128,128]{1,0:T(8,128)S(1)}, f32[128,128]{1,0:T(8,128)S(1)}, u32[]{:S(2)}, u32[]{:S(2)}) %collective-permute-start.6) | collective-permute-done | bytes 65568 | tf_op jit(solution)/shard_map/ppermute | solution.py:261
  41.6 2.5 %collective-permute-start.8 = (f32[32,32,128]{2,1,0:T(8,128)S(1)}, f32[32,32,128]{2,1,0:T(8,128)S(1)}, u32[]{:S(2)}, u32[]{:S(2)}) collective-permute-start(f32[32,32,128]{2,1,0:T(8,128)S(1)} %all-to-all-done.own_ref), channel_id=1, source_target_pairs={{32,64},{96,128},{160,192},{64,32},{128,96},{192,160},{33,65},{97,... | collective-permute-start | bytes 1572872 | tf_op jit(solution)/shard_map/ppermute | solution.py:302
  44.1 2.0 %collective-permute-start.10 = (f32[2,2,128,256]{3,2,1,0:T(8,128)}, f32[2,2,128,256]{3,2,1,0:T(8,128)}, u32[]{:S(2)}, u32[]{:S(2)}) collective-permute-start(f32[2,2,128,256]{3,2,1,0:T(8,128)} %own_ref.1), channel_id=1, source_target_pairs={{1,0},{2,1},{3,2},{4,3},{5,4},{6,5},{7,6},{8,7},{9,8},{10,9},{11,1... | collective-permute-start | bytes 1572872 | tf_op jit(solution)/shard_map/ppermute | solution.py:305
  46.2 0.7 own.1
  47.0 5.6 %mid.1.mid_ref = f32[64,8,512]{2,1,0:T(8,128)S(1)} custom-call(s32[72,128]{1,0:T(8,128)S(1)} %get-tuple-element.21.lists_ref, f32[64,8,512]{2,1,0:T(8,128)S(1)} %get-tuple-element.24.own_ref, f32[64,8,512]{2,1,0:T(8,128)S(1)} %get-tuple-element.25.table_ref, f32[32,32,128]{2,1,0:T(8,128)S(1)} %collective-permute-done.7.block_ref, ...), custom_call_target="tpu_custom_call" | custom-call | flops 6000000000 | bytes 4755456 | tf_op jit(solution)/shard_map/mid/pallas_call | solution.py:236
  52.6 5.9 %far.1 = f32[32,32,128]{2,1,0:T(8,128)} custom-call(s32[72,128]{1,0:T(8,128)S(1)} %get-tuple-element.20.lists_ref, f32[64,8,512]{2,1,0:T(8,128)S(1)} %mid.1.mid_ref, f32[64,8,512]{2,1,0:T(8,128)S(1)} %get-tuple-element.25.table_ref, f32[32,32,128]{2,1,0:T(8,128)S(1)} %collective-permute-done.8.block_ref, bf16[512,256]{1,0:T(8,128)(2,1)S(1)} %get-tuple-element.26.up0_ref, ...), custom_call_target="tpu_custom_call" | custom-call | flops 5000000000 | bytes 5279744 | tf_op jit(solution)/shard_map/far/pallas_call | solution.py:236
  58.5 6.9 %all-to-all-start.1 = ((f32[32,32,128]{2,1,0:T(8,128)}), f32[32,32,128]{2,1,0:T(8,128)S(1)}, u32[]{:S(2)}, u32[]{:S(2)}) async-start(f32[32,32,128]{2,1,0:T(8,128)} %far.1), calls=%async_computation.1 | async-start | bytes 1048576 | tf_op jit(solution)/shard_map/all_to_all | solution.py:328
  65.5 7.0 %near.1.near_ref = f32[2,2,128,256]{3,2,1,0:T(8,128)S(1)} custom-call(s32[2,9]{1,0:T(2,128)S(1)} %copy-done.5, f32[2,2,9,128,128]{4,3,2,1,0:T(8,128)S(1)} %copy-done, f32[2,2,128,256]{3,2,1,0:T(8,128)} %own_ref.1, f32[2,2,128,256]{3,2,1,0:T(8,128)} %collective-permute-done.9.left_ref, f32[2,2,128,256]{3,2,1,0:T(8,128)} %collective-permute-done.10.right_ref), custom_call_target="tpu_custom_call" | custom-call | flops 20000000000 | bytes 4456520 | tf_op jit(solution)/shard_map/near/pallas_call | solution.py:236
  72.4 11.2 %all-to-all-done.1.far_ref = f32[32,32,128]{2,1,0:T(8,128)S(1)} async-done(((f32[32,32,128]{2,1,0:T(8,128)}), f32[32,32,128]{2,1,0:T(8,128)S(1)}, u32[]{:S(2)}, u32[]{:S(2)}) %all-to-all-start.1) | async-done | bytes 524320 | tf_op jit(solution)/shard_map/all_to_all | solution.py:328
  83.7 0.9 %join.1 = f32[2,2,128,256]{3,2,1,0:T(8,128)} custom-call(f32[32,32,128]{2,1,0:T(8,128)S(1)} %all-to-all-done.1.far_ref, f32[2,2,128,256]{3,2,1,0:T(8,128)S(1)} %near.1.near_ref), custom_call_target="tpu_custom_call" | custom-call | bytes 1572864 | tf_op jit(solution)/shard_map/join/pallas_call | solution.py:236
  (33 shorter events, 0.3 us)
Async XLA Ops:
  0.0 13.7 %copy-start.6 = (f32[2,64,8]{1,2,0:T(8,128)S(1)}, f32[2,64,8]{1,2,0:T(8,128)}, u32[]{:S(2)}) copy-start(f32[2,64,8]{1,2,0:T(8,128)} %param.12) | copy-start | bytes 12292
  0.0 35.7 %copy-start.3 = (s32[64,32]{0,1:T(8,128)S(1)}, s32[64,32]{0,1:T(8,128)}, u32[]{:S(2)}) copy-start(s32[64,32]{0,1:T(8,128)} %param.13) | copy-start | bytes 24580
  0.0 35.7 %copy-start.4 = (s32[64,32]{0,1:T(8,128)S(1)}, s32[64,32]{0,1:T(8,128)}, u32[]{:S(2)}) copy-start(s32[64,32]{0,1:T(8,128)} %param.14) | copy-start | bytes 24580
  2.1 44.1 %copy-start.1 = (f32[2,256,128]{2,1,0:T(8,128)S(1)}, f32[2,256,128]{2,1,0:T(8,128)}, u32[]{:S(2)}) copy-start(f32[2,256,128]{2,1,0:T(8,128)} %aggregate_ref.1) | copy-start | bytes 786436
  2.1 44.1 %copy-start.2 = (f32[2,128,256]{2,1,0:T(8,128)S(1)}, f32[2,128,256]{2,1,0:T(8,128)}, u32[]{:S(2)}) copy-start(f32[2,128,256]{2,1,0:T(8,128)} %disaggregate_ref.1) | copy-start | bytes 786436
  2.1 39.3 %all-to-all-start = ((f32[32,32,128]{2,1,0:T(8,128)}), f32[32,32,128]{2,1,0:T(8,128)S(1)}, u32[]{:S(2)}, u32[]{:S(2)}) async-start(f32[32,32,128]{2,1,0:T(8,128)} %pack.1), calls=%async_computation | async-start | bytes 1048576 | tf_op jit(solution)/shard_map/all_to_all | solution.py:297
  13.8 4.7 %collective-permute-start = (f32[8,128]{1,0:T(8,128)S(1)}, f32[8,128]{1,0:T(8,128)S(1)}, u32[]{:S(2)}, u32[]{:S(2)}) collective-permute-start(f32[8,128]{1,0:T(8,128)S(1)} %reshape.3), channel_id=1, source_target_pairs={{0,1},{1,0},{2,3},{3,2},{4,5},{5,4},{6,7},{7,6},{8,9},{9,8},{10,11... | collective-permute-start | bytes 12296 | tf_op jit(solution)/shard_map/ppermute | solution.py:261
  15.7 5.3 %collective-permute-start.1 = (f32[8,128]{1,0:T(8,128)S(1)}, f32[8,128]{1,0:T(8,128)S(1)}, u32[]{:S(2)}, u32[]{:S(2)}) collective-permute-start(f32[8,128]{1,0:T(8,128)S(1)} %reshape.3), channel_id=1, source_target_pairs={{0,2},{1,3},{2,0},{3,1},{4,6},{5,7},{6,4},{7,5},{8,10},{9,11},{10,... | collective-permute-start | bytes 12296 | tf_op jit(solution)/shard_map/ppermute | solution.py:261
  18.3 4.9 %collective-permute-start.2 = (f32[8,128]{1,0:T(8,128)S(1)}, f32[8,128]{1,0:T(8,128)S(1)}, u32[]{:S(2)}, u32[]{:S(2)}) collective-permute-start(f32[8,128]{1,0:T(8,128)S(1)} %reshape.3), channel_id=1, source_target_pairs={{0,3},{1,2},{2,1},{3,0},{4,7},{5,6},{6,5},{7,4},{8,11},{9,10},{10,... | collective-permute-start | bytes 12296 | tf_op jit(solution)/shard_map/ppermute | solution.py:261
  23.2 4.4 %collective-permute-start.3 = (f32[32,128]{1,0:T(8,128)S(1)}, f32[32,128]{1,0:T(8,128)S(1)}, u32[]{:S(2)}, u32[]{:S(2)}) collective-permute-start(f32[32,128]{1,0:T(8,128)S(1)} %get-tuple-element.39), channel_id=1, source_target_pairs={{0,4},{1,5},{2,6},{3,7},{4,0},{5,1},{6,2},{7,3},{8,12},{9,13},{10,... | collective-permute-start | bytes 49160 | tf_op jit(solution)/shard_map/ppermute | solution.py:261
  24.7 4.9 %collective-permute-start.4 = (f32[32,128]{1,0:T(8,128)S(1)}, f32[32,128]{1,0:T(8,128)S(1)}, u32[]{:S(2)}, u32[]{:S(2)}) collective-permute-start(f32[32,128]{1,0:T(8,128)S(1)} %get-tuple-element.39), channel_id=1, source_target_pairs={{0,8},{1,9},{2,10},{3,11},{4,12},{5,13},{6,14},{7,15},{8,0},{9,1},... | collective-permute-start | bytes 49160 | tf_op jit(solution)/shard_map/ppermute | solution.py:261
  27.0 5.5 %collective-permute-start.5 = (f32[32,128]{1,0:T(8,128)S(1)}, f32[32,128]{1,0:T(8,128)S(1)}, u32[]{:S(2)}, u32[]{:S(2)}) collective-permute-start(f32[32,128]{1,0:T(8,128)S(1)} %get-tuple-element.39), channel_id=1, source_target_pairs={{0,12},{1,13},{2,14},{3,15},{4,8},{5,9},{6,10},{7,11},{8,4},{9,5},... | collective-permute-start | bytes 49160 | tf_op jit(solution)/shard_map/ppermute | solution.py:261
  32.6 8.9 %collective-permute-start.6 = (f32[128,128]{1,0:T(8,128)S(1)}, f32[128,128]{1,0:T(8,128)S(1)}, u32[]{:S(2)}, u32[]{:S(2)}) collective-permute-start(f32[128,128]{1,0:T(8,128)S(1)} %get-tuple-element.31), channel_id=1, source_target_pairs={{0,16},{1,17},{2,18},{3,19},{4,20},{5,21},{6,22},{7,23},{8,24},{9,... | collective-permute-start | bytes 196616 | tf_op jit(solution)/shard_map/ppermute | solution.py:261
  41.5 5.5 %collective-permute-start.7 = (f32[32,32,128]{2,1,0:T(8,128)S(1)}, f32[32,32,128]{2,1,0:T(8,128)S(1)}, u32[]{:S(2)}, u32[]{:S(2)}) collective-permute-start(f32[32,32,128]{2,1,0:T(8,128)S(1)} %all-to-all-done.own_ref), channel_id=1, source_target_pairs={{0,32},{64,96},{128,160},{192,224},{32,0},{96,64},{160,128},{224,1... | collective-permute-start | bytes 1572872 | tf_op jit(solution)/shard_map/ppermute | solution.py:303
  41.6 11.0 %collective-permute-start.8 = (f32[32,32,128]{2,1,0:T(8,128)S(1)}, f32[32,32,128]{2,1,0:T(8,128)S(1)}, u32[]{:S(2)}, u32[]{:S(2)}) collective-permute-start(f32[32,32,128]{2,1,0:T(8,128)S(1)} %all-to-all-done.own_ref), channel_id=1, source_target_pairs={{32,64},{96,128},{160,192},{64,32},{128,96},{192,160},{33,65},{97,... | collective-permute-start | bytes 1572872 | tf_op jit(solution)/shard_map/ppermute | solution.py:302
  44.1 21.3 %collective-permute-start.10 = (f32[2,2,128,256]{3,2,1,0:T(8,128)}, f32[2,2,128,256]{3,2,1,0:T(8,128)}, u32[]{:S(2)}, u32[]{:S(2)}) collective-permute-start(f32[2,2,128,256]{3,2,1,0:T(8,128)} %own_ref.1), channel_id=1, source_target_pairs={{1,0},{2,1},{3,2},{4,3},{5,4},{6,5},{7,6},{8,7},{9,8},{10,9},{11,1... | collective-permute-start | bytes 1572872 | tf_op jit(solution)/shard_map/ppermute | solution.py:305
  46.1 19.3 %collective-permute-start.9 = (f32[2,2,128,256]{3,2,1,0:T(8,128)}, f32[2,2,128,256]{3,2,1,0:T(8,128)}, u32[]{:S(2)}, u32[]{:S(2)}) collective-permute-start(f32[2,2,128,256]{3,2,1,0:T(8,128)} %own_ref.1), channel_id=1, source_target_pairs={{0,1},{1,2},{2,3},{3,4},{4,5},{5,6},{6,7},{7,8},{8,9},{9,10},{10,1... | collective-permute-start | bytes 1572872 | tf_op jit(solution)/shard_map/ppermute | solution.py:304
  52.6 12.9 %copy-start = (f32[2,2,9,128,128]{4,3,2,1,0:T(8,128)S(1)}, f32[2,2,9,128,128]{4,3,2,1,0:T(8,128)}, u32[]{:S(2)}) copy-start(f32[2,2,9,128,128]{4,3,2,1,0:T(8,128)} %blocks_ref.1) | copy-start | bytes 7077892
  52.6 12.9 %copy-start.5 = (s32[2,9]{1,0:T(2,128)S(1)}, s32[2,9]{1,0:T(2,128)}, u32[]{:S(2)}) copy-start(s32[2,9]{1,0:T(2,128)} %index_ref.1) | copy-start | bytes 220
  58.5 25.2 %all-to-all-start.1 = ((f32[32,32,128]{2,1,0:T(8,128)}), f32[32,32,128]{2,1,0:T(8,128)S(1)}, u32[]{:S(2)}, u32[]{:S(2)}) async-start(f32[32,32,128]{2,1,0:T(8,128)} %far.1), calls=%async_computation.1 | async-start | bytes 1048576 | tf_op jit(solution)/shard_map/all_to_all | solution.py:328

commit v8 on v7

--- a/solution.py
+++ b/solution.py
@@ -130,16 +130,22 @@
         ref[2 * entries + 2 : 2 * entries + 3, :] = jnp.broadcast_to(total, (1, ref.shape[1])).astype(jnp.int32)
 
 
-def own_kernel(own_ref, tables_ref, aggregate_ref, disaggregate_ref, radiated_ref, table_ref, up0_ref, up1_ref, down0_ref, down1_ref):
+def own_kernel(own_ref, aggregate_ref, disaggregate_ref, radiated_ref, up0_ref, up1_ref, down0_ref, down1_ref):
     boxes, sub, width = radiated_ref.shape
     up = split(complex_rows(aggregate_ref))
     up0_ref[...], up1_ref[...] = up
     down0_ref[...], down1_ref[...] = split(complex_rows(disaggregate_ref))
     radiated_ref[...] = radiate(own_ref, up).reshape(boxes, sub, width)
-    devices, lanes = own_ref.shape[0], tables_ref.shape[1]
-    rows = tables_ref.shape[0] // devices
+
+
+def table_kernel(first_ref, second_ref, table_ref, both_ref):
+    devices = lax.axis_size("dir")
+    count, lanes = both_ref.shape
+    rows = count // devices
+    both_ref[: count // 2] = first_ref[...]
+    both_ref[count // 2 :] = second_ref[...]
     me = lax.axis_index("dir")
-    ordered = [tables_ref[pl.ds(pl.multiple_of((me ^ d) * rows, rows), rows), :] for d in range(devices)]
+    ordered = [both_ref[pl.ds(pl.multiple_of((me ^ d) * rows, rows), rows), :] for d in range(devices)]
     table = jnp.concatenate(ordered, axis=0).T
     half = lanes // 2
     wide = jnp.concatenate([table[:half], table[half:]], axis=1)
@@ -251,10 +257,10 @@
     return jax.ShapeDtypeStruct(dims, kind)
 
 
-def gathered(block, devices):
+def gathered(block, devices, steps):
     step = 1
-    while step < devices:
-        count = min(4, devices // step)
+    while step < steps:
+        count = min(4, steps // step)
         blocks = [block]
         for p in range(1, count):
             pairs = [(i, i ^ (p * step)) for i in range(devices)]
@@ -295,19 +301,28 @@
         out_kind=ANY,
     )(currents)
     mine = lax.all_to_all(packed, "dir", 0, 0, tiled=True)
-    tables = gathered(jnp.transpose(translations, (2, 0, 1)).reshape(-1, parts * ops), devices)
+    tables = gathered(jnp.transpose(translations, (2, 0, 1)).reshape(-1, parts * ops), devices, devices // 2)
     lists = shape(2 * entries + LIST_ROWS, 128, kind=jnp.int32)
     early, late = call(plan_kernel, (lists, lists), (VMEM, VMEM), name="plan")(inter_source.T, inter_shift.T)
     mine, beside, early, late, tables = lax.optimization_barrier((mine, currents, early, late, tables))
     from_cross = lax.ppermute(mine, "slab", cross)
     from_same = lax.ppermute(mine, "slab", same)
+    others = lax.ppermute(tables, "dir", [(i, i ^ (devices // 2)) for i in range(devices)])
+    field = shape(boxes, own, width)
+    up, down = shape(width, 2 * unknowns, kind=BF16), shape(2 * unknowns, width, kind=BF16)
+    radiated, up0, up1, down0, down1 = call(
+        own_kernel, (field, up, up, down, down), (VMEM,) * 3, name="own"
+    )(mine, aggregate, disaggregate)
+    radiated, beside = lax.optimization_barrier((radiated, beside))
     left = lax.ppermute(beside, "dir", ring)
     right = lax.ppermute(beside, "dir", [(j, i) for i, j in ring])
-    field = shape(boxes, own, width)
-    up, down = shape(width, 2 * unknowns, kind=BF16), shape(2 * unknowns, width, kind=BF16)
-    radiated, table, up0, up1, down0, down1 = call(
-        own_kernel, (field, shape(ops, own, width), up, up, down, down), (VMEM,) * 4, name="own"
-    )(mine, tables, aggregate, disaggregate)
+    table = call(
+        table_kernel,
+        shape(ops, own, width),
+        (VMEM, VMEM),
+        scratch=(pltpu.VMEM((width // 2, parts * ops), F32),),
+        name="table",
+    )(tables, others)
     staging = (pltpu.SMEM(lists.shape, jnp.int32), pltpu.SemaphoreType.DMA)
     partial = call(
         mid_kernel,

time: 85 us -> 81.9 us (0.964)
  starting transfers between devices: 35.5 us -> 33.1 us
    ppermute x7 -> x6, waiting for transfers between devices: 14.9 us -> 8.88 us  [gathered(): blocks.append(lax.ppermute(block, 'dir', pairs))]
    ppermute x0 -> x1, waiting for transfers between devices: none -> 4.42 us  [body(): lax.ppermute(tables, 'dir', [(i, i ^ devices // 2) for i in range(devices)])]
    ppermute x7 -> x6, starting transfers between devices: 12.2 us -> 8.22 us  [gathered(): blocks.append(lax.ppermute(block, 'dir', pairs))]
    ppermute x0 -> x1, starting transfers between devices: none -> 2.43 us  [body(): lax.ppermute(tables, 'dir', [(i, i ^ devices // 2) for i in range(devices)])]
    all_to_all x1, starting transfers between devices: 6.93 us -> 5.83 us  [body(): back = lax.all_to_all(far, 'dir', 0, 0, tiled=True)]
    all_to_all x1, waiting for transfers between devices: 0.01 us -> 1.09 us  [body(): mine = lax.all_to_all(packed, 'dir', 0, 0, tiled=True)]
    pallas_call x7 -> x8, Pallas kernels: 22.6 us -> 22.6 us  [run(): pl.pallas_call(kernel, out_shape=outs, in_specs=specs, out_specs=jax.tree...]
  transfers between devices with their start and end apart: 13 -> 13, of which waited for: 6 -> 7; matrix products, arithmetic and copies ran while one was open for 0% -> 0% of each run, Pallas kernels for 23% -> 24%
where the time goes in v8:
time: 81.9 us; the launch traced here: 81.5 us
  starting transfers between devices  33.1 us (40%)
  waiting for transfers between devices  25.5 us (31%)
  Pallas kernels  22.6 us (28%)
    pallas_call x8, Pallas kernels, run(): pl.pallas_call(kernel, out_shape=outs, in_specs=specs, out_specs=jax.tree...  22.6 us
    all_to_all x1, starting transfers between devices, body(): mine = lax.all_to_all(packed, 'dir', 0, 0, tiled=True)  11.6 us
    all_to_all x1, waiting for transfers between devices, body(): back = lax.all_to_all(far, 'dir', 0, 0, tiled=True)  11.1 us
    ppermute x6, waiting for transfers between devices, gathered(): blocks.append(lax.ppermute(block, 'dir', pairs))  8.88 us
    ppermute x6, starting transfers between devices, gathered(): blocks.append(lax.ppermute(block, 'dir', pairs))  8.22 us
    all_to_all x1, starting transfers between devices, body(): back = lax.all_to_all(far, 'dir', 0, 0, tiled=True)  5.83 us
    ppermute x1, waiting for transfers between devices, body(): lax.ppermute(tables, 'dir', [(i, i ^ devices // 2) for i in range(devices)])  4.42 us
    ppermute x1, starting transfers between devices, body(): from_cross = lax.ppermute(mine, 'slab', cross)  2.54 us
  transfers between devices with their start and end apart: 13, of which 7 were waited for; matrix products, arithmetic and copies ran while one was open for 0% of the time, Pallas kernels for 24%

profile of v8, /device:TPU:2, one launch (start us, length us, event | category | flops | bytes accessed | tf_op | source)
XLA Modules:
  0.0 81.5 jit_solution(13981824057426407883)
XLA Ops:
  0.0 2.1 %pack.1 = f32[32,32,128]{2,1,0:T(8,128)} custom-call(f32[2,2,128,256]{3,2,1,0:T(8,128)} %own_ref.1), custom_call_target="tpu_custom_call" | custom-call | flops 1000000000 | bytes 1048576 | tf_op jit(solution)/shard_map/pack/pallas_call | solution.py:242
  2.1 11.6 %all-to-all-start = ((f32[32,32,128]{2,1,0:T(8,128)}), f32[32,32,128]{2,1,0:T(8,128)S(1)}, u32[]{:S(2)}, u32[]{:S(2)}) async-start(f32[32,32,128]{2,1,0:T(8,128)} %pack.1), calls=%async_computation | async-start | bytes 1048576 | tf_op jit(solution)/shard_map/all_to_all | solution.py:303
  13.8 3.0 %collective-permute-start.2 = (f32[8,128]{1,0:T(8,128)S(1)}, f32[8,128]{1,0:T(8,128)S(1)}, u32[]{:S(2)}, u32[]{:S(2)}) collective-permute-start(f32[8,128]{1,0:T(8,128)S(1)} %reshape.3), channel_id=1, source_target_pairs={{0,3},{1,2},{2,1},{3,0},{4,7},{5,6},{6,5},{7,4},{8,11},{9,10},{10,... | collective-permute-start | bytes 12296 | tf_op jit(solution)/shard_map/ppermute | solution.py:267
  16.9 0.9 %collective-permute-start.1 = (f32[8,128]{1,0:T(8,128)S(1)}, f32[8,128]{1,0:T(8,128)S(1)}, u32[]{:S(2)}, u32[]{:S(2)}) collective-permute-start(f32[8,128]{1,0:T(8,128)S(1)} %reshape.3), channel_id=1, source_target_pairs={{0,2},{1,3},{2,0},{3,1},{4,6},{5,7},{6,4},{7,5},{8,10},{9,11},{10,... | collective-permute-start | bytes 12296 | tf_op jit(solution)/shard_map/ppermute | solution.py:267
  17.7 0.2 collective-permute-start
  18.0 3.9 %collective-permute-done = f32[8,128]{1,0:T(8,128)S(1)} collective-permute-done((f32[8,128]{1,0:T(8,128)S(1)}, f32[8,128]{1,0:T(8,128)S(1)}, u32[]{:S(2)}, u32[]{:S(2)}) %collective-permute-start) | collective-permute-done | bytes 4128 | tf_op jit(solution)/shard_map/ppermute | solution.py:267
  22.0 1.5 %collective-permute-start.3 = (f32[32,128]{1,0:T(8,128)S(1)}, f32[32,128]{1,0:T(8,128)S(1)}, u32[]{:S(2)}, u32[]{:S(2)}) collective-permute-start(f32[32,128]{1,0:T(8,128)S(1)} %get-tuple-element.33), channel_id=1, source_target_pairs={{0,4},{1,5},{2,6},{3,7},{4,0},{5,1},{6,2},{7,3},{8,12},{9,13},{10,... | collective-permute-start | bytes 49160 | tf_op jit(solution)/shard_map/ppermute | solution.py:267
  23.5 0.4 plan.1
  24.0 2.5 %collective-permute-start.5 = (f32[32,128]{1,0:T(8,128)S(1)}, f32[32,128]{1,0:T(8,128)S(1)}, u32[]{:S(2)}, u32[]{:S(2)}) collective-permute-start(f32[32,128]{1,0:T(8,128)S(1)} %get-tuple-element.33), channel_id=1, source_target_pairs={{0,12},{1,13},{2,14},{3,15},{4,8},{5,9},{6,10},{7,11},{8,4},{9,5},... | collective-permute-start | bytes 49160 | tf_op jit(solution)/shard_map/ppermute | solution.py:267
  26.5 1.2 %collective-permute-done.3 = f32[32,128]{1,0:T(8,128)S(1)} collective-permute-done((f32[32,128]{1,0:T(8,128)S(1)}, f32[32,128]{1,0:T(8,128)S(1)}, u32[]{:S(2)}, u32[]{:S(2)}) %collective-permute-start.3) | collective-permute-done | bytes 16416 | tf_op jit(solution)/shard_map/ppermute | solution.py:267
  27.7 3.7 %collective-permute-done.4 = f32[32,128]{1,0:T(8,128)S(1)} collective-permute-done((f32[32,128]{1,0:T(8,128)S(1)}, f32[32,128]{1,0:T(8,128)S(1)}, u32[]{:S(2)}, u32[]{:S(2)}) %collective-permute-start.4) | collective-permute-done | bytes 16416 | tf_op jit(solution)/shard_map/ppermute | solution.py:267
  31.4 1.1 %all-to-all-done.own_ref = f32[32,32,128]{2,1,0:T(8,128)S(1)} async-done(((f32[32,32,128]{2,1,0:T(8,128)}), f32[32,32,128]{2,1,0:T(8,128)S(1)}, u32[]{:S(2)}, u32[]{:S(2)}) %all-to-all-start) | async-done | bytes 524320 | tf_op jit(solution)/shard_map/all_to_all | solution.py:303
  32.5 2.5 %collective-permute-start.8 = (f32[32,32,128]{2,1,0:T(8,128)S(1)}, f32[32,32,128]{2,1,0:T(8,128)S(1)}, u32[]{:S(2)}, u32[]{:S(2)}) collective-permute-start(f32[32,32,128]{2,1,0:T(8,128)S(1)} %all-to-all-done.own_ref), channel_id=1, source_target_pairs={{32,64},{96,128},{160,192},{64,32},{128,96},{192,160},{33,65},{97,... | collective-permute-start | bytes 1572872 | tf_op jit(solution)/shard_map/ppermute | solution.py:308
  35.0 2.4 %collective-permute-start.6 = (f32[128,128]{1,0:T(8,128)S(1)}, f32[128,128]{1,0:T(8,128)S(1)}, u32[]{:S(2)}, u32[]{:S(2)}) collective-permute-start(f32[128,128]{1,0:T(8,128)S(1)} %constant_dynamic-update-slice_fusion.4.first_ref), channel_id=1, source_target_pairs={{0,16},{1,17},{2,18},{3,19},{4,20},{5,21},{6,22},{7,23},{8,24},{9,... | collective-permute-start | bytes 196616 | tf_op jit(solution)/shard_map/ppermute | solution.py:310
  37.5 0.7 own.1
  38.2 2.4 %collective-permute-start.10 = (f32[2,2,128,256]{3,2,1,0:T(8,128)}, f32[2,2,128,256]{3,2,1,0:T(8,128)}, u32[]{:S(2)}, u32[]{:S(2)}) collective-permute-start(f32[2,2,128,256]{3,2,1,0:T(8,128)} %own_ref.1), channel_id=1, source_target_pairs={{1,0},{2,1},{3,2},{4,3},{5,4},{6,5},{7,6},{8,7},{9,8},{10,9},{11,1... | collective-permute-start | bytes 1572872 | tf_op jit(solution)/shard_map/ppermute | solution.py:318
  40.6 4.4 %collective-permute-done.6.second_ref = f32[128,128]{1,0:T(8,128)S(1)} collective-permute-done((f32[128,128]{1,0:T(8,128)S(1)}, f32[128,128]{1,0:T(8,128)S(1)}, u32[]{:S(2)}, u32[]{:S(2)}) %collective-permute-start.6) | collective-permute-done | bytes 65568 | tf_op jit(solution)/shard_map/ppermute | solution.py:310
  45.0 0.2 table.1.table_ref
  45.2 5.7 %mid.1.mid_ref = f32[64,8,512]{2,1,0:T(8,128)S(1)} custom-call(s32[72,128]{1,0:T(8,128)S(1)} %get-tuple-element.22.lists_ref, f32[64,8,512]{2,1,0:T(8,128)S(1)} %get-tuple-element.26.own_ref, f32[64,8,512]{2,1,0:T(8,128)S(1)} %table.1.table_ref, f32[32,32,128]{2,1,0:T(8,128)S(1)} %collective-permute-done.7.block_ref, ...), custom_call_target="tpu_custom_call" | custom-call | flops 6000000000 | bytes 4755456 | tf_op jit(solution)/shard_map/mid/pallas_call | solution.py:242
  50.9 5.7 %far.1 = f32[32,32,128]{2,1,0:T(8,128)} custom-call(s32[72,128]{1,0:T(8,128)S(1)} %get-tuple-element.21.lists_ref, f32[64,8,512]{2,1,0:T(8,128)S(1)} %mid.1.mid_ref, f32[64,8,512]{2,1,0:T(8,128)S(1)} %table.1.table_ref, f32[32,32,128]{2,1,0:T(8,128)S(1)} %collective-permute-done.8.block_ref, bf16[512,256]{1,0:T(8,128)(2,1)S(1)} %get-tuple-element.28.up0_ref, ...), custom_call_target="tpu_custom_call" | custom-call | flops 5000000000 | bytes 5279744 | tf_op jit(solution)/shard_map/far/pallas_call | solution.py:242
  56.6 5.8 %all-to-all-start.1 = ((f32[32,32,128]{2,1,0:T(8,128)}), f32[32,32,128]{2,1,0:T(8,128)S(1)}, u32[]{:S(2)}, u32[]{:S(2)}) async-start(f32[32,32,128]{2,1,0:T(8,128)} %far.1), calls=%async_computation.1 | async-start | bytes 1048576 | tf_op jit(solution)/shard_map/all_to_all | solution.py:343
  62.5 7.0 %near.1.near_ref = f32[2,2,128,256]{3,2,1,0:T(8,128)S(1)} custom-call(s32[2,9]{1,0:T(2,128)S(1)} %copy-done.5, f32[2,2,9,128,128]{4,3,2,1,0:T(8,128)S(1)} %copy-done, f32[2,2,128,256]{3,2,1,0:T(8,128)} %own_ref.1, f32[2,2,128,256]{3,2,1,0:T(8,128)} %collective-permute-done.9.left_ref, f32[2,2,128,256]{3,2,1,0:T(8,128)} %collective-permute-done.10.right_ref), custom_call_target="tpu_custom_call" | custom-call | flops 20000000000 | bytes 4456520 | tf_op jit(solution)/shard_map/near/pallas_call | solution.py:242
  69.5 11.1 %all-to-all-done.1.far_ref = f32[32,32,128]{2,1,0:T(8,128)S(1)} async-done(((f32[32,32,128]{2,1,0:T(8,128)}), f32[32,32,128]{2,1,0:T(8,128)S(1)}, u32[]{:S(2)}, u32[]{:S(2)}) %all-to-all-start.1) | async-done | bytes 524320 | tf_op jit(solution)/shard_map/all_to_all | solution.py:343
  80.6 0.9 %join.1 = f32[2,2,128,256]{3,2,1,0:T(8,128)} custom-call(f32[32,32,128]{2,1,0:T(8,128)S(1)} %all-to-all-done.1.far_ref, f32[2,2,128,256]{3,2,1,0:T(8,128)S(1)} %near.1.near_ref), custom_call_target="tpu_custom_call" | custom-call | bytes 1572864 | tf_op jit(solution)/shard_map/join/pallas_call | solution.py:242
  (33 shorter events, 0.3 us)
Async XLA Ops:
  0.0 13.7 %copy-start.6 = (f32[2,64,8]{1,2,0:T(8,128)S(1)}, f32[2,64,8]{1,2,0:T(8,128)}, u32[]{:S(2)}) copy-start(f32[2,64,8]{1,2,0:T(8,128)} %param.12) | copy-start | bytes 12292
  0.0 23.5 %copy-start.4 = (s32[64,32]{0,1:T(8,128)S(1)}, s32[64,32]{0,1:T(8,128)}, u32[]{:S(2)}) copy-start(s32[64,32]{0,1:T(8,128)} %param.14) | copy-start | bytes 24580
  0.0 23.5 %copy-start.3 = (s32[64,32]{0,1:T(8,128)S(1)}, s32[64,32]{0,1:T(8,128)}, u32[]{:S(2)}) copy-start(s32[64,32]{0,1:T(8,128)} %param.13) | copy-start | bytes 24580
  2.1 35.4 %copy-start.1 = (f32[2,256,128]{2,1,0:T(8,128)S(1)}, f32[2,256,128]{2,1,0:T(8,128)}, u32[]{:S(2)}) copy-start(f32[2,256,128]{2,1,0:T(8,128)} %aggregate_ref.1) | copy-start | bytes 786436
  2.1 35.4 %copy-start.2 = (f32[2,128,256]{2,1,0:T(8,128)S(1)}, f32[2,128,256]{2,1,0:T(8,128)}, u32[]{:S(2)}) copy-start(f32[2,128,256]{2,1,0:T(8,128)} %disaggregate_ref.1) | copy-start | bytes 786436
  2.1 30.4 %all-to-all-start = ((f32[32,32,128]{2,1,0:T(8,128)}), f32[32,32,128]{2,1,0:T(8,128)S(1)}, u32[]{:S(2)}, u32[]{:S(2)}) async-start(f32[32,32,128]{2,1,0:T(8,128)} %pack.1), calls=%async_computation | async-start | bytes 1048576 | tf_op jit(solution)/shard_map/all_to_all | solution.py:303
  13.8 8.1 %collective-permute-start.2 = (f32[8,128]{1,0:T(8,128)S(1)}, f32[8,128]{1,0:T(8,128)S(1)}, u32[]{:S(2)}, u32[]{:S(2)}) collective-permute-start(f32[8,128]{1,0:T(8,128)S(1)} %reshape.3), channel_id=1, source_target_pairs={{0,3},{1,2},{2,1},{3,0},{4,7},{5,6},{6,5},{7,4},{8,11},{9,10},{10,... | collective-permute-start | bytes 12296 | tf_op jit(solution)/shard_map/ppermute | solution.py:267
  16.9 5.1 %collective-permute-start.1 = (f32[8,128]{1,0:T(8,128)S(1)}, f32[8,128]{1,0:T(8,128)S(1)}, u32[]{:S(2)}, u32[]{:S(2)}) collective-permute-start(f32[8,128]{1,0:T(8,128)S(1)} %reshape.3), channel_id=1, source_target_pairs={{0,2},{1,3},{2,0},{3,1},{4,6},{5,7},{6,4},{7,5},{8,10},{9,11},{10,... | collective-permute-start | bytes 12296 | tf_op jit(solution)/shard_map/ppermute | solution.py:267
  17.7 4.2 %collective-permute-start = (f32[8,128]{1,0:T(8,128)S(1)}, f32[8,128]{1,0:T(8,128)S(1)}, u32[]{:S(2)}, u32[]{:S(2)}) collective-permute-start(f32[8,128]{1,0:T(8,128)S(1)} %reshape.3), channel_id=1, source_target_pairs={{0,1},{1,0},{2,3},{3,2},{4,5},{5,4},{6,7},{7,6},{8,9},{9,8},{10,11... | collective-permute-start | bytes 12296 | tf_op jit(solution)/shard_map/ppermute | solution.py:267
  22.0 5.7 %collective-permute-start.3 = (f32[32,128]{1,0:T(8,128)S(1)}, f32[32,128]{1,0:T(8,128)S(1)}, u32[]{:S(2)}, u32[]{:S(2)}) collective-permute-start(f32[32,128]{1,0:T(8,128)S(1)} %get-tuple-element.33), channel_id=1, source_target_pairs={{0,4},{1,5},{2,6},{3,7},{4,0},{5,1},{6,2},{7,3},{8,12},{9,13},{10,... | collective-permute-start | bytes 49160 | tf_op jit(solution)/shard_map/ppermute | solution.py:267
  24.0 7.4 %collective-permute-start.5 = (f32[32,128]{1,0:T(8,128)S(1)}, f32[32,128]{1,0:T(8,128)S(1)}, u32[]{:S(2)}, u32[]{:S(2)}) collective-permute-start(f32[32,128]{1,0:T(8,128)S(1)} %get-tuple-element.33), channel_id=1, source_target_pairs={{0,12},{1,13},{2,14},{3,15},{4,8},{5,9},{6,10},{7,11},{8,4},{9,5},... | collective-permute-start | bytes 49160 | tf_op jit(solution)/shard_map/ppermute | solution.py:267
  26.4 5.0 %collective-permute-start.4 = (f32[32,128]{1,0:T(8,128)S(1)}, f32[32,128]{1,0:T(8,128)S(1)}, u32[]{:S(2)}, u32[]{:S(2)}) collective-permute-start(f32[32,128]{1,0:T(8,128)S(1)} %get-tuple-element.33), channel_id=1, source_target_pairs={{0,8},{1,9},{2,10},{3,11},{4,12},{5,13},{6,14},{7,15},{8,0},{9,1},... | collective-permute-start | bytes 49160 | tf_op jit(solution)/shard_map/ppermute | solution.py:267
  32.5 12.7 %collective-permute-start.7 = (f32[32,32,128]{2,1,0:T(8,128)S(1)}, f32[32,32,128]{2,1,0:T(8,128)S(1)}, u32[]{:S(2)}, u32[]{:S(2)}) collective-permute-start(f32[32,32,128]{2,1,0:T(8,128)S(1)} %all-to-all-done.own_ref), channel_id=1, source_target_pairs={{0,32},{64,96},{128,160},{192,224},{32,0},{96,64},{160,128},{224,1... | collective-permute-start | bytes 1572872 | tf_op jit(solution)/shard_map/ppermute | solution.py:309
  32.5 18.4 %collective-permute-start.8 = (f32[32,32,128]{2,1,0:T(8,128)S(1)}, f32[32,32,128]{2,1,0:T(8,128)S(1)}, u32[]{:S(2)}, u32[]{:S(2)}) collective-permute-start(f32[32,32,128]{2,1,0:T(8,128)S(1)} %all-to-all-done.own_ref), channel_id=1, source_target_pairs={{32,64},{96,128},{160,192},{64,32},{128,96},{192,160},{33,65},{97,... | collective-permute-start | bytes 1572872 | tf_op jit(solution)/shard_map/ppermute | solution.py:308
  35.0 10.0 %collective-permute-start.6 = (f32[128,128]{1,0:T(8,128)S(1)}, f32[128,128]{1,0:T(8,128)S(1)}, u32[]{:S(2)}, u32[]{:S(2)}) collective-permute-start(f32[128,128]{1,0:T(8,128)S(1)} %constant_dynamic-update-slice_fusion.4.first_ref), channel_id=1, source_target_pairs={{0,16},{1,17},{2,18},{3,19},{4,20},{5,21},{6,22},{7,23},{8,24},{9,... | collective-permute-start | bytes 196616 | tf_op jit(solution)/shard_map/ppermute | solution.py:310
  38.2 24.3 %collective-permute-start.10 = (f32[2,2,128,256]{3,2,1,0:T(8,128)}, f32[2,2,128,256]{3,2,1,0:T(8,128)}, u32[]{:S(2)}, u32[]{:S(2)}) collective-permute-start(f32[2,2,128,256]{3,2,1,0:T(8,128)} %own_ref.1), channel_id=1, source_target_pairs={{1,0},{2,1},{3,2},{4,3},{5,4},{6,5},{7,6},{8,7},{9,8},{10,9},{11,1... | collective-permute-start | bytes 1572872 | tf_op jit(solution)/shard_map/ppermute | solution.py:318
  40.6 21.9 %collective-permute-start.9 = (f32[2,2,128,256]{3,2,1,0:T(8,128)}, f32[2,2,128,256]{3,2,1,0:T(8,128)}, u32[]{:S(2)}, u32[]{:S(2)}) collective-permute-start(f32[2,2,128,256]{3,2,1,0:T(8,128)} %own_ref.1), channel_id=1, source_target_pairs={{0,1},{1,2},{2,3},{3,4},{4,5},{5,6},{6,7},{7,8},{8,9},{9,10},{10,1... | collective-permute-start | bytes 1572872 | tf_op jit(solution)/shard_map/ppermute | solution.py:317
  50.9 11.6 %copy-start = (f32[2,2,9,128,128]{4,3,2,1,0:T(8,128)S(1)}, f32[2,2,9,128,128]{4,3,2,1,0:T(8,128)}, u32[]{:S(2)}) copy-start(f32[2,2,9,128,128]{4,3,2,1,0:T(8,128)} %blocks_ref.1) | copy-start | bytes 7077892
  50.9 11.6 %copy-start.5 = (s32[2,9]{1,0:T(2,128)S(1)}, s32[2,9]{1,0:T(2,128)}, u32[]{:S(2)}) copy-start(s32[2,9]{1,0:T(2,128)} %index_ref.1) | copy-start | bytes 220
  56.6 23.9 %all-to-all-start.1 = ((f32[32,32,128]{2,1,0:T(8,128)}), f32[32,32,128]{2,1,0:T(8,128)S(1)}, u32[]{:S(2)}, u32[]{:S(2)}) async-start(f32[32,32,128]{2,1,0:T(8,128)} %far.1), calls=%async_computation.1 | async-start | bytes 1048576 | tf_op jit(solution)/shard_map/all_to_all | solution.py:343

commit v9 on v6

--- a/solution.py
+++ b/solution.py
@@ -13,7 +13,7 @@
 ANY = pl.ANY
 MIB = 1 << 20
 RE_IM_ROWS = 32
-EARLY, LATE = 25, 15
+FIRST = 16
 LIST_ROWS = 8
 FULL = 63
 
@@ -32,6 +32,45 @@
 
 NN_FORM = ((1,), (0,))
 NT_FORM = ((1,), (1,))
+
+
+def plan_kernel(source_ref, shift_ref, early_ref, late_ref):
+    entries, boxes = source_ref.shape
+    odd = lax.axis_index("slab") % 2
+    source, shift = source_ref[...], shift_ref[...]
+    part, place = source // boxes, source % boxes
+    away = part == 2 * odd
+    where = jnp.where(part == 1, place, jnp.where(away, 2 * boxes + place, boxes + place))
+    one = jnp.where(away, 0, 1)
+    near_count = jnp.sum(one, axis=0, keepdims=True)
+    row = lax.broadcasted_iota(jnp.int32, (entries, boxes), 0)
+    to_near, to_away = jnp.zeros((1, boxes), jnp.int32), near_count
+    sorted_where = jnp.zeros((entries, boxes), jnp.int32)
+    sorted_shift = jnp.zeros((entries, boxes), jnp.int32)
+    for i in range(entries):
+        is_near = one[i : i + 1]
+        here = row == jnp.where(is_near == 1, to_near, to_away)
+        sorted_where = jnp.where(here, where[i : i + 1], sorted_where)
+        sorted_shift = jnp.where(here, shift[i : i + 1], sorted_shift)
+        to_near, to_away = to_near + is_near, to_away + (1 - is_near)
+    for ref in (early_ref, late_ref):
+        ref[...] = jnp.zeros(ref.shape, jnp.int32)
+        ref[entries : 2 * entries, :boxes] = sorted_shift
+    early_ref[:entries, :boxes] = jnp.minimum(sorted_where, 2 * boxes)
+    late_ref[:entries, :boxes] = sorted_where
+    late_ref[2 * entries : 2 * entries + 1, :boxes] = near_count
+    across = [lax.broadcasted_iota(jnp.int32, (boxes, boxes), n) for n in range(2)]
+    before, same = (across[1] < across[0]).astype(F32), (across[1] == across[0]).astype(F32)
+    lanes = late_ref.shape[1]
+    slot = lax.broadcasted_iota(jnp.int32, (boxes, lanes), 1).astype(F32)
+    box = lax.broadcasted_iota(jnp.int32, (boxes, lanes), 0).astype(F32)
+    few = jnp.broadcast_to((near_count < FIRST).astype(F32), (8, boxes))
+    rank = lax.dot_general(before, few, (NT_FORM, ((), ())), preferred_element_type=F32)[:, :1]
+    flag = lax.dot_general(same, few, (NT_FORM, ((), ())), preferred_element_type=F32)[:, :1]
+    listed = jnp.sum(jnp.where((slot == rank) & (flag > 0.5), box, 0.0), axis=0, keepdims=True)
+    late_ref[2 * entries + 1 : 2 * entries + 2, :] = listed.astype(jnp.int32)
+    total = jnp.sum(few, axis=1, keepdims=True)[:1]
+    late_ref[2 * entries + 2 : 2 * entries + 3, :] = jnp.broadcast_to(total, (1, lanes)).astype(jnp.int32)
 
 
 def pack_kernel(currents_ref, translations_ref, out_ref, block_ref, table_ref, packed_ref, in_sem, out_sem):
@@ -98,43 +137,6 @@
     )
 
 
-def plan_kernel(source_ref, shift_ref, early_ref, late_ref):
-    entries, boxes = source_ref.shape
-    odd = lax.axis_index("slab") % 2
-    source, shift = source_ref[...], shift_ref[...]
-    part, place = source // boxes, source % boxes
-    away = part == 2 * odd
-    row = lax.broadcasted_iota(jnp.int32, (entries, boxes), 0)
-    across = [lax.broadcasted_iota(jnp.int32, (boxes, boxes), n) for n in range(2)]
-    before, same = (across[1] < across[0]).astype(F32), (across[1] == across[0]).astype(F32)
-    slot = lax.broadcasted_iota(jnp.int32, (boxes, early_ref.shape[1]), 1).astype(F32)
-    for ref, fixed, chosen, where, zeros in (
-        (early_ref, EARLY, jnp.logical_not(away), jnp.where(part == 1, place, boxes + place), 2 * boxes),
-        (late_ref, LATE, away, place, boxes),
-    ):
-        one = chosen.astype(jnp.int32)
-        count = jnp.zeros((1, boxes), jnp.int32)
-        front_where = jnp.full((entries, boxes), zeros, jnp.int32)
-        front_shift = jnp.zeros((entries, boxes), jnp.int32)
-        for i in range(entries):
-            here = (row == count) & (one[i : i + 1] == 1)
-            front_where = jnp.where(here, where[i : i + 1], front_where)
-            front_shift = jnp.where(here, shift[i : i + 1], front_shift)
-            count = count + one[i : i + 1]
-        ref[...] = jnp.zeros(ref.shape, jnp.int32)
-        ref[:entries, :boxes] = front_where
-        ref[entries : 2 * entries, :boxes] = front_shift
-        ref[2 * entries : 2 * entries + 1, :boxes] = count
-        more = jnp.broadcast_to((count > fixed).astype(F32), (8, boxes))
-        rank = lax.dot_general(before, more, (NT_FORM, ((), ())), preferred_element_type=F32)[:, :1]
-        flag = lax.dot_general(same, more, (NT_FORM, ((), ())), preferred_element_type=F32)[:, :1]
-        box = lax.broadcasted_iota(jnp.int32, slot.shape, 0).astype(F32)
-        chosen_box = jnp.where((slot == rank) & (flag > 0.5), box, 0.0)
-        ref[2 * entries + 1 : 2 * entries + 2, :] = jnp.sum(chosen_box, axis=0, keepdims=True).astype(jnp.int32)
-        total = jnp.sum(more, axis=1, keepdims=True)[:1]
-        ref[2 * entries + 2 : 2 * entries + 3, :] = jnp.broadcast_to(total, (1, ref.shape[1])).astype(jnp.int32)
-
-
 def own_kernel(own_ref, aggregate_ref, disaggregate_ref, radiated_ref, table_ref, up0_ref, up1_ref, down0_ref, down1_ref):
     boxes, sub, width = radiated_ref.shape
     up = split(complex_rows(aggregate_ref))
@@ -160,27 +162,15 @@
     return real, imag
 
 
-def add_all(list_ref, fixed, start, out_ref, radiated_ref, table_ref):
-    entries = list_ref.shape[0] // 2 - LIST_ROWS // 2
+def add_all(list_ref, numbers, start, out_ref, radiated_ref, table_ref):
     half = table_ref.shape[2] // 2
 
     def one_box(g, carry):
-        total = add_entries(list_ref, g, range(fixed), start(g), radiated_ref, table_ref)
+        total = add_entries(list_ref, g, numbers, start(g), radiated_ref, table_ref)
         out_ref[g, :, :half], out_ref[g, :, half:] = total
         return carry
 
-    def beyond(place, carry):
-        g = list_ref[2 * entries + 1, place]
-
-        def rest(n, total):
-            return add_entries(list_ref, g, (n,), total, radiated_ref, table_ref)
-
-        both = lax.fori_loop(fixed, list_ref[2 * entries, g], rest, (out_ref[g, :, :half], out_ref[g, :, half:]))
-        out_ref[g, :, :half], out_ref[g, :, half:] = both
-        return carry
-
     lax.fori_loop(0, out_ref.shape[0], one_box, 0, unroll=4)
-    lax.fori_loop(0, list_ref[2 * entries + 2, 0], beyond, 0)
 
 
 def mid_kernel(
@@ -194,23 +184,38 @@
     radiated_ref[2 * boxes] = jnp.zeros((sub, width), F32)
     staged.wait()
     nothing = jnp.zeros((sub, width // 2), F32)
-    add_all(list_ref, EARLY, lambda g: (nothing, nothing), out_ref, radiated_ref, table_ref)
+    add_all(list_ref, range(FIRST), lambda g: (nothing, nothing), out_ref, radiated_ref, table_ref)
 
 
 def far_kernel(
-    lists_ref, mid_ref, table_ref, block_ref, up0_ref, up1_ref, down0_ref, down1_ref, out_ref, radiated_ref,
+    lists_ref, mid_ref, near_ref, table_ref, block_ref, up0_ref, up1_ref, down0_ref, down1_ref, out_ref, radiated_ref,
     incoming_ref, list_ref, sem,
 ):
     staged = pltpu.make_async_copy(lists_ref, list_ref, sem)
     staged.start()
     boxes, sub, width = mid_ref.shape
     half = width // 2
-    radiated_ref[:boxes] = radiate(block_ref, (up0_ref[...], up1_ref[...])).reshape(boxes, sub, width)
-    radiated_ref[boxes] = jnp.zeros((sub, width), F32)
+    entries = list_ref.shape[0] // 2 - LIST_ROWS // 2
+    radiated_ref[: 2 * boxes] = near_ref[: 2 * boxes]
+    radiated_ref[2 * boxes :] = radiate(block_ref, (up0_ref[...], up1_ref[...])).reshape(boxes, sub, width)
     staged.wait()
+    rest = range(FIRST, entries)
     add_all(
-        list_ref, LATE, lambda g: (mid_ref[g, :, :half], mid_ref[g, :, half:]), incoming_ref, radiated_ref, table_ref
+        list_ref, rest, lambda g: (mid_ref[g, :, :half], mid_ref[g, :, half:]), incoming_ref, radiated_ref, table_ref
     )
+
+    def skipped(place, carry):
+        g = list_ref[2 * entries + 1, place]
+
+        def one(n, total):
+            return add_entries(list_ref, g, (n,), total, radiated_ref, table_ref)
+
+        both = (incoming_ref[g, :, :half], incoming_ref[g, :, half:])
+        both = lax.fori_loop(list_ref[2 * entries, g], FIRST, one, both)
+        incoming_ref[g, :, :half], incoming_ref[g, :, half:] = both
+        return carry
+
+    lax.fori_loop(0, list_ref[2 * entries + 2, 0], skipped, 0)
     far = dot3(split(incoming_ref[...].reshape(boxes * sub, width)), (down0_ref[...], down1_ref[...]), NT_FORM)
     devices, rows, lanes = out_ref.shape
     out_ref[:, : rows // 2, :] = far[:, :lanes].reshape(devices, rows // 2, lanes)
@@ -300,22 +305,22 @@
         own_kernel, (field, shape(ops, own, width), up, up, down, down), (VMEM,) * 3, name="own"
     )(mine, aggregate, disaggregate)
     staging = (pltpu.SMEM(lists.shape, jnp.int32), pltpu.SemaphoreType.DMA)
-    partial = call(
+    partial, near_fields = call(
         mid_kernel,
-        field,
+        (field, shape(2 * boxes + 1, own, width)),
         (VMEM,) * 6,
-        scratch=(pltpu.VMEM((2 * boxes + 1, own, width), F32), *staging),
+        scratch=staging,
         micros=6,
         name="mid",
     )(early, radiated, table, from_same, up0, up1)
     far = call(
         far_kernel,
         shape(devices, rows, unknowns),
-        (VMEM,) * 8,
-        scratch=(pltpu.VMEM((boxes + 1, own, width), F32), pltpu.VMEM((boxes, own, width), F32), *staging),
+        (VMEM,) * 9,
+        scratch=(pltpu.VMEM((3 * boxes, own, width), F32), pltpu.VMEM((boxes, own, width), F32), *staging),
         micros=5,
         name="far",
-    )(late, partial, table, from_cross, up0, up1, down0, down1)
+    )(late, partial, near_fields, table, from_cross, up0, up1, down0, down1)
     back = lax.all_to_all(far, "dir", 0, 0, tiled=True)
 
     stack = pltpu.VMEM((3 * box_dev, 2 * unknowns, 2 * illum), BF16)

time: 77.8 us -> 76.5 us (0.983)
  Pallas kernels: 22.6 us -> 21.4 us
    pallas_call x7, Pallas kernels: 22.6 us -> 21.4 us  [run(): pl.pallas_call(kernel, out_shape=outs, in_specs=specs, out_specs=jax.tree...]
  transfers between devices with their start and end apart: 6 -> 6, of which waited for: 2 -> 2; matrix products, arithmetic and copies ran while one was open for 0% -> 0% of each run, Pallas kernels for 25% -> 24%
where the time goes in v9:
time: 76.5 us; the launch traced here: 76.3 us
  waiting for transfers between devices  31.2 us (41%)
  starting transfers between devices  23.5 us (31%)
  Pallas kernels  21.4 us (28%)
    pallas_call x7, Pallas kernels, run(): pl.pallas_call(kernel, out_shape=outs, in_specs=specs, out_specs=jax.tree...  21.4 us
    all_to_all x1, waiting for transfers between devices, body(): mine = lax.all_to_all(packed, 'dir', 0, 0, tiled=True)  19.8 us
    all_to_all x1, starting transfers between devices, body(): mine = lax.all_to_all(packed, 'dir', 0, 0, tiled=True)  11.5 us
    all_to_all x1, waiting for transfers between devices, body(): back = lax.all_to_all(far, 'dir', 0, 0, tiled=True)  11.4 us
    ppermute x1, starting transfers between devices, body(): right = lax.ppermute(beside, 'dir', [(j, i) for i, j in ring])  4.12 us
    all_to_all x1, starting transfers between devices, body(): back = lax.all_to_all(far, 'dir', 0, 0, tiled=True)  3.9 us
    ppermute x1, starting transfers between devices, body(): from_cross = lax.ppermute(sent, 'slab', cross)  2.53 us
  transfers between devices with their start and end apart: 6, of which 2 were waited for; matrix products, arithmetic and copies ran while one was open for 0% of the time, Pallas kernels for 24%

profile of v9, /device:TPU:2, one launch (start us, length us, event | category | flops | bytes accessed | tf_op | source)
XLA Modules:
  0.0 76.3 jit_solution(16236620894702945015)
XLA Ops:
  0.0 2.2 %pack.1 = f32[32,40,128]{2,1,0:T(8,128)} custom-call(f32[2,2,128,256]{3,2,1,0:T(8,128)} %own_ref.1, f32[2,8,64]{2,1,0:T(8,128)} %bitcast.5), custom_call_target="tpu_custom_call" | custom-call | flops 1000000000 | bytes 1183744 | tf_op jit(solution)/shard_map/pack/pallas_call | solution.py:243
  2.2 11.5 %all-to-all-start = ((f32[32,40,128]{2,1,0:T(8,128)}), f32[32,40,128]{2,1,0:T(8,128)S(1)}, u32[]{:S(2)}, u32[]{:S(2)}) async-start(f32[32,40,128]{2,1,0:T(8,128)} %pack.1), calls=%async_computation | async-start | bytes 1310720 | tf_op jit(solution)/shard_map/all_to_all | solution.py:293
  13.7 0.0 copy-start.1
  13.7 0.0 copy-start.2
  13.7 0.3 plan.1
  14.1 19.8 %all-to-all-done.own_ref = f32[32,40,128]{2,1,0:T(8,128)S(1)} async-done(((f32[32,40,128]{2,1,0:T(8,128)}), f32[32,40,128]{2,1,0:T(8,128)S(1)}, u32[]{:S(2)}, u32[]{:S(2)}) %all-to-all-start) | async-done | bytes 655392 | tf_op jit(solution)/shard_map/all_to_all | solution.py:293
  33.9 0.1 slice.3
  34.0 0.1 collective-permute-start
  34.1 2.5 %collective-permute-start.1 = (f32[32,32,128]{2,1,0:T(8,128)S(1)}, f32[32,32,128]{2,1,0:T(8,128)S(1)}, u32[]{:S(2)}, u32[]{:S(2)}) collective-permute-start(f32[32,32,128]{2,1,0:T(8,128)S(1)} %slice.3), channel_id=1, source_target_pairs={{32,64},{96,128},{160,192},{64,32},{128,96},{192,160},{33,65},{97,... | collective-permute-start | bytes 1572872 | tf_op jit(solution)/shard_map/ppermute | solution.py:298
  36.6 1.3 %collective-permute-start.2 = (f32[2,2,128,256]{3,2,1,0:T(8,128)}, f32[2,2,128,256]{3,2,1,0:T(8,128)}, u32[]{:S(2)}, u32[]{:S(2)}) collective-permute-start(f32[2,2,128,256]{3,2,1,0:T(8,128)} %own_ref.1), channel_id=1, source_target_pairs={{0,1},{1,2},{2,3},{3,4},{4,5},{5,6},{6,7},{7,8},{8,9},{9,10},{10,1... | collective-permute-start | bytes 1572872 | tf_op jit(solution)/shard_map/ppermute | solution.py:300
  37.9 4.1 %collective-permute-start.3 = (f32[2,2,128,256]{3,2,1,0:T(8,128)}, f32[2,2,128,256]{3,2,1,0:T(8,128)}, u32[]{:S(2)}, u32[]{:S(2)}) collective-permute-start(f32[2,2,128,256]{3,2,1,0:T(8,128)} %own_ref.1), channel_id=1, source_target_pairs={{1,0},{2,1},{3,2},{4,3},{5,4},{6,5},{7,6},{8,7},{9,8},{10,9},{11,1... | collective-permute-start | bytes 1572872 | tf_op jit(solution)/shard_map/ppermute | solution.py:301
  42.0 0.8 own.1
  42.8 0.0 collective-permute-done.block_ref
  42.8 4.0 %mid.1 = (f32[64,8,512]{2,1,0:T(8,128)S(1)}, f32[129,8,512]{2,1,0:T(8,128)S(1)}) custom-call(s32[72,128]{1,0:T(8,128)S(1)} %get-tuple-element.22.lists_ref, f32[64,8,512]{2,1,0:T(8,128)S(1)} %get-tuple-element.24.own_ref, f32[64,8,512]{2,1,0:T(8,128)S(1)} %get-tuple-element.25.table_ref, f32[32,32,128]{2,1,0:T(8,128)S(1)} %collective-permute-done.block_ref, ...), custom_call_target="tpu_custom_call" | custom-call | flops 6000000000 | bytes 6868992 | tf_op jit(solution)/shard_map/mid/pallas_call | solution.py:243
  46.8 0.0 collective-permute-done.1.block_ref
  46.8 0.0 copy-start
  46.8 0.0 copy-start.5
  46.8 6.1 %far.1 = f32[32,32,128]{2,1,0:T(8,128)} custom-call(s32[72,128]{1,0:T(8,128)S(1)} %get-tuple-element.21.lists_ref, f32[64,8,512]{2,1,0:T(8,128)S(1)} %get-tuple-element.28.mid_ref, f32[129,8,512]{2,1,0:T(8,128)S(1)} %get-tuple-element.29.near_ref, f32[64,8,512]{2,1,0:T(8,128)S(1)} %get-tuple-element.25.table_ref, ...), custom_call_target="tpu_custom_call" | custom-call | flops 5000000000 | bytes 7393280 | tf_op jit(solution)/shard_map/far/pallas_call | solution.py:243
  53.0 3.9 %all-to-all-start.1 = ((f32[32,32,128]{2,1,0:T(8,128)}), f32[32,32,128]{2,1,0:T(8,128)S(1)}, u32[]{:S(2)}, u32[]{:S(2)}) async-start(f32[32,32,128]{2,1,0:T(8,128)} %far.1), calls=%async_computation.1 | async-start | bytes 1048576 | tf_op jit(solution)/shard_map/all_to_all | solution.py:324
  56.9 0.0 collective-permute-done.2.left_ref
  56.9 0.0 collective-permute-done.3.right_ref
  56.9 7.0 %near.1.near_ref = f32[2,2,128,256]{3,2,1,0:T(8,128)S(1)} custom-call(s32[2,9]{1,0:T(2,128)S(1)} %copy-done.5, f32[2,2,9,128,128]{4,3,2,1,0:T(8,128)S(1)} %copy-done, f32[2,2,128,256]{3,2,1,0:T(8,128)} %own_ref.1, f32[2,2,128,256]{3,2,1,0:T(8,128)} %collective-permute-done.2.left_ref, f32[2,2,128,256]{3,2,1,0:T(8,128)} %collective-permute-done.3.right_ref), custom_call_target="tpu_custom_call" | custom-call | flops 20000000000 | bytes 4456520 | tf_op jit(solution)/shard_map/near/pallas_call | solution.py:243
  64.0 11.4 %all-to-all-done.1.far_ref = f32[32,32,128]{2,1,0:T(8,128)S(1)} async-done(((f32[32,32,128]{2,1,0:T(8,128)}), f32[32,32,128]{2,1,0:T(8,128)S(1)}, u32[]{:S(2)}, u32[]{:S(2)}) %all-to-all-start.1) | async-done | bytes 524320 | tf_op jit(solution)/shard_map/all_to_all | solution.py:324
  75.4 0.9 %join.1 = f32[2,2,128,256]{3,2,1,0:T(8,128)} custom-call(f32[32,32,128]{2,1,0:T(8,128)S(1)} %all-to-all-done.1.far_ref, f32[2,2,128,256]{3,2,1,0:T(8,128)S(1)} %near.1.near_ref), custom_call_target="tpu_custom_call" | custom-call | bytes 1572864 | tf_op jit(solution)/shard_map/join/pallas_call | solution.py:243
  (8 shorter events, 0.0 us)
Async XLA Ops:
  0.0 13.7 %copy-start.3 = (s32[64,32]{0,1:T(8,128)S(1)}, s32[64,32]{0,1:T(8,128)}, u32[]{:S(2)}) copy-start(s32[64,32]{0,1:T(8,128)} %param.13) | copy-start | bytes 24580
  0.0 13.7 %copy-start.4 = (s32[64,32]{0,1:T(8,128)S(1)}, s32[64,32]{0,1:T(8,128)}, u32[]{:S(2)}) copy-start(s32[64,32]{0,1:T(8,128)} %param.14) | copy-start | bytes 24580
  2.2 31.7 %all-to-all-start = ((f32[32,40,128]{2,1,0:T(8,128)}), f32[32,40,128]{2,1,0:T(8,128)S(1)}, u32[]{:S(2)}, u32[]{:S(2)}) async-start(f32[32,40,128]{2,1,0:T(8,128)} %pack.1), calls=%async_computation | async-start | bytes 1310720 | tf_op jit(solution)/shard_map/all_to_all | solution.py:293
  13.7 28.3 %copy-start.1 = (f32[2,256,128]{2,1,0:T(8,128)S(1)}, f32[2,256,128]{2,1,0:T(8,128)}, u32[]{:S(2)}) copy-start(f32[2,256,128]{2,1,0:T(8,128)} %aggregate_ref.1) | copy-start | bytes 786436
  13.7 28.3 %copy-start.2 = (f32[2,128,256]{2,1,0:T(8,128)S(1)}, f32[2,128,256]{2,1,0:T(8,128)}, u32[]{:S(2)}) copy-start(f32[2,128,256]{2,1,0:T(8,128)} %disaggregate_ref.1) | copy-start | bytes 786436
  34.0 8.8 %collective-permute-start = (f32[32,32,128]{2,1,0:T(8,128)S(1)}, f32[32,32,128]{2,1,0:T(8,128)S(1)}, u32[]{:S(2)}, u32[]{:S(2)}) collective-permute-start(f32[32,32,128]{2,1,0:T(8,128)S(1)} %slice.3), channel_id=1, source_target_pairs={{0,32},{64,96},{128,160},{192,224},{32,0},{96,64},{160,128},{224,1... | collective-permute-start | bytes 1572872 | tf_op jit(solution)/shard_map/ppermute | solution.py:299
  34.1 12.8 %collective-permute-start.1 = (f32[32,32,128]{2,1,0:T(8,128)S(1)}, f32[32,32,128]{2,1,0:T(8,128)S(1)}, u32[]{:S(2)}, u32[]{:S(2)}) collective-permute-start(f32[32,32,128]{2,1,0:T(8,128)S(1)} %slice.3), channel_id=1, source_target_pairs={{32,64},{96,128},{160,192},{64,32},{128,96},{192,160},{33,65},{97,... | collective-permute-start | bytes 1572872 | tf_op jit(solution)/shard_map/ppermute | solution.py:298
  36.6 20.3 %collective-permute-start.2 = (f32[2,2,128,256]{3,2,1,0:T(8,128)}, f32[2,2,128,256]{3,2,1,0:T(8,128)}, u32[]{:S(2)}, u32[]{:S(2)}) collective-permute-start(f32[2,2,128,256]{3,2,1,0:T(8,128)} %own_ref.1), channel_id=1, source_target_pairs={{0,1},{1,2},{2,3},{3,4},{4,5},{5,6},{6,7},{7,8},{8,9},{9,10},{10,1... | collective-permute-start | bytes 1572872 | tf_op jit(solution)/shard_map/ppermute | solution.py:300
  37.9 19.0 %collective-permute-start.3 = (f32[2,2,128,256]{3,2,1,0:T(8,128)}, f32[2,2,128,256]{3,2,1,0:T(8,128)}, u32[]{:S(2)}, u32[]{:S(2)}) collective-permute-start(f32[2,2,128,256]{3,2,1,0:T(8,128)} %own_ref.1), channel_id=1, source_target_pairs={{1,0},{2,1},{3,2},{4,3},{5,4},{6,5},{7,6},{8,7},{9,8},{10,9},{11,1... | collective-permute-start | bytes 1572872 | tf_op jit(solution)/shard_map/ppermute | solution.py:301
  46.8 10.1 %copy-start = (f32[2,2,9,128,128]{4,3,2,1,0:T(8,128)S(1)}, f32[2,2,9,128,128]{4,3,2,1,0:T(8,128)}, u32[]{:S(2)}) copy-start(f32[2,2,9,128,128]{4,3,2,1,0:T(8,128)} %blocks_ref.1) | copy-start | bytes 7077892
  46.8 10.1 %copy-start.5 = (s32[2,9]{1,0:T(2,128)S(1)}, s32[2,9]{1,0:T(2,128)}, u32[]{:S(2)}) copy-start(s32[2,9]{1,0:T(2,128)} %index_ref.1) | copy-start | bytes 220
  53.0 22.4 %all-to-all-start.1 = ((f32[32,32,128]{2,1,0:T(8,128)}), f32[32,32,128]{2,1,0:T(8,128)S(1)}, u32[]{:S(2)}, u32[]{:S(2)}) async-start(f32[32,32,128]{2,1,0:T(8,128)} %far.1), calls=%async_computation.1 | async-start | bytes 1048576 | tf_op jit(solution)/shard_map/all_to_all | solution.py:324

commit v10 on v9

--- a/solution.py
+++ b/solution.py
@@ -14,6 +14,7 @@
 MIB = 1 << 20
 RE_IM_ROWS = 32
 FIRST = 16
+PARTS = 4
 LIST_ROWS = 8
 FULL = 63
 
@@ -189,7 +190,7 @@
 
 def far_kernel(
     lists_ref, mid_ref, near_ref, table_ref, block_ref, up0_ref, up1_ref, down0_ref, down1_ref, out_ref, radiated_ref,
-    incoming_ref, list_ref, sem,
+    incoming_ref, rows_ref, store_sem, list_ref, sem,
 ):
     staged = pltpu.make_async_copy(lists_ref, list_ref, sem)
     staged.start()
@@ -216,10 +217,19 @@
         return carry
 
     lax.fori_loop(0, list_ref[2 * entries + 2, 0], skipped, 0)
-    far = dot3(split(incoming_ref[...].reshape(boxes * sub, width)), (down0_ref[...], down1_ref[...]), NT_FORM)
+    down = down0_ref[...], down1_ref[...]
     devices, rows, lanes = out_ref.shape
-    out_ref[:, : rows // 2, :] = far[:, :lanes].reshape(devices, rows // 2, lanes)
-    out_ref[:, rows // 2 :, :] = far[:, lanes:].reshape(devices, rows // 2, lanes)
+    half_rows, some, batch = rows // 2, devices // PARTS, boxes // PARTS
+    stores = []
+    for n in range(PARTS):
+        here = pl.ds(n * some, some)
+        far = dot3(split(incoming_ref[n * batch : (n + 1) * batch].reshape(batch * sub, width)), down, NT_FORM)
+        rows_ref[here, :half_rows, :] = far[:, :lanes].reshape(some, half_rows, lanes)
+        rows_ref[here, half_rows:, :] = far[:, lanes:].reshape(some, half_rows, lanes)
+        stores.append(pltpu.make_async_copy(rows_ref.at[here], out_ref.at[here], store_sem.at[n]))
+        stores[n].start()
+    for store in stores:
+        store.wait()
 
 
 def join_kernel(far_ref, near_ref, out_ref, sum_ref, sem):
@@ -317,9 +327,16 @@
         far_kernel,
         shape(devices, rows, unknowns),
         (VMEM,) * 9,
-        scratch=(pltpu.VMEM((3 * boxes, own, width), F32), pltpu.VMEM((boxes, own, width), F32), *staging),
+        scratch=(
+            pltpu.VMEM((3 * boxes, own, width), F32),
+            pltpu.VMEM((boxes, own, width), F32),
+            pltpu.VMEM((devices, rows, unknowns), F32),
+            pltpu.SemaphoreType.DMA((PARTS,)),
+            *staging,
+        ),
         micros=5,
         name="far",
+        out_kind=ANY,
     )(late, partial, near_fields, table, from_cross, up0, up1, down0, down1)
     back = lax.all_to_all(far, "dir", 0, 0, tiled=True)
 

time: 76.5 us -> 76.3 us (level)
  no operation moved by 1% of the time
where the time goes in v10:
time: 76.3 us; the launch traced here: 76 us
  waiting for transfers between devices  31.1 us (41%)
  starting transfers between devices  23.5 us (31%)
  Pallas kernels  21.2 us (28%)
    pallas_call x7, Pallas kernels, run(): pl.pallas_call(kernel, out_shape=outs, in_specs=specs, out_specs=jax.tree...  21.2 us
    all_to_all x1, waiting for transfers between devices, body(): mine = lax.all_to_all(packed, 'dir', 0, 0, tiled=True)  19.8 us
    all_to_all x1, starting transfers between devices, body(): mine = lax.all_to_all(packed, 'dir', 0, 0, tiled=True)  11.5 us
    all_to_all x1, waiting for transfers between devices, body(): back = lax.all_to_all(far, 'dir', 0, 0, tiled=True)  11.3 us
    ppermute x1, starting transfers between devices, body(): right = lax.ppermute(beside, 'dir', [(j, i) for i, j in ring])  4.12 us
    all_to_all x1, starting transfers between devices, body(): back = lax.all_to_all(far, 'dir', 0, 0, tiled=True)  3.9 us
    ppermute x1, starting transfers between devices, body(): from_cross = lax.ppermute(sent, 'slab', cross)  2.53 us
  transfers between devices with their start and end apart: 6, of which 2 were waited for; matrix products, arithmetic and copies ran while one was open for 0% of the time, Pallas kernels for 24%

profile of v10, /device:TPU:2, one launch (start us, length us, event | category | flops | bytes accessed | tf_op | source)
XLA Modules:
  0.0 76.0 jit_solution(5979675248591389087)
XLA Ops:
  0.0 2.2 %pack.1 = f32[32,40,128]{2,1,0:T(8,128)} custom-call(f32[2,2,128,256]{3,2,1,0:T(8,128)} %own_ref.1, f32[2,8,64]{2,1,0:T(8,128)} %bitcast.5), custom_call_target="tpu_custom_call" | custom-call | flops 1000000000 | bytes 1183744 | tf_op jit(solution)/shard_map/pack/pallas_call | solution.py:253
  2.2 11.5 %all-to-all-start = ((f32[32,40,128]{2,1,0:T(8,128)}), f32[32,40,128]{2,1,0:T(8,128)S(1)}, u32[]{:S(2)}, u32[]{:S(2)}) async-start(f32[32,40,128]{2,1,0:T(8,128)} %pack.1), calls=%async_computation | async-start | bytes 1310720 | tf_op jit(solution)/shard_map/all_to_all | solution.py:303
  13.7 0.0 copy-start.1
  13.7 0.0 copy-start.2
  13.7 0.3 plan.1
  14.1 19.8 %all-to-all-done.own_ref = f32[32,40,128]{2,1,0:T(8,128)S(1)} async-done(((f32[32,40,128]{2,1,0:T(8,128)}), f32[32,40,128]{2,1,0:T(8,128)S(1)}, u32[]{:S(2)}, u32[]{:S(2)}) %all-to-all-start) | async-done | bytes 655392 | tf_op jit(solution)/shard_map/all_to_all | solution.py:303
  33.9 0.1 slice.3
  34.0 0.1 collective-permute-start
  34.1 2.5 %collective-permute-start.1 = (f32[32,32,128]{2,1,0:T(8,128)S(1)}, f32[32,32,128]{2,1,0:T(8,128)S(1)}, u32[]{:S(2)}, u32[]{:S(2)}) collective-permute-start(f32[32,32,128]{2,1,0:T(8,128)S(1)} %slice.3), channel_id=1, source_target_pairs={{32,64},{96,128},{160,192},{64,32},{128,96},{192,160},{33,65},{97,... | collective-permute-start | bytes 1572872 | tf_op jit(solution)/shard_map/ppermute | solution.py:308
  36.6 1.3 %collective-permute-start.2 = (f32[2,2,128,256]{3,2,1,0:T(8,128)}, f32[2,2,128,256]{3,2,1,0:T(8,128)}, u32[]{:S(2)}, u32[]{:S(2)}) collective-permute-start(f32[2,2,128,256]{3,2,1,0:T(8,128)} %own_ref.1), channel_id=1, source_target_pairs={{0,1},{1,2},{2,3},{3,4},{4,5},{5,6},{6,7},{7,8},{8,9},{9,10},{10,1... | collective-permute-start | bytes 1572872 | tf_op jit(solution)/shard_map/ppermute | solution.py:310
  37.9 4.1 %collective-permute-start.3 = (f32[2,2,128,256]{3,2,1,0:T(8,128)}, f32[2,2,128,256]{3,2,1,0:T(8,128)}, u32[]{:S(2)}, u32[]{:S(2)}) collective-permute-start(f32[2,2,128,256]{3,2,1,0:T(8,128)} %own_ref.1), channel_id=1, source_target_pairs={{1,0},{2,1},{3,2},{4,3},{5,4},{6,5},{7,6},{8,7},{9,8},{10,9},{11,1... | collective-permute-start | bytes 1572872 | tf_op jit(solution)/shard_map/ppermute | solution.py:311
  42.0 0.8 own.1
  42.8 0.0 collective-permute-done.block_ref
  42.8 4.0 %mid.1 = (f32[64,8,512]{2,1,0:T(8,128)S(1)}, f32[129,8,512]{2,1,0:T(8,128)S(1)}) custom-call(s32[72,128]{1,0:T(8,128)S(1)} %get-tuple-element.22.lists_ref, f32[64,8,512]{2,1,0:T(8,128)S(1)} %get-tuple-element.24.own_ref, f32[64,8,512]{2,1,0:T(8,128)S(1)} %get-tuple-element.25.table_ref, f32[32,32,128]{2,1,0:T(8,128)S(1)} %collective-permute-done.block_ref, ...), custom_call_target="tpu_custom_call" | custom-call | flops 6000000000 | bytes 6868992 | tf_op jit(solution)/shard_map/mid/pallas_call | solution.py:253
  46.8 0.0 collective-permute-done.1.block_ref
  46.8 0.0 copy-start
  46.8 0.0 copy-start.5
  46.8 6.0 %far.1 = f32[32,32,128]{2,1,0:T(8,128)} custom-call(s32[72,128]{1,0:T(8,128)S(1)} %get-tuple-element.21.lists_ref, f32[64,8,512]{2,1,0:T(8,128)S(1)} %get-tuple-element.28.mid_ref, f32[129,8,512]{2,1,0:T(8,128)S(1)} %get-tuple-element.29.near_ref, f32[64,8,512]{2,1,0:T(8,128)S(1)} %get-tuple-element.25.table_ref, ...), custom_call_target="tpu_custom_call" | custom-call | flops 5000000000 | bytes 7393280 | tf_op jit(solution)/shard_map/far/pallas_call | solution.py:253
  52.8 3.9 %all-to-all-start.1 = ((f32[32,32,128]{2,1,0:T(8,128)}), f32[32,32,128]{2,1,0:T(8,128)S(1)}, u32[]{:S(2)}, u32[]{:S(2)}) async-start(f32[32,32,128]{2,1,0:T(8,128)} %far.1), calls=%async_computation.1 | async-start | bytes 1048576 | tf_op jit(solution)/shard_map/all_to_all | solution.py:341
  56.7 0.0 collective-permute-done.2.left_ref
  56.7 0.0 collective-permute-done.3.right_ref
  56.8 7.0 %near.1.near_ref = f32[2,2,128,256]{3,2,1,0:T(8,128)S(1)} custom-call(s32[2,9]{1,0:T(2,128)S(1)} %copy-done.5, f32[2,2,9,128,128]{4,3,2,1,0:T(8,128)S(1)} %copy-done, f32[2,2,128,256]{3,2,1,0:T(8,128)} %own_ref.1, f32[2,2,128,256]{3,2,1,0:T(8,128)} %collective-permute-done.2.left_ref, f32[2,2,128,256]{3,2,1,0:T(8,128)} %collective-permute-done.3.right_ref), custom_call_target="tpu_custom_call" | custom-call | flops 20000000000 | bytes 4456520 | tf_op jit(solution)/shard_map/near/pallas_call | solution.py:253
  63.8 11.3 %all-to-all-done.1.far_ref = f32[32,32,128]{2,1,0:T(8,128)S(1)} async-done(((f32[32,32,128]{2,1,0:T(8,128)}), f32[32,32,128]{2,1,0:T(8,128)S(1)}, u32[]{:S(2)}, u32[]{:S(2)}) %all-to-all-start.1) | async-done | bytes 524320 | tf_op jit(solution)/shard_map/all_to_all | solution.py:341
  75.1 0.9 %join.1 = f32[2,2,128,256]{3,2,1,0:T(8,128)} custom-call(f32[32,32,128]{2,1,0:T(8,128)S(1)} %all-to-all-done.1.far_ref, f32[2,2,128,256]{3,2,1,0:T(8,128)S(1)} %near.1.near_ref), custom_call_target="tpu_custom_call" | custom-call | bytes 1572864 | tf_op jit(solution)/shard_map/join/pallas_call | solution.py:253
  (8 shorter events, 0.0 us)
Async XLA Ops:
  0.0 13.7 %copy-start.3 = (s32[64,32]{0,1:T(8,128)S(1)}, s32[64,32]{0,1:T(8,128)}, u32[]{:S(2)}) copy-start(s32[64,32]{0,1:T(8,128)} %param.13) | copy-start | bytes 24580
  0.0 13.7 %copy-start.4 = (s32[64,32]{0,1:T(8,128)S(1)}, s32[64,32]{0,1:T(8,128)}, u32[]{:S(2)}) copy-start(s32[64,32]{0,1:T(8,128)} %param.14) | copy-start | bytes 24580
  2.2 31.7 %all-to-all-start = ((f32[32,40,128]{2,1,0:T(8,128)}), f32[32,40,128]{2,1,0:T(8,128)S(1)}, u32[]{:S(2)}, u32[]{:S(2)}) async-start(f32[32,40,128]{2,1,0:T(8,128)} %pack.1), calls=%async_computation | async-start | bytes 1310720 | tf_op jit(solution)/shard_map/all_to_all | solution.py:303
  13.7 28.3 %copy-start.1 = (f32[2,256,128]{2,1,0:T(8,128)S(1)}, f32[2,256,128]{2,1,0:T(8,128)}, u32[]{:S(2)}) copy-start(f32[2,256,128]{2,1,0:T(8,128)} %aggregate_ref.1) | copy-start | bytes 786436
  13.7 28.3 %copy-start.2 = (f32[2,128,256]{2,1,0:T(8,128)S(1)}, f32[2,128,256]{2,1,0:T(8,128)}, u32[]{:S(2)}) copy-start(f32[2,128,256]{2,1,0:T(8,128)} %disaggregate_ref.1) | copy-start | bytes 786436
  34.0 8.8 %collective-permute-start = (f32[32,32,128]{2,1,0:T(8,128)S(1)}, f32[32,32,128]{2,1,0:T(8,128)S(1)}, u32[]{:S(2)}, u32[]{:S(2)}) collective-permute-start(f32[32,32,128]{2,1,0:T(8,128)S(1)} %slice.3), channel_id=1, source_target_pairs={{0,32},{64,96},{128,160},{192,224},{32,0},{96,64},{160,128},{224,1... | collective-permute-start | bytes 1572872 | tf_op jit(solution)/shard_map/ppermute | solution.py:309
  34.1 12.8 %collective-permute-start.1 = (f32[32,32,128]{2,1,0:T(8,128)S(1)}, f32[32,32,128]{2,1,0:T(8,128)S(1)}, u32[]{:S(2)}, u32[]{:S(2)}) collective-permute-start(f32[32,32,128]{2,1,0:T(8,128)S(1)} %slice.3), channel_id=1, source_target_pairs={{32,64},{96,128},{160,192},{64,32},{128,96},{192,160},{33,65},{97,... | collective-permute-start | bytes 1572872 | tf_op jit(solution)/shard_map/ppermute | solution.py:308
  36.6 20.1 %collective-permute-start.2 = (f32[2,2,128,256]{3,2,1,0:T(8,128)}, f32[2,2,128,256]{3,2,1,0:T(8,128)}, u32[]{:S(2)}, u32[]{:S(2)}) collective-permute-start(f32[2,2,128,256]{3,2,1,0:T(8,128)} %own_ref.1), channel_id=1, source_target_pairs={{0,1},{1,2},{2,3},{3,4},{4,5},{5,6},{6,7},{7,8},{8,9},{9,10},{10,1... | collective-permute-start | bytes 1572872 | tf_op jit(solution)/shard_map/ppermute | solution.py:310
  37.9 18.8 %collective-permute-start.3 = (f32[2,2,128,256]{3,2,1,0:T(8,128)}, f32[2,2,128,256]{3,2,1,0:T(8,128)}, u32[]{:S(2)}, u32[]{:S(2)}) collective-permute-start(f32[2,2,128,256]{3,2,1,0:T(8,128)} %own_ref.1), channel_id=1, source_target_pairs={{1,0},{2,1},{3,2},{4,3},{5,4},{6,5},{7,6},{8,7},{9,8},{10,9},{11,1... | collective-permute-start | bytes 1572872 | tf_op jit(solution)/shard_map/ppermute | solution.py:311
  46.8 9.9 %copy-start = (f32[2,2,9,128,128]{4,3,2,1,0:T(8,128)S(1)}, f32[2,2,9,128,128]{4,3,2,1,0:T(8,128)}, u32[]{:S(2)}) copy-start(f32[2,2,9,128,128]{4,3,2,1,0:T(8,128)} %blocks_ref.1) | copy-start | bytes 7077892
  46.8 9.9 %copy-start.5 = (s32[2,9]{1,0:T(2,128)S(1)}, s32[2,9]{1,0:T(2,128)}, u32[]{:S(2)}) copy-start(s32[2,9]{1,0:T(2,128)} %index_ref.1) | copy-start | bytes 220
  52.8 22.3 %all-to-all-start.1 = ((f32[32,32,128]{2,1,0:T(8,128)}), f32[32,32,128]{2,1,0:T(8,128)S(1)}, u32[]{:S(2)}, u32[]{:S(2)}) async-start(f32[32,32,128]{2,1,0:T(8,128)} %far.1), calls=%async_computation.1 | async-start | bytes 1048576 | tf_op jit(solution)/shard_map/all_to_all | solution.py:341

commit v11 on v10

--- a/solution.py
+++ b/solution.py
@@ -14,7 +14,8 @@
 MIB = 1 << 20
 RE_IM_ROWS = 32
 FIRST = 16
-PARTS = 4
+PARTS = 2
+HALVES = 2
 LIST_ROWS = 8
 FULL = 63
 
@@ -35,7 +36,11 @@
 NT_FORM = ((1,), (1,))
 
 
-def plan_kernel(source_ref, shift_ref, early_ref, late_ref):
+def plan_kernel(
+    source_ref, shift_ref, aggregate_ref, disaggregate_ref, early_ref, late_ref, up0_ref, up1_ref, down0_ref, down1_ref
+):
+    up0_ref[...], up1_ref[...] = split(complex_rows(aggregate_ref))
+    down0_ref[...], down1_ref[...] = split(complex_rows(disaggregate_ref))
     entries, boxes = source_ref.shape
     odd = lax.axis_index("slab") % 2
     source, shift = source_ref[...], shift_ref[...]
@@ -75,27 +80,31 @@
 
 
 def pack_kernel(currents_ref, translations_ref, out_ref, block_ref, table_ref, packed_ref, in_sem, out_sem):
-    devices, rows, lanes = out_ref.shape
+    devices, _, lanes = out_ref.shape
     parts, boxes, _, illum = currents_ref.shape
     own = illum // devices
-    pieces = [(c, b) for c in range(parts) for b in range(boxes)]
-    last = len(pieces)
-    loads = [pltpu.make_async_copy(currents_ref.at[c, b], block_ref.at[n], in_sem.at[n]) for n, (c, b) in enumerate(pieces)]
-    loads.append(pltpu.make_async_copy(translations_ref, table_ref, in_sem.at[last]))
-    stores = [
-        pltpu.make_async_copy(packed_ref.at[:, pl.ds(n * own, own), :], out_ref.at[:, pl.ds(n * own, own), :], out_sem.at[n])
-        for n in range(last + 1)
-    ]
+    pieces = parts * boxes
+    some, columns = devices // HALVES, illum // HALVES
+    table_load = pltpu.make_async_copy(translations_ref, table_ref, in_sem.at[HALVES * pieces])
+    loads = []
+    for h in range(HALVES):
+        for n in range(pieces):
+            piece = currents_ref.at[n // boxes, n % boxes, :, pl.ds(h * columns, columns)]
+            loads.append(pltpu.make_async_copy(piece, block_ref.at[h, n], in_sem.at[h * pieces + n]))
+    table_load.start()
     for load in loads:
         load.start()
-    for n in range(last):
-        loads[n].wait()
-        packed_ref[:, n * own : (n + 1) * own, :] = block_ref[n].T.reshape(devices, own, lanes)
-        stores[n].start()
-    loads[last].wait()
+    table_load.wait()
     table = jnp.concatenate([table_ref[0], table_ref[1]], axis=1)
-    packed_ref[:, last * own :, :] = jnp.broadcast_to(table[None], (devices, own, lanes))
-    stores[last].start()
+    packed_ref[:, pieces * own :, :] = jnp.broadcast_to(table[None], (devices, table.shape[0], lanes))
+    stores = []
+    for h in range(HALVES):
+        here = pl.ds(h * some, some)
+        for n in range(pieces):
+            loads[h * pieces + n].wait()
+            packed_ref[here, n * own : (n + 1) * own, :] = block_ref[h, n].T.reshape(some, own, lanes)
+        stores.append(pltpu.make_async_copy(packed_ref.at[here], out_ref.at[here], out_sem.at[h]))
+        stores[h].start()
     for store in stores:
         store.wait()
 
@@ -138,12 +147,9 @@
     )
 
 
-def own_kernel(own_ref, aggregate_ref, disaggregate_ref, radiated_ref, table_ref, up0_ref, up1_ref, down0_ref, down1_ref):
+def own_kernel(own_ref, up0_ref, up1_ref, radiated_ref, table_ref):
     boxes, sub, width = radiated_ref.shape
-    up = split(complex_rows(aggregate_ref))
-    up0_ref[...], up1_ref[...] = up
-    down0_ref[...], down1_ref[...] = split(complex_rows(disaggregate_ref))
-    radiated_ref[...] = radiate(own_ref, up).reshape(boxes, sub, width)
+    radiated_ref[...] = radiate(own_ref, (up0_ref[...], up1_ref[...])).reshape(boxes, sub, width)
     devices, rows, lanes = own_ref.shape
     table = own_ref[:, RE_IM_ROWS:, :].reshape(devices * (rows - RE_IM_ROWS), lanes).T
     half = lanes // 2
@@ -290,11 +296,11 @@
         whole,
         (ANY, ANY),
         scratch=(
-            blocks,
+            pltpu.VMEM((HALVES, pieces, unknowns, illum // HALVES), F32),
             pltpu.VMEM(turned.shape, F32),
             pltpu.VMEM(whole.shape, F32),
-            pltpu.SemaphoreType.DMA((pieces + 1,)),
-            pltpu.SemaphoreType.DMA((pieces + 1,)),
+            pltpu.SemaphoreType.DMA((HALVES * pieces + 1,)),
+            pltpu.SemaphoreType.DMA((HALVES,)),
         ),
         limit=FULL,
         name="pack",
@@ -302,25 +308,26 @@
     )(currents, turned)
     mine = lax.all_to_all(packed, "dir", 0, 0, tiled=True)
     lists = shape(2 * entries + LIST_ROWS, 128, kind=jnp.int32)
-    early, late = call(plan_kernel, (lists, lists), (VMEM, VMEM), name="plan")(inter_source.T, inter_shift.T)
-    mine, beside, early, late = lax.optimization_barrier((mine, currents, early, late))
+    up, down = shape(width, 2 * unknowns, kind=BF16), shape(2 * unknowns, width, kind=BF16)
+    planned = call(plan_kernel, (lists, lists, up, up, down, down), (VMEM,) * 4, name="plan")(
+        inter_source.T, inter_shift.T, aggregate, disaggregate
+    )
+    mine, beside, planned = lax.optimization_barrier((mine, currents, planned))
+    early, late, up0, up1, down0, down1 = planned
     sent = mine[:, :rows]
     from_cross = lax.ppermute(sent, "slab", cross)
     from_same = lax.ppermute(sent, "slab", same)
     left = lax.ppermute(beside, "dir", ring)
     right = lax.ppermute(beside, "dir", [(j, i) for i, j in ring])
     field = shape(boxes, own, width)
-    up, down = shape(width, 2 * unknowns, kind=BF16), shape(2 * unknowns, width, kind=BF16)
-    radiated, table, up0, up1, down0, down1 = call(
-        own_kernel, (field, shape(ops, own, width), up, up, down, down), (VMEM,) * 3, name="own"
-    )(mine, aggregate, disaggregate)
+    radiated, table = call(own_kernel, (field, shape(ops, own, width)), (VMEM,) * 3, micros=0, name="own")(mine, up0, up1)
     staging = (pltpu.SMEM(lists.shape, jnp.int32), pltpu.SemaphoreType.DMA)
     partial, near_fields = call(
         mid_kernel,
         (field, shape(2 * boxes + 1, own, width)),
         (VMEM,) * 6,
         scratch=staging,
-        micros=6,
+        micros=0,
         name="mid",
     )(early, radiated, table, from_same, up0, up1)
     far = call(
@@ -334,7 +341,7 @@
             pltpu.SemaphoreType.DMA((PARTS,)),
             *staging,
         ),
-        micros=5,
+        micros=0,
         name="far",
         out_kind=ANY,
     )(late, partial, near_fields, table, from_cross, up0, up1, down0, down1)

time: 76.3 us -> 76.2 us (level)
  local copies, waits for them, and re-layouts: 0.09 us -> 1.74 us
  waiting for transfers between devices: 31.1 us -> 30.1 us
  Pallas kernels: 21.2 us -> 20.3 us
    unnamed x12 -> x14, local copies, waits for them, and re-layouts: 0.03 us -> 1.69 us
    pallas_call x7, Pallas kernels: 21.2 us -> 20.3 us  [run(): pl.pallas_call(kernel, out_shape=outs, in_specs=specs, out_specs=jax.tree...]
    all_to_all x1, waiting for transfers between devices: 11.3 us -> 10.5 us  [body(): back = lax.all_to_all(far, 'dir', 0, 0, tiled=True)]
  transfers between devices with their start and end apart: 6 -> 6, of which waited for: 2 -> 2; matrix products, arithmetic and copies ran while one was open for 0% -> 0% of each run, Pallas kernels for 24% -> 22%
where the time goes in v11:
time: 76.2 us; the launch traced here: 75.8 us
  waiting for transfers between devices  30.1 us (40%)
  starting transfers between devices  23.4 us (31%)
  Pallas kernels  20.3 us (27%)
  local copies, waits for them, and re-layouts  1.74 us (2%)
    pallas_call x7, Pallas kernels, run(): pl.pallas_call(kernel, out_shape=outs, in_specs=specs, out_specs=jax.tree...  20.3 us
    all_to_all x1, waiting for transfers between devices, body(): mine = lax.all_to_all(packed, 'dir', 0, 0, tiled=True)  19.6 us
    all_to_all x1, starting transfers between devices, body(): mine = lax.all_to_all(packed, 'dir', 0, 0, tiled=True)  11.5 us
    all_to_all x1, waiting for transfers between devices, body(): back = lax.all_to_all(far, 'dir', 0, 0, tiled=True)  10.5 us
    ppermute x1, starting transfers between devices, body(): right = lax.ppermute(beside, 'dir', [(j, i) for i, j in ring])  4.12 us
    all_to_all x1, starting transfers between devices, body(): back = lax.all_to_all(far, 'dir', 0, 0, tiled=True)  3.9 us
    ppermute x1, starting transfers between devices, body(): from_cross = lax.ppermute(sent, 'slab', cross)  2.53 us
    unnamed x14, local copies, waits for them, and re-layouts  1.69 us
  transfers between devices with their start and end apart: 6, of which 2 were waited for; matrix products, arithmetic and copies ran while one was open for 0% of the time, Pallas kernels for 22%

profile of v11, /device:TPU:2, one launch (start us, length us, event | category | flops | bytes accessed | tf_op | source)
XLA Modules:
  0.0 75.8 jit_solution(8843157568701557953)
XLA Ops:
  0.0 2.5 %pack.1 = f32[32,40,128]{2,1,0:T(8,128)} custom-call(f32[2,2,128,256]{3,2,1,0:T(8,128)} %own_ref.1, f32[2,8,64]{2,1,0:T(8,128)} %bitcast.5), custom_call_target="tpu_custom_call" | custom-call | flops 1000000000 | bytes 1183744 | tf_op jit(solution)/shard_map/pack/pallas_call | solution.py:259
  2.6 11.5 %all-to-all-start = ((f32[32,40,128]{2,1,0:T(8,128)}), f32[32,40,128]{2,1,0:T(8,128)S(1)}, u32[]{:S(2)}, u32[]{:S(2)}) async-start(f32[32,40,128]{2,1,0:T(8,128)} %pack.1), calls=%async_computation | async-start | bytes 1310720 | tf_op jit(solution)/shard_map/all_to_all | solution.py:309
  14.1 0.0 copy-start.1
  14.1 0.5 plan.1
  14.7 19.6 %all-to-all-done.own_ref = f32[32,40,128]{2,1,0:T(8,128)S(1)} async-done(((f32[32,40,128]{2,1,0:T(8,128)}), f32[32,40,128]{2,1,0:T(8,128)S(1)}, u32[]{:S(2)}, u32[]{:S(2)}) %all-to-all-start) | async-done | bytes 655392 | tf_op jit(solution)/shard_map/all_to_all | solution.py:309
  34.3 0.1 slice.3
  34.3 0.1 collective-permute-start
  34.4 2.5 %collective-permute-start.1 = (f32[32,32,128]{2,1,0:T(8,128)S(1)}, f32[32,32,128]{2,1,0:T(8,128)S(1)}, u32[]{:S(2)}, u32[]{:S(2)}) collective-permute-start(f32[32,32,128]{2,1,0:T(8,128)S(1)} %slice.3), channel_id=1, source_target_pairs={{32,64},{96,128},{160,192},{64,32},{128,96},{192,160},{33,65},{97,... | collective-permute-start | bytes 1572872 | tf_op jit(solution)/shard_map/ppermute | solution.py:318
  37.0 1.3 %collective-permute-start.2 = (f32[2,2,128,256]{3,2,1,0:T(8,128)S(1)}, f32[2,2,128,256]{3,2,1,0:T(8,128)S(1)}, u32[]{:S(2)}, u32[]{:S(2)}) collective-permute-start(f32[2,2,128,256]{3,2,1,0:T(8,128)S(1)} %copy-done.1), channel_id=1, source_target_pairs={{0,1},{1,2},{2,3},{3,4},{4,5},{5,6},{6,7},{7,8},{8,9},{9,10},{10,1... | collective-permute-start | bytes 1572872 | tf_op jit(solution)/shard_map/ppermute | solution.py:320
  38.3 4.1 %collective-permute-start.3 = (f32[2,2,128,256]{3,2,1,0:T(8,128)S(1)}, f32[2,2,128,256]{3,2,1,0:T(8,128)S(1)}, u32[]{:S(2)}, u32[]{:S(2)}) collective-permute-start(f32[2,2,128,256]{3,2,1,0:T(8,128)S(1)} %copy-done.1), channel_id=1, source_target_pairs={{1,0},{2,1},{3,2},{4,3},{5,4},{6,5},{7,6},{8,7},{9,8},{10,9},{11,1... | collective-permute-start | bytes 1572872 | tf_op jit(solution)/shard_map/ppermute | solution.py:321
  42.4 0.6 own.1
  43.1 0.0 collective-permute-done.block_ref
  43.1 4.0 %mid.1 = (f32[64,8,512]{2,1,0:T(8,128)S(1)}, f32[129,8,512]{2,1,0:T(8,128)S(1)}) custom-call(s32[72,128]{1,0:T(8,128)S(1)} %get-tuple-element.30.lists_ref, f32[64,8,512]{2,1,0:T(8,128)S(1)} %get-tuple-element.34.own_ref, f32[64,8,512]{2,1,0:T(8,128)S(1)} %get-tuple-element.35.table_ref, f32[32,32,128]{2,1,0:T(8,128)S(1)} %collective-permute-done.block_ref, ...), custom_call_target="tpu_custom_call" | custom-call | bytes 6868992 | tf_op jit(solution)/shard_map/mid/pallas_call | solution.py:259
  47.1 0.0 collective-permute-done.1.block_ref
  47.1 0.0 copy-start.6
  47.1 5.5 %far.1 = f32[32,32,128]{2,1,0:T(8,128)} custom-call(s32[72,128]{1,0:T(8,128)S(1)} %get-tuple-element.29.lists_ref, f32[64,8,512]{2,1,0:T(8,128)S(1)} %get-tuple-element.36.mid_ref, f32[129,8,512]{2,1,0:T(8,128)S(1)} %get-tuple-element.37.near_ref, f32[64,8,512]{2,1,0:T(8,128)S(1)} %get-tuple-element.35.table_ref, ...), custom_call_target="tpu_custom_call" | custom-call | bytes 7393280 | tf_op jit(solution)/shard_map/far/pallas_call | solution.py:259
  52.6 3.9 %all-to-all-start.1 = ((f32[32,32,128]{2,1,0:T(8,128)}), f32[32,32,128]{2,1,0:T(8,128)S(1)}, u32[]{:S(2)}, u32[]{:S(2)}) async-start(f32[32,32,128]{2,1,0:T(8,128)} %far.1), calls=%async_computation.1 | async-start | bytes 1048576 | tf_op jit(solution)/shard_map/all_to_all | solution.py:348
  56.5 0.0 collective-permute-done.2.left_ref
  56.5 0.0 collective-permute-done.3.right_ref
  56.6 0.0 copy-start
  56.6 1.7 %copy-done = f32[2,2,9,128,128]{4,3,2,1,0:T(8,128)S(1)} copy-done((f32[2,2,9,128,128]{4,3,2,1,0:T(8,128)S(1)}, f32[2,2,9,128,128]{4,3,2,1,0:T(8,128)}, u32[]{:S(2)}) %copy-start) | copy-done | bytes 2359320
  58.2 6.1 %near.1.near_ref = f32[2,2,128,256]{3,2,1,0:T(8,128)S(1)} custom-call(s32[2,9]{1,0:T(2,128)S(1)} %copy-done.6, f32[2,2,9,128,128]{4,3,2,1,0:T(8,128)S(1)} %copy-done, f32[2,2,128,256]{3,2,1,0:T(8,128)S(1)} %copy-done.1, f32[2,2,128,256]{3,2,1,0:T(8,128)S(1)} %collective-permute-done.2.left_ref, f32[2,2,128,256]{3,2,1,0:T(8,128)S(1)} %collective-permute-done.3.right_ref), custom_call_target="tpu_custom_call" | custom-call | flops 20000000000 | bytes 4456520 | tf_op jit(solution)/shard_map/near/pallas_call | solution.py:259
  64.4 10.5 %all-to-all-done.1.far_ref = f32[32,32,128]{2,1,0:T(8,128)S(1)} async-done(((f32[32,32,128]{2,1,0:T(8,128)}), f32[32,32,128]{2,1,0:T(8,128)S(1)}, u32[]{:S(2)}, u32[]{:S(2)}) %all-to-all-start.1) | async-done | bytes 524320 | tf_op jit(solution)/shard_map/all_to_all | solution.py:348
  74.8 0.9 %join.1 = f32[2,2,128,256]{3,2,1,0:T(8,128)} custom-call(f32[32,32,128]{2,1,0:T(8,128)S(1)} %all-to-all-done.1.far_ref, f32[2,2,128,256]{3,2,1,0:T(8,128)S(1)} %near.1.near_ref), custom_call_target="tpu_custom_call" | custom-call | bytes 1572864 | tf_op jit(solution)/shard_map/join/pallas_call | solution.py:259
  (10 shorter events, 0.0 us)
Async XLA Ops:
  0.0 14.1 %copy-start.2 = (f32[2,256,128]{2,1,0:T(8,128)S(1)}, f32[2,256,128]{2,1,0:T(8,128)}, u32[]{:S(2)}) copy-start(f32[2,256,128]{2,1,0:T(8,128)} %aggregate_ref.1) | copy-start | bytes 786436
  0.0 14.1 %copy-start.3 = (f32[2,128,256]{2,1,0:T(8,128)S(1)}, f32[2,128,256]{2,1,0:T(8,128)}, u32[]{:S(2)}) copy-start(f32[2,128,256]{2,1,0:T(8,128)} %disaggregate_ref.1) | copy-start | bytes 786436
  0.0 14.1 %copy-start.4 = (s32[64,32]{0,1:T(8,128)S(1)}, s32[64,32]{0,1:T(8,128)}, u32[]{:S(2)}) copy-start(s32[64,32]{0,1:T(8,128)} %param.13) | copy-start | bytes 24580
  0.0 14.1 %copy-start.5 = (s32[64,32]{0,1:T(8,128)S(1)}, s32[64,32]{0,1:T(8,128)}, u32[]{:S(2)}) copy-start(s32[64,32]{0,1:T(8,128)} %param.14) | copy-start | bytes 24580
  2.6 31.7 %all-to-all-start = ((f32[32,40,128]{2,1,0:T(8,128)}), f32[32,40,128]{2,1,0:T(8,128)S(1)}, u32[]{:S(2)}, u32[]{:S(2)}) async-start(f32[32,40,128]{2,1,0:T(8,128)} %pack.1), calls=%async_computation | async-start | bytes 1310720 | tf_op jit(solution)/shard_map/all_to_all | solution.py:309
  14.1 22.9 %copy-start.1 = (f32[2,2,128,256]{3,2,1,0:T(8,128)S(1)}, f32[2,2,128,256]{3,2,1,0:T(8,128)}, u32[]{:S(2)}) copy-start(f32[2,2,128,256]{3,2,1,0:T(8,128)} %own_ref.1) | copy-start | bytes 1572868
  34.3 8.7 %collective-permute-start = (f32[32,32,128]{2,1,0:T(8,128)S(1)}, f32[32,32,128]{2,1,0:T(8,128)S(1)}, u32[]{:S(2)}, u32[]{:S(2)}) collective-permute-start(f32[32,32,128]{2,1,0:T(8,128)S(1)} %slice.3), channel_id=1, source_target_pairs={{0,32},{64,96},{128,160},{192,224},{32,0},{96,64},{160,128},{224,1... | collective-permute-start | bytes 1572872 | tf_op jit(solution)/shard_map/ppermute | solution.py:319
  34.4 12.7 %collective-permute-start.1 = (f32[32,32,128]{2,1,0:T(8,128)S(1)}, f32[32,32,128]{2,1,0:T(8,128)S(1)}, u32[]{:S(2)}, u32[]{:S(2)}) collective-permute-start(f32[32,32,128]{2,1,0:T(8,128)S(1)} %slice.3), channel_id=1, source_target_pairs={{32,64},{96,128},{160,192},{64,32},{128,96},{192,160},{33,65},{97,... | collective-permute-start | bytes 1572872 | tf_op jit(solution)/shard_map/ppermute | solution.py:318
  37.0 19.6 %collective-permute-start.2 = (f32[2,2,128,256]{3,2,1,0:T(8,128)S(1)}, f32[2,2,128,256]{3,2,1,0:T(8,128)S(1)}, u32[]{:S(2)}, u32[]{:S(2)}) collective-permute-start(f32[2,2,128,256]{3,2,1,0:T(8,128)S(1)} %copy-done.1), channel_id=1, source_target_pairs={{0,1},{1,2},{2,3},{3,4},{4,5},{5,6},{6,7},{7,8},{8,9},{9,10},{10,1... | collective-permute-start | bytes 1572872 | tf_op jit(solution)/shard_map/ppermute | solution.py:320
  38.3 18.3 %collective-permute-start.3 = (f32[2,2,128,256]{3,2,1,0:T(8,128)S(1)}, f32[2,2,128,256]{3,2,1,0:T(8,128)S(1)}, u32[]{:S(2)}, u32[]{:S(2)}) collective-permute-start(f32[2,2,128,256]{3,2,1,0:T(8,128)S(1)} %copy-done.1), channel_id=1, source_target_pairs={{1,0},{2,1},{3,2},{4,3},{5,4},{6,5},{7,6},{8,7},{9,8},{10,9},{11,1... | collective-permute-start | bytes 1572872 | tf_op jit(solution)/shard_map/ppermute | solution.py:321
  47.1 9.5 %copy-start.6 = (s32[2,9]{1,0:T(2,128)S(1)}, s32[2,9]{1,0:T(2,128)}, u32[]{:S(2)}) copy-start(s32[2,9]{1,0:T(2,128)} %index_ref.1) | copy-start | bytes 220
  52.6 22.2 %all-to-all-start.1 = ((f32[32,32,128]{2,1,0:T(8,128)}), f32[32,32,128]{2,1,0:T(8,128)S(1)}, u32[]{:S(2)}, u32[]{:S(2)}) async-start(f32[32,32,128]{2,1,0:T(8,128)} %far.1), calls=%async_computation.1 | async-start | bytes 1048576 | tf_op jit(solution)/shard_map/all_to_all | solution.py:348
  56.6 1.7 %copy-start = (f32[2,2,9,128,128]{4,3,2,1,0:T(8,128)S(1)}, f32[2,2,9,128,128]{4,3,2,1,0:T(8,128)}, u32[]{:S(2)}) copy-start(f32[2,2,9,128,128]{4,3,2,1,0:T(8,128)} %blocks_ref.1) | copy-start | bytes 7077892

commit v12 on v10

--- a/solution.py
+++ b/solution.py
@@ -14,7 +14,7 @@
 MIB = 1 << 20
 RE_IM_ROWS = 32
 FIRST = 16
-PARTS = 4
+PARTS = 2
 LIST_ROWS = 8
 FULL = 63
 
@@ -35,7 +35,11 @@
 NT_FORM = ((1,), (1,))
 
 
-def plan_kernel(source_ref, shift_ref, early_ref, late_ref):
+def plan_kernel(
+    source_ref, shift_ref, aggregate_ref, disaggregate_ref, early_ref, late_ref, up0_ref, up1_ref, down0_ref, down1_ref
+):
+    up0_ref[...], up1_ref[...] = split(complex_rows(aggregate_ref))
+    down0_ref[...], down1_ref[...] = split(complex_rows(disaggregate_ref))
     entries, boxes = source_ref.shape
     odd = lax.axis_index("slab") % 2
     source, shift = source_ref[...], shift_ref[...]
@@ -86,16 +90,16 @@
         pltpu.make_async_copy(packed_ref.at[:, pl.ds(n * own, own), :], out_ref.at[:, pl.ds(n * own, own), :], out_sem.at[n])
         for n in range(last + 1)
     ]
-    for load in loads:
+    for load in [loads[last], *loads[:last]]:
         load.start()
+    loads[last].wait()
+    table = jnp.concatenate([table_ref[0], table_ref[1]], axis=1)
+    packed_ref[:, last * own :, :] = jnp.broadcast_to(table[None], (devices, own, lanes))
+    stores[last].start()
     for n in range(last):
         loads[n].wait()
         packed_ref[:, n * own : (n + 1) * own, :] = block_ref[n].T.reshape(devices, own, lanes)
         stores[n].start()
-    loads[last].wait()
-    table = jnp.concatenate([table_ref[0], table_ref[1]], axis=1)
-    packed_ref[:, last * own :, :] = jnp.broadcast_to(table[None], (devices, own, lanes))
-    stores[last].start()
     for store in stores:
         store.wait()
 
@@ -138,12 +142,9 @@
     )
 
 
-def own_kernel(own_ref, aggregate_ref, disaggregate_ref, radiated_ref, table_ref, up0_ref, up1_ref, down0_ref, down1_ref):
+def own_kernel(own_ref, up0_ref, up1_ref, radiated_ref, table_ref):
     boxes, sub, width = radiated_ref.shape
-    up = split(complex_rows(aggregate_ref))
-    up0_ref[...], up1_ref[...] = up
-    down0_ref[...], down1_ref[...] = split(complex_rows(disaggregate_ref))
-    radiated_ref[...] = radiate(own_ref, up).reshape(boxes, sub, width)
+    radiated_ref[...] = radiate(own_ref, (up0_ref[...], up1_ref[...])).reshape(boxes, sub, width)
     devices, rows, lanes = own_ref.shape
     table = own_ref[:, RE_IM_ROWS:, :].reshape(devices * (rows - RE_IM_ROWS), lanes).T
     half = lanes // 2
@@ -302,25 +303,26 @@
     )(currents, turned)
     mine = lax.all_to_all(packed, "dir", 0, 0, tiled=True)
     lists = shape(2 * entries + LIST_ROWS, 128, kind=jnp.int32)
-    early, late = call(plan_kernel, (lists, lists), (VMEM, VMEM), name="plan")(inter_source.T, inter_shift.T)
-    mine, beside, early, late = lax.optimization_barrier((mine, currents, early, late))
+    up, down = shape(width, 2 * unknowns, kind=BF16), shape(2 * unknowns, width, kind=BF16)
+    planned = call(plan_kernel, (lists, lists, up, up, down, down), (VMEM,) * 4, name="plan")(
+        inter_source.T, inter_shift.T, aggregate, disaggregate
+    )
+    mine, beside, planned = lax.optimization_barrier((mine, currents, planned))
+    early, late, up0, up1, down0, down1 = planned
     sent = mine[:, :rows]
     from_cross = lax.ppermute(sent, "slab", cross)
     from_same = lax.ppermute(sent, "slab", same)
     left = lax.ppermute(beside, "dir", ring)
     right = lax.ppermute(beside, "dir", [(j, i) for i, j in ring])
     field = shape(boxes, own, width)
-    up, down = shape(width, 2 * unknowns, kind=BF16), shape(2 * unknowns, width, kind=BF16)
-    radiated, table, up0, up1, down0, down1 = call(
-        own_kernel, (field, shape(ops, own, width), up, up, down, down), (VMEM,) * 3, name="own"
-    )(mine, aggregate, disaggregate)
+    radiated, table = call(own_kernel, (field, shape(ops, own, width)), (VMEM,) * 3, micros=0, name="own")(mine, up0, up1)
     staging = (pltpu.SMEM(lists.shape, jnp.int32), pltpu.SemaphoreType.DMA)
     partial, near_fields = call(
         mid_kernel,
         (field, shape(2 * boxes + 1, own, width)),
         (VMEM,) * 6,
         scratch=staging,
-        micros=6,
+        micros=0,
         name="mid",
     )(early, radiated, table, from_same, up0, up1)
     far = call(
@@ -334,7 +336,7 @@
             pltpu.SemaphoreType.DMA((PARTS,)),
             *staging,
         ),
-        micros=5,
+        micros=0,
         name="far",
         out_kind=ANY,
     )(late, partial, near_fields, table, from_cross, up0, up1, down0, down1)

time: 76.3 us -> 75.7 us (level)
  local copies, waits for them, and re-layouts: 0.09 us -> 1.74 us
  Pallas kernels: 21.2 us -> 19.9 us
  waiting for transfers between devices: 31.1 us -> 29.9 us
    unnamed x12 -> x14, local copies, waits for them, and re-layouts: 0.03 us -> 1.69 us
    pallas_call x7, Pallas kernels: 21.2 us -> 19.9 us  [run(): pl.pallas_call(kernel, out_shape=outs, in_specs=specs, out_specs=jax.tree...]
    all_to_all x1, waiting for transfers between devices: 11.3 us -> 10.3 us  [body(): back = lax.all_to_all(far, 'dir', 0, 0, tiled=True)]
  transfers between devices with their start and end apart: 6 -> 6, of which waited for: 2 -> 2; matrix products, arithmetic and copies ran while one was open for 0% -> 0% of each run, Pallas kernels for 24% -> 22%
where the time goes in v12:
time: 75.7 us; the launch traced here: 75.2 us
  waiting for transfers between devices  29.9 us (39%)
  starting transfers between devices  23.4 us (31%)
  Pallas kernels  19.9 us (26%)
  local copies, waits for them, and re-layouts  1.74 us (2%)
    pallas_call x7, Pallas kernels, run(): pl.pallas_call(kernel, out_shape=outs, in_specs=specs, out_specs=jax.tree...  19.9 us
    all_to_all x1, waiting for transfers between devices, body(): mine = lax.all_to_all(packed, 'dir', 0, 0, tiled=True)  19.6 us
    all_to_all x1, starting transfers between devices, body(): mine = lax.all_to_all(packed, 'dir', 0, 0, tiled=True)  11.5 us
    all_to_all x1, waiting for transfers between devices, body(): back = lax.all_to_all(far, 'dir', 0, 0, tiled=True)  10.3 us
    ppermute x1, starting transfers between devices, body(): right = lax.ppermute(beside, 'dir', [(j, i) for i, j in ring])  4.12 us
    all_to_all x1, starting transfers between devices, body(): back = lax.all_to_all(far, 'dir', 0, 0, tiled=True)  3.9 us
    ppermute x1, starting transfers between devices, body(): from_cross = lax.ppermute(sent, 'slab', cross)  2.53 us
    unnamed x14, local copies, waits for them, and re-layouts  1.69 us
  transfers between devices with their start and end apart: 6, of which 2 were waited for; matrix products, arithmetic and copies ran while one was open for 0% of the time, Pallas kernels for 22%

profile of v12, /device:TPU:2, one launch (start us, length us, event | category | flops | bytes accessed | tf_op | source)
XLA Modules:
  0.0 75.2 jit_solution(4627713019308341303)
XLA Ops:
  0.0 2.1 %pack.1 = f32[32,40,128]{2,1,0:T(8,128)} custom-call(f32[2,2,128,256]{3,2,1,0:T(8,128)} %own_ref.1, f32[2,8,64]{2,1,0:T(8,128)} %bitcast.5), custom_call_target="tpu_custom_call" | custom-call | flops 1000000000 | bytes 1183744 | tf_op jit(solution)/shard_map/pack/pallas_call | solution.py:254
  2.2 11.5 %all-to-all-start = ((f32[32,40,128]{2,1,0:T(8,128)}), f32[32,40,128]{2,1,0:T(8,128)S(1)}, u32[]{:S(2)}, u32[]{:S(2)}) async-start(f32[32,40,128]{2,1,0:T(8,128)} %pack.1), calls=%async_computation | async-start | bytes 1310720 | tf_op jit(solution)/shard_map/all_to_all | solution.py:304
  13.7 0.0 copy-start.1
  13.7 0.5 plan.1
  14.3 19.6 %all-to-all-done.own_ref = f32[32,40,128]{2,1,0:T(8,128)S(1)} async-done(((f32[32,40,128]{2,1,0:T(8,128)}), f32[32,40,128]{2,1,0:T(8,128)S(1)}, u32[]{:S(2)}, u32[]{:S(2)}) %all-to-all-start) | async-done | bytes 655392 | tf_op jit(solution)/shard_map/all_to_all | solution.py:304
  33.9 0.1 slice.3
  33.9 0.1 collective-permute-start
  34.0 2.5 %collective-permute-start.1 = (f32[32,32,128]{2,1,0:T(8,128)S(1)}, f32[32,32,128]{2,1,0:T(8,128)S(1)}, u32[]{:S(2)}, u32[]{:S(2)}) collective-permute-start(f32[32,32,128]{2,1,0:T(8,128)S(1)} %slice.3), channel_id=1, source_target_pairs={{32,64},{96,128},{160,192},{64,32},{128,96},{192,160},{33,65},{97,... | collective-permute-start | bytes 1572872 | tf_op jit(solution)/shard_map/ppermute | solution.py:313
  36.6 1.3 %collective-permute-start.2 = (f32[2,2,128,256]{3,2,1,0:T(8,128)S(1)}, f32[2,2,128,256]{3,2,1,0:T(8,128)S(1)}, u32[]{:S(2)}, u32[]{:S(2)}) collective-permute-start(f32[2,2,128,256]{3,2,1,0:T(8,128)S(1)} %copy-done.1), channel_id=1, source_target_pairs={{0,1},{1,2},{2,3},{3,4},{4,5},{5,6},{6,7},{7,8},{8,9},{9,10},{10,1... | collective-permute-start | bytes 1572872 | tf_op jit(solution)/shard_map/ppermute | solution.py:315
  37.9 4.1 %collective-permute-start.3 = (f32[2,2,128,256]{3,2,1,0:T(8,128)S(1)}, f32[2,2,128,256]{3,2,1,0:T(8,128)S(1)}, u32[]{:S(2)}, u32[]{:S(2)}) collective-permute-start(f32[2,2,128,256]{3,2,1,0:T(8,128)S(1)} %copy-done.1), channel_id=1, source_target_pairs={{1,0},{2,1},{3,2},{4,3},{5,4},{6,5},{7,6},{8,7},{9,8},{10,9},{11,1... | collective-permute-start | bytes 1572872 | tf_op jit(solution)/shard_map/ppermute | solution.py:316
  42.0 0.6 own.1
  42.7 0.0 collective-permute-done.block_ref
  42.7 4.0 %mid.1 = (f32[64,8,512]{2,1,0:T(8,128)S(1)}, f32[129,8,512]{2,1,0:T(8,128)S(1)}) custom-call(s32[72,128]{1,0:T(8,128)S(1)} %get-tuple-element.30.lists_ref, f32[64,8,512]{2,1,0:T(8,128)S(1)} %get-tuple-element.34.own_ref, f32[64,8,512]{2,1,0:T(8,128)S(1)} %get-tuple-element.35.table_ref, f32[32,32,128]{2,1,0:T(8,128)S(1)} %collective-permute-done.block_ref, ...), custom_call_target="tpu_custom_call" | custom-call | bytes 6868992 | tf_op jit(solution)/shard_map/mid/pallas_call | solution.py:254
  46.7 0.0 collective-permute-done.1.block_ref
  46.7 0.0 copy-start.6
  46.7 5.5 %far.1 = f32[32,32,128]{2,1,0:T(8,128)} custom-call(s32[72,128]{1,0:T(8,128)S(1)} %get-tuple-element.29.lists_ref, f32[64,8,512]{2,1,0:T(8,128)S(1)} %get-tuple-element.36.mid_ref, f32[129,8,512]{2,1,0:T(8,128)S(1)} %get-tuple-element.37.near_ref, f32[64,8,512]{2,1,0:T(8,128)S(1)} %get-tuple-element.35.table_ref, ...), custom_call_target="tpu_custom_call" | custom-call | bytes 7393280 | tf_op jit(solution)/shard_map/far/pallas_call | solution.py:254
  52.2 3.9 %all-to-all-start.1 = ((f32[32,32,128]{2,1,0:T(8,128)}), f32[32,32,128]{2,1,0:T(8,128)S(1)}, u32[]{:S(2)}, u32[]{:S(2)}) async-start(f32[32,32,128]{2,1,0:T(8,128)} %far.1), calls=%async_computation.1 | async-start | bytes 1048576 | tf_op jit(solution)/shard_map/all_to_all | solution.py:343
  56.1 0.0 collective-permute-done.2.left_ref
  56.1 0.0 collective-permute-done.3.right_ref
  56.2 0.0 copy-start
  56.2 1.7 %copy-done = f32[2,2,9,128,128]{4,3,2,1,0:T(8,128)S(1)} copy-done((f32[2,2,9,128,128]{4,3,2,1,0:T(8,128)S(1)}, f32[2,2,9,128,128]{4,3,2,1,0:T(8,128)}, u32[]{:S(2)}) %copy-start) | copy-done | bytes 2359320
  57.8 6.1 %near.1.near_ref = f32[2,2,128,256]{3,2,1,0:T(8,128)S(1)} custom-call(s32[2,9]{1,0:T(2,128)S(1)} %copy-done.6, f32[2,2,9,128,128]{4,3,2,1,0:T(8,128)S(1)} %copy-done, f32[2,2,128,256]{3,2,1,0:T(8,128)S(1)} %copy-done.1, f32[2,2,128,256]{3,2,1,0:T(8,128)S(1)} %collective-permute-done.2.left_ref, f32[2,2,128,256]{3,2,1,0:T(8,128)S(1)} %collective-permute-done.3.right_ref), custom_call_target="tpu_custom_call" | custom-call | flops 20000000000 | bytes 4456520 | tf_op jit(solution)/shard_map/near/pallas_call | solution.py:254
  64.0 10.3 %all-to-all-done.1.far_ref = f32[32,32,128]{2,1,0:T(8,128)S(1)} async-done(((f32[32,32,128]{2,1,0:T(8,128)}), f32[32,32,128]{2,1,0:T(8,128)S(1)}, u32[]{:S(2)}, u32[]{:S(2)}) %all-to-all-start.1) | async-done | bytes 524320 | tf_op jit(solution)/shard_map/all_to_all | solution.py:343
  74.2 0.9 %join.1 = f32[2,2,128,256]{3,2,1,0:T(8,128)} custom-call(f32[32,32,128]{2,1,0:T(8,128)S(1)} %all-to-all-done.1.far_ref, f32[2,2,128,256]{3,2,1,0:T(8,128)S(1)} %near.1.near_ref), custom_call_target="tpu_custom_call" | custom-call | bytes 1572864 | tf_op jit(solution)/shard_map/join/pallas_call | solution.py:254
  (10 shorter events, 0.0 us)
Async XLA Ops:
  0.0 13.7 %copy-start.2 = (f32[2,256,128]{2,1,0:T(8,128)S(1)}, f32[2,256,128]{2,1,0:T(8,128)}, u32[]{:S(2)}) copy-start(f32[2,256,128]{2,1,0:T(8,128)} %aggregate_ref.1) | copy-start | bytes 786436
  0.0 13.7 %copy-start.3 = (f32[2,128,256]{2,1,0:T(8,128)S(1)}, f32[2,128,256]{2,1,0:T(8,128)}, u32[]{:S(2)}) copy-start(f32[2,128,256]{2,1,0:T(8,128)} %disaggregate_ref.1) | copy-start | bytes 786436
  0.0 13.7 %copy-start.4 = (s32[64,32]{0,1:T(8,128)S(1)}, s32[64,32]{0,1:T(8,128)}, u32[]{:S(2)}) copy-start(s32[64,32]{0,1:T(8,128)} %param.13) | copy-start | bytes 24580
  0.0 13.7 %copy-start.5 = (s32[64,32]{0,1:T(8,128)S(1)}, s32[64,32]{0,1:T(8,128)}, u32[]{:S(2)}) copy-start(s32[64,32]{0,1:T(8,128)} %param.14) | copy-start | bytes 24580
  2.2 31.7 %all-to-all-start = ((f32[32,40,128]{2,1,0:T(8,128)}), f32[32,40,128]{2,1,0:T(8,128)S(1)}, u32[]{:S(2)}, u32[]{:S(2)}) async-start(f32[32,40,128]{2,1,0:T(8,128)} %pack.1), calls=%async_computation | async-start | bytes 1310720 | tf_op jit(solution)/shard_map/all_to_all | solution.py:304
  13.7 22.9 %copy-start.1 = (f32[2,2,128,256]{3,2,1,0:T(8,128)S(1)}, f32[2,2,128,256]{3,2,1,0:T(8,128)}, u32[]{:S(2)}) copy-start(f32[2,2,128,256]{3,2,1,0:T(8,128)} %own_ref.1) | copy-start | bytes 1572868
  33.9 8.7 %collective-permute-start = (f32[32,32,128]{2,1,0:T(8,128)S(1)}, f32[32,32,128]{2,1,0:T(8,128)S(1)}, u32[]{:S(2)}, u32[]{:S(2)}) collective-permute-start(f32[32,32,128]{2,1,0:T(8,128)S(1)} %slice.3), channel_id=1, source_target_pairs={{0,32},{64,96},{128,160},{192,224},{32,0},{96,64},{160,128},{224,1... | collective-permute-start | bytes 1572872 | tf_op jit(solution)/shard_map/ppermute | solution.py:314
  34.0 12.7 %collective-permute-start.1 = (f32[32,32,128]{2,1,0:T(8,128)S(1)}, f32[32,32,128]{2,1,0:T(8,128)S(1)}, u32[]{:S(2)}, u32[]{:S(2)}) collective-permute-start(f32[32,32,128]{2,1,0:T(8,128)S(1)} %slice.3), channel_id=1, source_target_pairs={{32,64},{96,128},{160,192},{64,32},{128,96},{192,160},{33,65},{97,... | collective-permute-start | bytes 1572872 | tf_op jit(solution)/shard_map/ppermute | solution.py:313
  36.6 19.6 %collective-permute-start.2 = (f32[2,2,128,256]{3,2,1,0:T(8,128)S(1)}, f32[2,2,128,256]{3,2,1,0:T(8,128)S(1)}, u32[]{:S(2)}, u32[]{:S(2)}) collective-permute-start(f32[2,2,128,256]{3,2,1,0:T(8,128)S(1)} %copy-done.1), channel_id=1, source_target_pairs={{0,1},{1,2},{2,3},{3,4},{4,5},{5,6},{6,7},{7,8},{8,9},{9,10},{10,1... | collective-permute-start | bytes 1572872 | tf_op jit(solution)/shard_map/ppermute | solution.py:315
  37.9 18.3 %collective-permute-start.3 = (f32[2,2,128,256]{3,2,1,0:T(8,128)S(1)}, f32[2,2,128,256]{3,2,1,0:T(8,128)S(1)}, u32[]{:S(2)}, u32[]{:S(2)}) collective-permute-start(f32[2,2,128,256]{3,2,1,0:T(8,128)S(1)} %copy-done.1), channel_id=1, source_target_pairs={{1,0},{2,1},{3,2},{4,3},{5,4},{6,5},{7,6},{8,7},{9,8},{10,9},{11,1... | collective-permute-start | bytes 1572872 | tf_op jit(solution)/shard_map/ppermute | solution.py:316
  46.7 9.5 %copy-start.6 = (s32[2,9]{1,0:T(2,128)S(1)}, s32[2,9]{1,0:T(2,128)}, u32[]{:S(2)}) copy-start(s32[2,9]{1,0:T(2,128)} %index_ref.1) | copy-start | bytes 220
  52.2 22.0 %all-to-all-start.1 = ((f32[32,32,128]{2,1,0:T(8,128)}), f32[32,32,128]{2,1,0:T(8,128)S(1)}, u32[]{:S(2)}, u32[]{:S(2)}) async-start(f32[32,32,128]{2,1,0:T(8,128)} %far.1), calls=%async_computation.1 | async-start | bytes 1048576 | tf_op jit(solution)/shard_map/all_to_all | solution.py:343
  56.2 1.7 %copy-start = (f32[2,2,9,128,128]{4,3,2,1,0:T(8,128)S(1)}, f32[2,2,9,128,128]{4,3,2,1,0:T(8,128)}, u32[]{:S(2)}) copy-start(f32[2,2,9,128,128]{4,3,2,1,0:T(8,128)} %blocks_ref.1) | copy-start | bytes 7077892

commit v13 on v12

--- a/solution.py
+++ b/solution.py
@@ -312,8 +312,6 @@
     sent = mine[:, :rows]
     from_cross = lax.ppermute(sent, "slab", cross)
     from_same = lax.ppermute(sent, "slab", same)
-    left = lax.ppermute(beside, "dir", ring)
-    right = lax.ppermute(beside, "dir", [(j, i) for i, j in ring])
     field = shape(boxes, own, width)
     radiated, table = call(own_kernel, (field, shape(ops, own, width)), (VMEM,) * 3, micros=0, name="own")(mine, up0, up1)
     staging = (pltpu.SMEM(lists.shape, jnp.int32), pltpu.SemaphoreType.DMA)
@@ -325,6 +323,9 @@
         micros=0,
         name="mid",
     )(early, radiated, table, from_same, up0, up1)
+    partial, beside = lax.optimization_barrier((partial, beside))
+    left = lax.ppermute(beside, "dir", ring)
+    right = lax.ppermute(beside, "dir", [(j, i) for i, j in ring])
     far = call(
         far_kernel,
         shape(devices, rows, unknowns),

time: 75.7 us -> 76.4 us (level)
  waiting for transfers between devices: 29.9 us -> 31.5 us
  starting transfers between devices: 23.4 us -> 22.5 us
    ppermute x1, waiting for transfers between devices: 0.01 us -> 4.02 us  [body(): left = lax.ppermute(beside, 'dir', ring)]
    all_to_all x1, waiting for transfers between devices: 10.3 us -> 6.52 us  [body(): back = lax.all_to_all(far, 'dir', 0, 0, tiled=True)]
    ppermute x1, starting transfers between devices: 4.12 us -> 1.21 us  [body(): right = lax.ppermute(beside, 'dir', [(j, i) for i, j in ring])]
    all_to_all x1, starting transfers between devices: 3.9 us -> 6.26 us  [body(): back = lax.all_to_all(far, 'dir', 0, 0, tiled=True)]
    ppermute x1, waiting for transfers between devices: 0.01 us -> 1.3 us  [body(): from_cross = lax.ppermute(sent, 'slab', cross)]
  transfers between devices with their start and end apart: 6 -> 6, of which waited for: 2 -> 4; matrix products, arithmetic and copies ran while one was open for 0% -> 0% of each run, Pallas kernels for 22% -> 22%
where the time goes in v13:
time: 76.4 us; the launch traced here: 75.7 us
  waiting for transfers between devices  31.5 us (41%)
  starting transfers between devices  22.5 us (29%)
  Pallas kernels  19.9 us (26%)
  local copies, waits for them, and re-layouts  1.74 us (2%)
    pallas_call x7, Pallas kernels, run(): pl.pallas_call(kernel, out_shape=outs, in_specs=specs, out_specs=jax.tree...  19.9 us
    all_to_all x1, waiting for transfers between devices, body(): mine = lax.all_to_all(packed, 'dir', 0, 0, tiled=True)  19.6 us
    all_to_all x1, starting transfers between devices, body(): mine = lax.all_to_all(packed, 'dir', 0, 0, tiled=True)  11.5 us
    all_to_all x1, waiting for transfers between devices, body(): back = lax.all_to_all(far, 'dir', 0, 0, tiled=True)  6.52 us
    all_to_all x1, starting transfers between devices, body(): back = lax.all_to_all(far, 'dir', 0, 0, tiled=True)  6.26 us
    ppermute x1, waiting for transfers between devices, body(): left = lax.ppermute(beside, 'dir', ring)  4.02 us
    ppermute x1, starting transfers between devices, body(): from_cross = lax.ppermute(sent, 'slab', cross)  2.53 us
    unnamed x14, local copies, waits for them, and re-layouts  1.69 us
  transfers between devices with their start and end apart: 6, of which 4 were waited for; matrix products, arithmetic and copies ran while one was open for 0% of the time, Pallas kernels for 22%

profile of v13, /device:TPU:2, one launch (start us, length us, event | category | flops | bytes accessed | tf_op | source)
XLA Modules:
  0.0 75.7 jit_solution(15433683002399679966)
XLA Ops:
  0.0 0.0 copy-start.5
  0.0 2.1 %pack.1 = f32[32,40,128]{2,1,0:T(8,128)} custom-call(f32[2,2,128,256]{3,2,1,0:T(8,128)} %own_ref.1, f32[2,8,64]{2,1,0:T(8,128)} %bitcast.5), custom_call_target="tpu_custom_call" | custom-call | flops 1000000000 | bytes 1183744 | tf_op jit(solution)/shard_map/pack/pallas_call | solution.py:254
  2.2 11.5 %all-to-all-start = ((f32[32,40,128]{2,1,0:T(8,128)}), f32[32,40,128]{2,1,0:T(8,128)S(1)}, u32[]{:S(2)}, u32[]{:S(2)}) async-start(f32[32,40,128]{2,1,0:T(8,128)} %pack.1), calls=%async_computation | async-start | bytes 1310720 | tf_op jit(solution)/shard_map/all_to_all | solution.py:304
  13.7 0.5 plan.1
  14.3 19.6 %all-to-all-done.own_ref = f32[32,40,128]{2,1,0:T(8,128)S(1)} async-done(((f32[32,40,128]{2,1,0:T(8,128)}), f32[32,40,128]{2,1,0:T(8,128)S(1)}, u32[]{:S(2)}, u32[]{:S(2)}) %all-to-all-start) | async-done | bytes 655392 | tf_op jit(solution)/shard_map/all_to_all | solution.py:304
  33.9 0.1 slice.3
  33.9 0.0 copy-start.1
  33.9 0.1 collective-permute-start
  34.0 2.5 %collective-permute-start.1 = (f32[32,32,128]{2,1,0:T(8,128)S(1)}, f32[32,32,128]{2,1,0:T(8,128)S(1)}, u32[]{:S(2)}, u32[]{:S(2)}) collective-permute-start(f32[32,32,128]{2,1,0:T(8,128)S(1)} %slice.3), channel_id=1, source_target_pairs={{32,64},{96,128},{160,192},{64,32},{128,96},{192,160},{33,65},{97,... | collective-permute-start | bytes 1572872 | tf_op jit(solution)/shard_map/ppermute | solution.py:313
  36.6 0.6 own.1
  37.2 0.0 collective-permute-done.block_ref
  37.2 4.0 %mid.1 = (f32[64,8,512]{2,1,0:T(8,128)S(1)}, f32[129,8,512]{2,1,0:T(8,128)S(1)}) custom-call(s32[72,128]{1,0:T(8,128)S(1)} %get-tuple-element.32.lists_ref, f32[64,8,512]{2,1,0:T(8,128)S(1)} %get-tuple-element.36.own_ref, f32[64,8,512]{2,1,0:T(8,128)S(1)} %get-tuple-element.37.table_ref, f32[32,32,128]{2,1,0:T(8,128)S(1)} %collective-permute-done.block_ref, ...), custom_call_target="tpu_custom_call" | custom-call | bytes 6868992 | tf_op jit(solution)/shard_map/mid/pallas_call | solution.py:254
  41.3 0.0 copy-done.1
  41.3 1.2 %collective-permute-start.3 = (f32[2,2,128,256]{3,2,1,0:T(8,128)S(1)}, f32[2,2,128,256]{3,2,1,0:T(8,128)S(1)}, u32[]{:S(2)}, u32[]{:S(2)}) collective-permute-start(f32[2,2,128,256]{3,2,1,0:T(8,128)S(1)} %copy-done.1), channel_id=1, source_target_pairs={{1,0},{2,1},{3,2},{4,3},{5,4},{6,5},{7,6},{8,7},{9,8},{10,9},{11,1... | collective-permute-start | bytes 1572872 | tf_op jit(solution)/shard_map/ppermute | solution.py:328
  42.5 0.9 %collective-permute-start.2 = (f32[2,2,128,256]{3,2,1,0:T(8,128)S(1)}, f32[2,2,128,256]{3,2,1,0:T(8,128)S(1)}, u32[]{:S(2)}, u32[]{:S(2)}) collective-permute-start(f32[2,2,128,256]{3,2,1,0:T(8,128)S(1)} %copy-done.1), channel_id=1, source_target_pairs={{0,1},{1,2},{2,3},{3,4},{4,5},{5,6},{6,7},{7,8},{8,9},{9,10},{10,1... | collective-permute-start | bytes 1572872 | tf_op jit(solution)/shard_map/ppermute | solution.py:327
  43.4 1.3 %collective-permute-done.1.block_ref = f32[32,32,128]{2,1,0:T(8,128)S(1)} collective-permute-done((f32[32,32,128]{2,1,0:T(8,128)S(1)}, f32[32,32,128]{2,1,0:T(8,128)S(1)}, u32[]{:S(2)}, u32[]{:S(2)}) %collective-permute-start.1) | collective-permute-done | bytes 524320 | tf_op jit(solution)/shard_map/ppermute | solution.py:313
  44.7 5.5 %far.1 = f32[32,32,128]{2,1,0:T(8,128)} custom-call(s32[72,128]{1,0:T(8,128)S(1)} %get-tuple-element.31.lists_ref, f32[64,8,512]{2,1,0:T(8,128)S(1)} %get-tuple-element.40.mid_ref, f32[129,8,512]{2,1,0:T(8,128)S(1)} %get-tuple-element.41.near_ref, f32[64,8,512]{2,1,0:T(8,128)S(1)} %get-tuple-element.37.table_ref, ...), custom_call_target="tpu_custom_call" | custom-call | bytes 7393280 | tf_op jit(solution)/shard_map/far/pallas_call | solution.py:254
  50.2 6.3 %all-to-all-start.1 = ((f32[32,32,128]{2,1,0:T(8,128)}), f32[32,32,128]{2,1,0:T(8,128)S(1)}, u32[]{:S(2)}, u32[]{:S(2)}) async-start(f32[32,32,128]{2,1,0:T(8,128)} %far.1), calls=%async_computation.1 | async-start | bytes 1048576 | tf_op jit(solution)/shard_map/all_to_all | solution.py:344
  56.4 0.0 collective-permute-done.3.right_ref
  56.5 4.0 %collective-permute-done.2.left_ref = f32[2,2,128,256]{3,2,1,0:T(8,128)S(1)} collective-permute-done((f32[2,2,128,256]{3,2,1,0:T(8,128)S(1)}, f32[2,2,128,256]{3,2,1,0:T(8,128)S(1)}, u32[]{:S(2)}, u32[]{:S(2)}) %collective-permute-start.2) | collective-permute-done | bytes 524320 | tf_op jit(solution)/shard_map/ppermute | solution.py:327
  60.5 1.7 %copy-done = f32[2,2,9,128,128]{4,3,2,1,0:T(8,128)S(1)} copy-done((f32[2,2,9,128,128]{4,3,2,1,0:T(8,128)S(1)}, f32[2,2,9,128,128]{4,3,2,1,0:T(8,128)}, u32[]{:S(2)}) %copy-start) | copy-done | bytes 2359320
  62.1 6.1 %near.1.near_ref = f32[2,2,128,256]{3,2,1,0:T(8,128)S(1)} custom-call(s32[2,9]{1,0:T(2,128)S(1)} %copy-done.6, f32[2,2,9,128,128]{4,3,2,1,0:T(8,128)S(1)} %copy-done, f32[2,2,128,256]{3,2,1,0:T(8,128)S(1)} %copy-done.1, f32[2,2,128,256]{3,2,1,0:T(8,128)S(1)} %collective-permute-done.2.left_ref, f32[2,2,128,256]{3,2,1,0:T(8,128)S(1)} %collective-permute-done.3.right_ref), custom_call_target="tpu_custom_call" | custom-call | flops 20000000000 | bytes 4456520 | tf_op jit(solution)/shard_map/near/pallas_call | solution.py:254
  68.3 6.5 %all-to-all-done.1.far_ref = f32[32,32,128]{2,1,0:T(8,128)S(1)} async-done(((f32[32,32,128]{2,1,0:T(8,128)}), f32[32,32,128]{2,1,0:T(8,128)S(1)}, u32[]{:S(2)}, u32[]{:S(2)}) %all-to-all-start.1) | async-done | bytes 524320 | tf_op jit(solution)/shard_map/all_to_all | solution.py:344
  74.8 0.9 %join.1 = f32[2,2,128,256]{3,2,1,0:T(8,128)} custom-call(f32[32,32,128]{2,1,0:T(8,128)S(1)} %all-to-all-done.1.far_ref, f32[2,2,128,256]{3,2,1,0:T(8,128)S(1)} %near.1.near_ref), custom_call_target="tpu_custom_call" | custom-call | bytes 1572864 | tf_op jit(solution)/shard_map/join/pallas_call | solution.py:254
  (10 shorter events, 0.0 us)
Async XLA Ops:
  0.0 13.7 %copy-start.2 = (f32[2,256,128]{2,1,0:T(8,128)S(1)}, f32[2,256,128]{2,1,0:T(8,128)}, u32[]{:S(2)}) copy-start(f32[2,256,128]{2,1,0:T(8,128)} %aggregate_ref.1) | copy-start | bytes 786436
  0.0 13.7 %copy-start.3 = (f32[2,128,256]{2,1,0:T(8,128)S(1)}, f32[2,128,256]{2,1,0:T(8,128)}, u32[]{:S(2)}) copy-start(f32[2,128,256]{2,1,0:T(8,128)} %disaggregate_ref.1) | copy-start | bytes 786436
  0.0 13.7 %copy-start.4 = (s32[64,32]{0,1:T(8,128)S(1)}, s32[64,32]{0,1:T(8,128)}, u32[]{:S(2)}) copy-start(s32[64,32]{0,1:T(8,128)} %param.13) | copy-start | bytes 24580
  0.0 13.7 %copy-start.5 = (s32[64,32]{0,1:T(8,128)S(1)}, s32[64,32]{0,1:T(8,128)}, u32[]{:S(2)}) copy-start(s32[64,32]{0,1:T(8,128)} %param.14) | copy-start | bytes 24580
  2.2 31.7 %all-to-all-start = ((f32[32,40,128]{2,1,0:T(8,128)}), f32[32,40,128]{2,1,0:T(8,128)S(1)}, u32[]{:S(2)}, u32[]{:S(2)}) async-start(f32[32,40,128]{2,1,0:T(8,128)} %pack.1), calls=%async_computation | async-start | bytes 1310720 | tf_op jit(solution)/shard_map/all_to_all | solution.py:304
  33.9 7.3 %copy-start.1 = (f32[2,2,128,256]{3,2,1,0:T(8,128)S(1)}, f32[2,2,128,256]{3,2,1,0:T(8,128)}, u32[]{:S(2)}) copy-start(f32[2,2,128,256]{3,2,1,0:T(8,128)} %own_ref.1) | copy-start | bytes 1572868
  33.9 3.3 %collective-permute-start = (f32[32,32,128]{2,1,0:T(8,128)S(1)}, f32[32,32,128]{2,1,0:T(8,128)S(1)}, u32[]{:S(2)}, u32[]{:S(2)}) collective-permute-start(f32[32,32,128]{2,1,0:T(8,128)S(1)} %slice.3), channel_id=1, source_target_pairs={{0,32},{64,96},{128,160},{192,224},{32,0},{96,64},{160,128},{224,1... | collective-permute-start | bytes 1572872 | tf_op jit(solution)/shard_map/ppermute | solution.py:314
  34.0 10.6 %collective-permute-start.1 = (f32[32,32,128]{2,1,0:T(8,128)S(1)}, f32[32,32,128]{2,1,0:T(8,128)S(1)}, u32[]{:S(2)}, u32[]{:S(2)}) collective-permute-start(f32[32,32,128]{2,1,0:T(8,128)S(1)} %slice.3), channel_id=1, source_target_pairs={{32,64},{96,128},{160,192},{64,32},{128,96},{192,160},{33,65},{97,... | collective-permute-start | bytes 1572872 | tf_op jit(solution)/shard_map/ppermute | solution.py:313
  41.3 15.2 %collective-permute-start.3 = (f32[2,2,128,256]{3,2,1,0:T(8,128)S(1)}, f32[2,2,128,256]{3,2,1,0:T(8,128)S(1)}, u32[]{:S(2)}, u32[]{:S(2)}) collective-permute-start(f32[2,2,128,256]{3,2,1,0:T(8,128)S(1)} %copy-done.1), channel_id=1, source_target_pairs={{1,0},{2,1},{3,2},{4,3},{5,4},{6,5},{7,6},{8,7},{9,8},{10,9},{11,1... | collective-permute-start | bytes 1572872 | tf_op jit(solution)/shard_map/ppermute | solution.py:328
  42.5 18.0 %collective-permute-start.2 = (f32[2,2,128,256]{3,2,1,0:T(8,128)S(1)}, f32[2,2,128,256]{3,2,1,0:T(8,128)S(1)}, u32[]{:S(2)}, u32[]{:S(2)}) collective-permute-start(f32[2,2,128,256]{3,2,1,0:T(8,128)S(1)} %copy-done.1), channel_id=1, source_target_pairs={{0,1},{1,2},{2,3},{3,4},{4,5},{5,6},{6,7},{7,8},{8,9},{9,10},{10,1... | collective-permute-start | bytes 1572872 | tf_op jit(solution)/shard_map/ppermute | solution.py:327
  44.7 15.8 %copy-start.6 = (s32[2,9]{1,0:T(2,128)S(1)}, s32[2,9]{1,0:T(2,128)}, u32[]{:S(2)}) copy-start(s32[2,9]{1,0:T(2,128)} %index_ref.1) | copy-start | bytes 220
  50.2 24.6 %all-to-all-start.1 = ((f32[32,32,128]{2,1,0:T(8,128)}), f32[32,32,128]{2,1,0:T(8,128)S(1)}, u32[]{:S(2)}, u32[]{:S(2)}) async-start(f32[32,32,128]{2,1,0:T(8,128)} %far.1), calls=%async_computation.1 | async-start | bytes 1048576 | tf_op jit(solution)/shard_map/all_to_all | solution.py:344
  60.5 1.7 %copy-start = (f32[2,2,9,128,128]{4,3,2,1,0:T(8,128)S(1)}, f32[2,2,9,128,128]{4,3,2,1,0:T(8,128)}, u32[]{:S(2)}) copy-start(f32[2,2,9,128,128]{4,3,2,1,0:T(8,128)} %blocks_ref.1) | copy-start | bytes 7077892

commit v14 on v12

--- a/solution.py
+++ b/solution.py
@@ -172,7 +172,7 @@
         out_ref[g, :, :half], out_ref[g, :, half:] = total
         return carry
 
-    lax.fori_loop(0, out_ref.shape[0], one_box, 0, unroll=4)
+    lax.fori_loop(0, out_ref.shape[0], one_box, 0, unroll=8)
 
 
 def mid_kernel(

time: 75.7 us -> 75.7 us (level)
  no operation moved by 1% of the time
where the time goes in v14:
time: 75.7 us; the launch traced here: 75.2 us
  waiting for transfers between devices  30 us (40%)
  starting transfers between devices  23.4 us (31%)
  Pallas kernels  19.7 us (26%)
  local copies, waits for them, and re-layouts  1.74 us (2%)
    pallas_call x7, Pallas kernels, run(): pl.pallas_call(kernel, out_shape=outs, in_specs=specs, out_specs=jax.tree...  19.7 us
    all_to_all x1, waiting for transfers between devices, body(): mine = lax.all_to_all(packed, 'dir', 0, 0, tiled=True)  19.6 us
    all_to_all x1, starting transfers between devices, body(): mine = lax.all_to_all(packed, 'dir', 0, 0, tiled=True)  11.5 us
    all_to_all x1, waiting for transfers between devices, body(): back = lax.all_to_all(far, 'dir', 0, 0, tiled=True)  10.4 us
    ppermute x1, starting transfers between devices, body(): right = lax.ppermute(beside, 'dir', [(j, i) for i, j in ring])  4.12 us
    all_to_all x1, starting transfers between devices, body(): back = lax.all_to_all(far, 'dir', 0, 0, tiled=True)  3.9 us
    ppermute x1, starting transfers between devices, body(): from_cross = lax.ppermute(sent, 'slab', cross)  2.53 us
    unnamed x14, local copies, waits for them, and re-layouts  1.69 us
  transfers between devices with their start and end apart: 6, of which 2 were waited for; matrix products, arithmetic and copies ran while one was open for 0% of the time, Pallas kernels for 22%

profile of v14, /device:TPU:2, one launch (start us, length us, event | category | flops | bytes accessed | tf_op | source)
XLA Modules:
  0.0 75.2 jit_solution(6405386068683641649)
XLA Ops:
  0.0 2.1 %pack.1 = f32[32,40,128]{2,1,0:T(8,128)} custom-call(f32[2,2,128,256]{3,2,1,0:T(8,128)} %own_ref.1, f32[2,8,64]{2,1,0:T(8,128)} %bitcast.5), custom_call_target="tpu_custom_call" | custom-call | flops 1000000000 | bytes 1183744 | tf_op jit(solution)/shard_map/pack/pallas_call | solution.py:254
  2.2 11.5 %all-to-all-start = ((f32[32,40,128]{2,1,0:T(8,128)}), f32[32,40,128]{2,1,0:T(8,128)S(1)}, u32[]{:S(2)}, u32[]{:S(2)}) async-start(f32[32,40,128]{2,1,0:T(8,128)} %pack.1), calls=%async_computation | async-start | bytes 1310720 | tf_op jit(solution)/shard_map/all_to_all | solution.py:304
  13.7 0.0 copy-start.1
  13.7 0.5 plan.1
  14.3 19.6 %all-to-all-done.own_ref = f32[32,40,128]{2,1,0:T(8,128)S(1)} async-done(((f32[32,40,128]{2,1,0:T(8,128)}), f32[32,40,128]{2,1,0:T(8,128)S(1)}, u32[]{:S(2)}, u32[]{:S(2)}) %all-to-all-start) | async-done | bytes 655392 | tf_op jit(solution)/shard_map/all_to_all | solution.py:304
  33.9 0.1 slice.3
  33.9 0.1 collective-permute-start
  34.0 2.5 %collective-permute-start.1 = (f32[32,32,128]{2,1,0:T(8,128)S(1)}, f32[32,32,128]{2,1,0:T(8,128)S(1)}, u32[]{:S(2)}, u32[]{:S(2)}) collective-permute-start(f32[32,32,128]{2,1,0:T(8,128)S(1)} %slice.3), channel_id=1, source_target_pairs={{32,64},{96,128},{160,192},{64,32},{128,96},{192,160},{33,65},{97,... | collective-permute-start | bytes 1572872 | tf_op jit(solution)/shard_map/ppermute | solution.py:313
  36.6 1.3 %collective-permute-start.2 = (f32[2,2,128,256]{3,2,1,0:T(8,128)S(1)}, f32[2,2,128,256]{3,2,1,0:T(8,128)S(1)}, u32[]{:S(2)}, u32[]{:S(2)}) collective-permute-start(f32[2,2,128,256]{3,2,1,0:T(8,128)S(1)} %copy-done.1), channel_id=1, source_target_pairs={{0,1},{1,2},{2,3},{3,4},{4,5},{5,6},{6,7},{7,8},{8,9},{9,10},{10,1... | collective-permute-start | bytes 1572872 | tf_op jit(solution)/shard_map/ppermute | solution.py:315
  37.9 4.1 %collective-permute-start.3 = (f32[2,2,128,256]{3,2,1,0:T(8,128)S(1)}, f32[2,2,128,256]{3,2,1,0:T(8,128)S(1)}, u32[]{:S(2)}, u32[]{:S(2)}) collective-permute-start(f32[2,2,128,256]{3,2,1,0:T(8,128)S(1)} %copy-done.1), channel_id=1, source_target_pairs={{1,0},{2,1},{3,2},{4,3},{5,4},{6,5},{7,6},{8,7},{9,8},{10,9},{11,1... | collective-permute-start | bytes 1572872 | tf_op jit(solution)/shard_map/ppermute | solution.py:316
  42.0 0.6 own.1
  42.7 0.0 collective-permute-done.block_ref
  42.7 4.0 %mid.1 = (f32[64,8,512]{2,1,0:T(8,128)S(1)}, f32[129,8,512]{2,1,0:T(8,128)S(1)}) custom-call(s32[72,128]{1,0:T(8,128)S(1)} %get-tuple-element.30.lists_ref, f32[64,8,512]{2,1,0:T(8,128)S(1)} %get-tuple-element.34.own_ref, f32[64,8,512]{2,1,0:T(8,128)S(1)} %get-tuple-element.35.table_ref, f32[32,32,128]{2,1,0:T(8,128)S(1)} %collective-permute-done.block_ref, ...), custom_call_target="tpu_custom_call" | custom-call | bytes 6868992 | tf_op jit(solution)/shard_map/mid/pallas_call | solution.py:254
  46.6 0.0 collective-permute-done.1.block_ref
  46.6 0.0 copy-start.6
  46.6 5.4 %far.1 = f32[32,32,128]{2,1,0:T(8,128)} custom-call(s32[72,128]{1,0:T(8,128)S(1)} %get-tuple-element.29.lists_ref, f32[64,8,512]{2,1,0:T(8,128)S(1)} %get-tuple-element.36.mid_ref, f32[129,8,512]{2,1,0:T(8,128)S(1)} %get-tuple-element.37.near_ref, f32[64,8,512]{2,1,0:T(8,128)S(1)} %get-tuple-element.35.table_ref, ...), custom_call_target="tpu_custom_call" | custom-call | bytes 7393280 | tf_op jit(solution)/shard_map/far/pallas_call | solution.py:254
  52.1 3.9 %all-to-all-start.1 = ((f32[32,32,128]{2,1,0:T(8,128)}), f32[32,32,128]{2,1,0:T(8,128)S(1)}, u32[]{:S(2)}, u32[]{:S(2)}) async-start(f32[32,32,128]{2,1,0:T(8,128)} %far.1), calls=%async_computation.1 | async-start | bytes 1048576 | tf_op jit(solution)/shard_map/all_to_all | solution.py:343
  56.0 0.0 collective-permute-done.2.left_ref
  56.0 0.0 collective-permute-done.3.right_ref
  56.0 0.0 copy-start
  56.0 1.7 %copy-done = f32[2,2,9,128,128]{4,3,2,1,0:T(8,128)S(1)} copy-done((f32[2,2,9,128,128]{4,3,2,1,0:T(8,128)S(1)}, f32[2,2,9,128,128]{4,3,2,1,0:T(8,128)}, u32[]{:S(2)}) %copy-start) | copy-done | bytes 2359320
  57.7 6.1 %near.1.near_ref = f32[2,2,128,256]{3,2,1,0:T(8,128)S(1)} custom-call(s32[2,9]{1,0:T(2,128)S(1)} %copy-done.6, f32[2,2,9,128,128]{4,3,2,1,0:T(8,128)S(1)} %copy-done, f32[2,2,128,256]{3,2,1,0:T(8,128)S(1)} %copy-done.1, f32[2,2,128,256]{3,2,1,0:T(8,128)S(1)} %collective-permute-done.2.left_ref, f32[2,2,128,256]{3,2,1,0:T(8,128)S(1)} %collective-permute-done.3.right_ref), custom_call_target="tpu_custom_call" | custom-call | flops 20000000000 | bytes 4456520 | tf_op jit(solution)/shard_map/near/pallas_call | solution.py:254
  63.8 10.4 %all-to-all-done.1.far_ref = f32[32,32,128]{2,1,0:T(8,128)S(1)} async-done(((f32[32,32,128]{2,1,0:T(8,128)}), f32[32,32,128]{2,1,0:T(8,128)S(1)}, u32[]{:S(2)}, u32[]{:S(2)}) %all-to-all-start.1) | async-done | bytes 524320 | tf_op jit(solution)/shard_map/all_to_all | solution.py:343
  74.2 0.9 %join.1 = f32[2,2,128,256]{3,2,1,0:T(8,128)} custom-call(f32[32,32,128]{2,1,0:T(8,128)S(1)} %all-to-all-done.1.far_ref, f32[2,2,128,256]{3,2,1,0:T(8,128)S(1)} %near.1.near_ref), custom_call_target="tpu_custom_call" | custom-call | bytes 1572864 | tf_op jit(solution)/shard_map/join/pallas_call | solution.py:254
  (10 shorter events, 0.0 us)
Async XLA Ops:
  0.0 13.7 %copy-start.2 = (f32[2,256,128]{2,1,0:T(8,128)S(1)}, f32[2,256,128]{2,1,0:T(8,128)}, u32[]{:S(2)}) copy-start(f32[2,256,128]{2,1,0:T(8,128)} %aggregate_ref.1) | copy-start | bytes 786436
  0.0 13.7 %copy-start.3 = (f32[2,128,256]{2,1,0:T(8,128)S(1)}, f32[2,128,256]{2,1,0:T(8,128)}, u32[]{:S(2)}) copy-start(f32[2,128,256]{2,1,0:T(8,128)} %disaggregate_ref.1) | copy-start | bytes 786436
  0.0 13.7 %copy-start.4 = (s32[64,32]{0,1:T(8,128)S(1)}, s32[64,32]{0,1:T(8,128)}, u32[]{:S(2)}) copy-start(s32[64,32]{0,1:T(8,128)} %param.13) | copy-start | bytes 24580
  0.0 13.7 %copy-start.5 = (s32[64,32]{0,1:T(8,128)S(1)}, s32[64,32]{0,1:T(8,128)}, u32[]{:S(2)}) copy-start(s32[64,32]{0,1:T(8,128)} %param.14) | copy-start | bytes 24580
  2.2 31.7 %all-to-all-start = ((f32[32,40,128]{2,1,0:T(8,128)}), f32[32,40,128]{2,1,0:T(8,128)S(1)}, u32[]{:S(2)}, u32[]{:S(2)}) async-start(f32[32,40,128]{2,1,0:T(8,128)} %pack.1), calls=%async_computation | async-start | bytes 1310720 | tf_op jit(solution)/shard_map/all_to_all | solution.py:304
  13.7 22.9 %copy-start.1 = (f32[2,2,128,256]{3,2,1,0:T(8,128)S(1)}, f32[2,2,128,256]{3,2,1,0:T(8,128)}, u32[]{:S(2)}) copy-start(f32[2,2,128,256]{3,2,1,0:T(8,128)} %own_ref.1) | copy-start | bytes 1572868
  33.9 8.7 %collective-permute-start = (f32[32,32,128]{2,1,0:T(8,128)S(1)}, f32[32,32,128]{2,1,0:T(8,128)S(1)}, u32[]{:S(2)}, u32[]{:S(2)}) collective-permute-start(f32[32,32,128]{2,1,0:T(8,128)S(1)} %slice.3), channel_id=1, source_target_pairs={{0,32},{64,96},{128,160},{192,224},{32,0},{96,64},{160,128},{224,1... | collective-permute-start | bytes 1572872 | tf_op jit(solution)/shard_map/ppermute | solution.py:314
  34.0 12.6 %collective-permute-start.1 = (f32[32,32,128]{2,1,0:T(8,128)S(1)}, f32[32,32,128]{2,1,0:T(8,128)S(1)}, u32[]{:S(2)}, u32[]{:S(2)}) collective-permute-start(f32[32,32,128]{2,1,0:T(8,128)S(1)} %slice.3), channel_id=1, source_target_pairs={{32,64},{96,128},{160,192},{64,32},{128,96},{192,160},{33,65},{97,... | collective-permute-start | bytes 1572872 | tf_op jit(solution)/shard_map/ppermute | solution.py:313
  36.6 19.4 %collective-permute-start.2 = (f32[2,2,128,256]{3,2,1,0:T(8,128)S(1)}, f32[2,2,128,256]{3,2,1,0:T(8,128)S(1)}, u32[]{:S(2)}, u32[]{:S(2)}) collective-permute-start(f32[2,2,128,256]{3,2,1,0:T(8,128)S(1)} %copy-done.1), channel_id=1, source_target_pairs={{0,1},{1,2},{2,3},{3,4},{4,5},{5,6},{6,7},{7,8},{8,9},{9,10},{10,1... | collective-permute-start | bytes 1572872 | tf_op jit(solution)/shard_map/ppermute | solution.py:315
  37.9 18.1 %collective-permute-start.3 = (f32[2,2,128,256]{3,2,1,0:T(8,128)S(1)}, f32[2,2,128,256]{3,2,1,0:T(8,128)S(1)}, u32[]{:S(2)}, u32[]{:S(2)}) collective-permute-start(f32[2,2,128,256]{3,2,1,0:T(8,128)S(1)} %copy-done.1), channel_id=1, source_target_pairs={{1,0},{2,1},{3,2},{4,3},{5,4},{6,5},{7,6},{8,7},{9,8},{10,9},{11,1... | collective-permute-start | bytes 1572872 | tf_op jit(solution)/shard_map/ppermute | solution.py:316
  46.6 9.4 %copy-start.6 = (s32[2,9]{1,0:T(2,128)S(1)}, s32[2,9]{1,0:T(2,128)}, u32[]{:S(2)}) copy-start(s32[2,9]{1,0:T(2,128)} %index_ref.1) | copy-start | bytes 220
  52.1 22.2 %all-to-all-start.1 = ((f32[32,32,128]{2,1,0:T(8,128)}), f32[32,32,128]{2,1,0:T(8,128)S(1)}, u32[]{:S(2)}, u32[]{:S(2)}) async-start(f32[32,32,128]{2,1,0:T(8,128)} %far.1), calls=%async_computation.1 | async-start | bytes 1048576 | tf_op jit(solution)/shard_map/all_to_all | solution.py:343
  56.0 1.7 %copy-start = (f32[2,2,9,128,128]{4,3,2,1,0:T(8,128)S(1)}, f32[2,2,9,128,128]{4,3,2,1,0:T(8,128)}, u32[]{:S(2)}) copy-start(f32[2,2,9,128,128]{4,3,2,1,0:T(8,128)} %blocks_ref.1) | copy-start | bytes 7077892

commit v15 on v14

--- a/solution.py
+++ b/solution.py
@@ -13,7 +13,7 @@
 ANY = pl.ANY
 MIB = 1 << 20
 RE_IM_ROWS = 32
-FIRST = 16
+FIRST = 17
 PARTS = 2
 LIST_ROWS = 8
 FULL = 63

time: 75.7 us -> 75.9 us (level)
  no operation moved by 1% of the time
where the time goes in v15:
time: 75.9 us; the launch traced here: 75.6 us
  waiting for transfers between devices  30.3 us (40%)
  starting transfers between devices  23.4 us (31%)
  Pallas kernels  19.9 us (26%)
  local copies, waits for them, and re-layouts  1.74 us (2%)
    pallas_call x7, Pallas kernels, run(): pl.pallas_call(kernel, out_shape=outs, in_specs=specs, out_specs=jax.tree...  19.9 us
    all_to_all x1, waiting for transfers between devices, body(): mine = lax.all_to_all(packed, 'dir', 0, 0, tiled=True)  19.6 us
    all_to_all x1, starting transfers between devices, body(): mine = lax.all_to_all(packed, 'dir', 0, 0, tiled=True)  11.5 us
    all_to_all x1, waiting for transfers between devices, body(): back = lax.all_to_all(far, 'dir', 0, 0, tiled=True)  10.7 us
    ppermute x1, starting transfers between devices, body(): right = lax.ppermute(beside, 'dir', [(j, i) for i, j in ring])  4.12 us
    all_to_all x1, starting transfers between devices, body(): back = lax.all_to_all(far, 'dir', 0, 0, tiled=True)  3.9 us
    ppermute x1, starting transfers between devices, body(): from_cross = lax.ppermute(sent, 'slab', cross)  2.53 us
    unnamed x14, local copies, waits for them, and re-layouts  1.69 us
  transfers between devices with their start and end apart: 6, of which 2 were waited for; matrix products, arithmetic and copies ran while one was open for 0% of the time, Pallas kernels for 22%

profile of v15, /device:TPU:2, one launch (start us, length us, event | category | flops | bytes accessed | tf_op | source)
XLA Modules:
  0.0 75.6 jit_solution(14857619648081471166)
XLA Ops:
  0.0 2.1 %pack.1 = f32[32,40,128]{2,1,0:T(8,128)} custom-call(f32[2,2,128,256]{3,2,1,0:T(8,128)} %own_ref.1, f32[2,8,64]{2,1,0:T(8,128)} %bitcast.5), custom_call_target="tpu_custom_call" | custom-call | flops 1000000000 | bytes 1183744 | tf_op jit(solution)/shard_map/pack/pallas_call | solution.py:254
  2.2 11.5 %all-to-all-start = ((f32[32,40,128]{2,1,0:T(8,128)}), f32[32,40,128]{2,1,0:T(8,128)S(1)}, u32[]{:S(2)}, u32[]{:S(2)}) async-start(f32[32,40,128]{2,1,0:T(8,128)} %pack.1), calls=%async_computation | async-start | bytes 1310720 | tf_op jit(solution)/shard_map/all_to_all | solution.py:304
  13.7 0.0 copy-start.1
  13.7 0.5 plan.1
  14.3 19.6 %all-to-all-done.own_ref = f32[32,40,128]{2,1,0:T(8,128)S(1)} async-done(((f32[32,40,128]{2,1,0:T(8,128)}), f32[32,40,128]{2,1,0:T(8,128)S(1)}, u32[]{:S(2)}, u32[]{:S(2)}) %all-to-all-start) | async-done | bytes 655392 | tf_op jit(solution)/shard_map/all_to_all | solution.py:304
  33.9 0.1 slice.3
  33.9 0.1 collective-permute-start
  34.0 2.5 %collective-permute-start.1 = (f32[32,32,128]{2,1,0:T(8,128)S(1)}, f32[32,32,128]{2,1,0:T(8,128)S(1)}, u32[]{:S(2)}, u32[]{:S(2)}) collective-permute-start(f32[32,32,128]{2,1,0:T(8,128)S(1)} %slice.3), channel_id=1, source_target_pairs={{32,64},{96,128},{160,192},{64,32},{128,96},{192,160},{33,65},{97,... | collective-permute-start | bytes 1572872 | tf_op jit(solution)/shard_map/ppermute | solution.py:313
  36.6 1.3 %collective-permute-start.2 = (f32[2,2,128,256]{3,2,1,0:T(8,128)S(1)}, f32[2,2,128,256]{3,2,1,0:T(8,128)S(1)}, u32[]{:S(2)}, u32[]{:S(2)}) collective-permute-start(f32[2,2,128,256]{3,2,1,0:T(8,128)S(1)} %copy-done.1), channel_id=1, source_target_pairs={{0,1},{1,2},{2,3},{3,4},{4,5},{5,6},{6,7},{7,8},{8,9},{9,10},{10,1... | collective-permute-start | bytes 1572872 | tf_op jit(solution)/shard_map/ppermute | solution.py:315
  37.9 4.1 %collective-permute-start.3 = (f32[2,2,128,256]{3,2,1,0:T(8,128)S(1)}, f32[2,2,128,256]{3,2,1,0:T(8,128)S(1)}, u32[]{:S(2)}, u32[]{:S(2)}) collective-permute-start(f32[2,2,128,256]{3,2,1,0:T(8,128)S(1)} %copy-done.1), channel_id=1, source_target_pairs={{1,0},{2,1},{3,2},{4,3},{5,4},{6,5},{7,6},{8,7},{9,8},{10,9},{11,1... | collective-permute-start | bytes 1572872 | tf_op jit(solution)/shard_map/ppermute | solution.py:316
  42.0 0.6 own.1
  42.7 0.0 collective-permute-done.block_ref
  42.7 4.1 %mid.1 = (f32[64,8,512]{2,1,0:T(8,128)S(1)}, f32[129,8,512]{2,1,0:T(8,128)S(1)}) custom-call(s32[72,128]{1,0:T(8,128)S(1)} %get-tuple-element.30.lists_ref, f32[64,8,512]{2,1,0:T(8,128)S(1)} %get-tuple-element.34.own_ref, f32[64,8,512]{2,1,0:T(8,128)S(1)} %get-tuple-element.35.table_ref, f32[32,32,128]{2,1,0:T(8,128)S(1)} %collective-permute-done.block_ref, ...), custom_call_target="tpu_custom_call" | custom-call | bytes 6868992 | tf_op jit(solution)/shard_map/mid/pallas_call | solution.py:254
  46.8 0.0 collective-permute-done.1.block_ref
  46.8 0.0 copy-start.6
  46.8 5.5 %far.1 = f32[32,32,128]{2,1,0:T(8,128)} custom-call(s32[72,128]{1,0:T(8,128)S(1)} %get-tuple-element.29.lists_ref, f32[64,8,512]{2,1,0:T(8,128)S(1)} %get-tuple-element.36.mid_ref, f32[129,8,512]{2,1,0:T(8,128)S(1)} %get-tuple-element.37.near_ref, f32[64,8,512]{2,1,0:T(8,128)S(1)} %get-tuple-element.35.table_ref, ...), custom_call_target="tpu_custom_call" | custom-call | bytes 7393280 | tf_op jit(solution)/shard_map/far/pallas_call | solution.py:254
  52.3 3.9 %all-to-all-start.1 = ((f32[32,32,128]{2,1,0:T(8,128)}), f32[32,32,128]{2,1,0:T(8,128)S(1)}, u32[]{:S(2)}, u32[]{:S(2)}) async-start(f32[32,32,128]{2,1,0:T(8,128)} %far.1), calls=%async_computation.1 | async-start | bytes 1048576 | tf_op jit(solution)/shard_map/all_to_all | solution.py:343
  56.2 0.0 collective-permute-done.2.left_ref
  56.2 0.0 collective-permute-done.3.right_ref
  56.2 0.0 copy-start
  56.2 1.7 %copy-done = f32[2,2,9,128,128]{4,3,2,1,0:T(8,128)S(1)} copy-done((f32[2,2,9,128,128]{4,3,2,1,0:T(8,128)S(1)}, f32[2,2,9,128,128]{4,3,2,1,0:T(8,128)}, u32[]{:S(2)}) %copy-start) | copy-done | bytes 2359320
  57.9 6.1 %near.1.near_ref = f32[2,2,128,256]{3,2,1,0:T(8,128)S(1)} custom-call(s32[2,9]{1,0:T(2,128)S(1)} %copy-done.6, f32[2,2,9,128,128]{4,3,2,1,0:T(8,128)S(1)} %copy-done, f32[2,2,128,256]{3,2,1,0:T(8,128)S(1)} %copy-done.1, f32[2,2,128,256]{3,2,1,0:T(8,128)S(1)} %collective-permute-done.2.left_ref, f32[2,2,128,256]{3,2,1,0:T(8,128)S(1)} %collective-permute-done.3.right_ref), custom_call_target="tpu_custom_call" | custom-call | flops 20000000000 | bytes 4456520 | tf_op jit(solution)/shard_map/near/pallas_call | solution.py:254
  64.0 10.7 %all-to-all-done.1.far_ref = f32[32,32,128]{2,1,0:T(8,128)S(1)} async-done(((f32[32,32,128]{2,1,0:T(8,128)}), f32[32,32,128]{2,1,0:T(8,128)S(1)}, u32[]{:S(2)}, u32[]{:S(2)}) %all-to-all-start.1) | async-done | bytes 524320 | tf_op jit(solution)/shard_map/all_to_all | solution.py:343
  74.7 0.9 %join.1 = f32[2,2,128,256]{3,2,1,0:T(8,128)} custom-call(f32[32,32,128]{2,1,0:T(8,128)S(1)} %all-to-all-done.1.far_ref, f32[2,2,128,256]{3,2,1,0:T(8,128)S(1)} %near.1.near_ref), custom_call_target="tpu_custom_call" | custom-call | bytes 1572864 | tf_op jit(solution)/shard_map/join/pallas_call | solution.py:254
  (10 shorter events, 0.0 us)
Async XLA Ops:
  0.0 13.7 %copy-start.2 = (f32[2,256,128]{2,1,0:T(8,128)S(1)}, f32[2,256,128]{2,1,0:T(8,128)}, u32[]{:S(2)}) copy-start(f32[2,256,128]{2,1,0:T(8,128)} %aggregate_ref.1) | copy-start | bytes 786436
  0.0 13.7 %copy-start.3 = (f32[2,128,256]{2,1,0:T(8,128)S(1)}, f32[2,128,256]{2,1,0:T(8,128)}, u32[]{:S(2)}) copy-start(f32[2,128,256]{2,1,0:T(8,128)} %disaggregate_ref.1) | copy-start | bytes 786436
  0.0 13.7 %copy-start.4 = (s32[64,32]{0,1:T(8,128)S(1)}, s32[64,32]{0,1:T(8,128)}, u32[]{:S(2)}) copy-start(s32[64,32]{0,1:T(8,128)} %param.13) | copy-start | bytes 24580
  0.0 13.7 %copy-start.5 = (s32[64,32]{0,1:T(8,128)S(1)}, s32[64,32]{0,1:T(8,128)}, u32[]{:S(2)}) copy-start(s32[64,32]{0,1:T(8,128)} %param.14) | copy-start | bytes 24580
  2.2 31.7 %all-to-all-start = ((f32[32,40,128]{2,1,0:T(8,128)}), f32[32,40,128]{2,1,0:T(8,128)S(1)}, u32[]{:S(2)}, u32[]{:S(2)}) async-start(f32[32,40,128]{2,1,0:T(8,128)} %pack.1), calls=%async_computation | async-start | bytes 1310720 | tf_op jit(solution)/shard_map/all_to_all | solution.py:304
  13.7 22.9 %copy-start.1 = (f32[2,2,128,256]{3,2,1,0:T(8,128)S(1)}, f32[2,2,128,256]{3,2,1,0:T(8,128)}, u32[]{:S(2)}) copy-start(f32[2,2,128,256]{3,2,1,0:T(8,128)} %own_ref.1) | copy-start | bytes 1572868
  33.9 8.7 %collective-permute-start = (f32[32,32,128]{2,1,0:T(8,128)S(1)}, f32[32,32,128]{2,1,0:T(8,128)S(1)}, u32[]{:S(2)}, u32[]{:S(2)}) collective-permute-start(f32[32,32,128]{2,1,0:T(8,128)S(1)} %slice.3), channel_id=1, source_target_pairs={{0,32},{64,96},{128,160},{192,224},{32,0},{96,64},{160,128},{224,1... | collective-permute-start | bytes 1572872 | tf_op jit(solution)/shard_map/ppermute | solution.py:314
  34.0 12.8 %collective-permute-start.1 = (f32[32,32,128]{2,1,0:T(8,128)S(1)}, f32[32,32,128]{2,1,0:T(8,128)S(1)}, u32[]{:S(2)}, u32[]{:S(2)}) collective-permute-start(f32[32,32,128]{2,1,0:T(8,128)S(1)} %slice.3), channel_id=1, source_target_pairs={{32,64},{96,128},{160,192},{64,32},{128,96},{192,160},{33,65},{97,... | collective-permute-start | bytes 1572872 | tf_op jit(solution)/shard_map/ppermute | solution.py:313
  36.6 19.6 %collective-permute-start.2 = (f32[2,2,128,256]{3,2,1,0:T(8,128)S(1)}, f32[2,2,128,256]{3,2,1,0:T(8,128)S(1)}, u32[]{:S(2)}, u32[]{:S(2)}) collective-permute-start(f32[2,2,128,256]{3,2,1,0:T(8,128)S(1)} %copy-done.1), channel_id=1, source_target_pairs={{0,1},{1,2},{2,3},{3,4},{4,5},{5,6},{6,7},{7,8},{8,9},{9,10},{10,1... | collective-permute-start | bytes 1572872 | tf_op jit(solution)/shard_map/ppermute | solution.py:315
  37.9 18.3 %collective-permute-start.3 = (f32[2,2,128,256]{3,2,1,0:T(8,128)S(1)}, f32[2,2,128,256]{3,2,1,0:T(8,128)S(1)}, u32[]{:S(2)}, u32[]{:S(2)}) collective-permute-start(f32[2,2,128,256]{3,2,1,0:T(8,128)S(1)} %copy-done.1), channel_id=1, source_target_pairs={{1,0},{2,1},{3,2},{4,3},{5,4},{6,5},{7,6},{8,7},{9,8},{10,9},{11,1... | collective-permute-start | bytes 1572872 | tf_op jit(solution)/shard_map/ppermute | solution.py:316
  46.8 9.4 %copy-start.6 = (s32[2,9]{1,0:T(2,128)S(1)}, s32[2,9]{1,0:T(2,128)}, u32[]{:S(2)}) copy-start(s32[2,9]{1,0:T(2,128)} %index_ref.1) | copy-start | bytes 220
  52.3 22.4 %all-to-all-start.1 = ((f32[32,32,128]{2,1,0:T(8,128)}), f32[32,32,128]{2,1,0:T(8,128)S(1)}, u32[]{:S(2)}, u32[]{:S(2)}) async-start(f32[32,32,128]{2,1,0:T(8,128)} %far.1), calls=%async_computation.1 | async-start | bytes 1048576 | tf_op jit(solution)/shard_map/all_to_all | solution.py:343
  56.2 1.7 %copy-start = (f32[2,2,9,128,128]{4,3,2,1,0:T(8,128)S(1)}, f32[2,2,9,128,128]{4,3,2,1,0:T(8,128)}, u32[]{:S(2)}) copy-start(f32[2,2,9,128,128]{4,3,2,1,0:T(8,128)} %blocks_ref.1) | copy-start | bytes 7077892
